TPU v7x, 32 devices: a whole 2x2x4 slice. The times are simulated.
32 devices in a mesh: dp: 8 (over y, x, core), tensor: 4 (over z).
Axes of the slice: x: 2, y: 2, z: 4, core: 2. Of those that a mesh axis runs over, the one named last changes fastest.
Arguments:
- inputs: bfloat16 [8192, 2048], P('dp'), may hold values from -6 to 6
- segments: int32 [8, 1024], P('dp'), may hold values from 0 to 7, never falling along the last dimension, each value on 1 to 512 neighbouring positions
- cotangent: bfloat16 [8192, 2048], P('dp'), may hold values from -6 to 6
- norm1_gain: float32 [2048], replicated, may hold values from 0.25 to 1.75
- norm1_bias: float32 [2048], replicated, may hold values from -3 to 3
- query_weight: bfloat16 [2048, 2048], P(None, 'tensor'), may hold values from -0.125 to 0.125
- query_bias: float32 [2048], P('tensor'), may hold values from -3 to 3
- key_weight: bfloat16 [2048, 2048], P(None, 'tensor'), may hold values from -0.125 to 0.125
- value_weight: bfloat16 [2048, 2048], P(None, 'tensor'), may hold values from -0.125 to 0.125
- value_bias: float32 [2048], P('tensor'), may hold values from -2 to 2
- output_weight: bfloat16 [2048, 2048], P('tensor'), may hold values from -0.25 to 0.25
- output_bias: float32 [2048], replicated, may hold values from -3 to 3
- norm2_gain: float32 [2048], replicated, may hold values from 0.25 to 1.75
- norm2_bias: float32 [2048], replicated, may hold values from -3 to 3
- up_weight: bfloat16 [2048, 8192], P(None, 'tensor'), may hold values from -0.125 to 0.125
- up_bias: float32 [8192], P('tensor'), may hold values from -3 to 3
- down_weight: bfloat16 [8192, 2048], P('tensor'), may hold values from -0.0625 to 0.0625
- down_bias: float32 [2048], replicated, may hold values from -3 to 3
Outputs:
- output: bfloat16 [8192, 2048], P(('dp', 'tensor'))
- input_grad: float32 [8192, 2048], P(('dp', 'tensor'))
- norm1_gain_grad: float32 [2048], P('dp')
- norm1_bias_grad: float32 [2048], P('dp')
- query_weight_grad: float32 [2048, 2048], P('dp', 'tensor')
- query_bias_grad: float32 [2048], P(('tensor', 'dp'))
- key_weight_grad: float32 [2048, 2048], P('dp', 'tensor')
- value_weight_grad: float32 [2048, 2048], P('dp', 'tensor')
- value_bias_grad: float32 [2048], P(('tensor', 'dp'))
- output_weight_grad: float32 [2048, 2048], P('tensor', 'dp')
- output_bias_grad: float32 [2048], P('dp')
- norm2_gain_grad: float32 [2048], P('dp')
- norm2_bias_grad: float32 [2048], P('dp')
- up_weight_grad: float32 [2048, 8192], P('dp', 'tensor')
- up_bias_grad: float32 [8192], P(('tensor', 'dp'))
- down_weight_grad: float32 [8192, 2048], P('tensor', 'dp')
- down_bias_grad: float32 [2048], P('dp')
Inputs may be any that keep to these rules, and one draw needn't show every extreme that they name: `segments`: each row is one sequence; its document numbers start at 0 and never fall along the row; each of the 8 documents has 1 to 512 tokens and one has exactly 512.
All inputs are finite; a program needn't handle non-finite values.
Results may differ from a plain program's by a relative error of at most 0.014.
Values may be sent and summed in bfloat16 or wider, within the bound.
No kernel may reach another device: no remote copies, remote signals or barrier semaphores. Data moves between devices by JAX's collectives and lax.ppermute only.
A program may use at most 256 MiB of HBM per device.

v0:
```python
import jax
import jax.numpy as jnp
from jax import lax
from jax.sharding import PartitionSpec as P

HEAD_DIM = 128


EPSILON = 1e-05
MASKED_SCORE = -1e30


def layer_norm(row_block, gain_vector, shift_vector):
    average = jnp.mean(row_block, axis=-1, keepdims=True)
    centred = row_block - average
    spread = jnp.mean(centred * centred, axis=-1, keepdims=True)
    return centred * lax.rsqrt(spread + EPSILON) * gain_vector + shift_vector


def gelu_exact(values):
    return jax.nn.gelu(values, approximate=False)


def times_trans(left_side, right_side):
    return lax.dot_general(
        left_side, right_side, (((1,), (1,)), ((), ())), preferred_element_type=jnp.float32
    )


def trans_times(left_side, right_side):
    return lax.dot_general(
        left_side, right_side, (((0,), (0,)), ((), ())), preferred_element_type=jnp.float32
    )


def column_sums(values):
    return jnp.sum(values.astype(jnp.float32), axis=0)


def take_rows(values, first_row, row_count):
    return lax.dynamic_slice_in_dim(values, first_row, row_count, 0)


def allowed_keys(seg_row):
    places = jnp.arange(seg_row.shape[0])
    return (places[:, None] >= places[None, :]) & (seg_row[:, None] == seg_row[None, :])


def masked_scores(query_seq, key_seq, seg_row):
    scores = jnp.einsum("qhd,khd->hqk", query_seq, key_seq, preferred_element_type=jnp.float32)
    return jnp.where(allowed_keys(seg_row)[None], scores, MASKED_SCORE)


def attend_forward(blocks):
    query_seq, key_seq, value_seq, seg_row = blocks
    scores = masked_scores(query_seq, key_seq, seg_row)
    highest = jnp.max(scores, axis=-1, keepdims=True)
    weights = jnp.exp(scores - highest)
    totals = jnp.sum(weights, axis=-1, keepdims=True)
    probabilities = (weights / totals).astype(jnp.bfloat16)
    attended = jnp.einsum(
        "hqk,khd->qhd", probabilities, value_seq, preferred_element_type=jnp.float32
    )
    return (attended.astype(jnp.bfloat16), (highest + jnp.log(totals))[..., 0])


def attend_backward(blocks):
    query_seq, key_seq, value_seq, seg_row, log_totals, d_attended = blocks
    scaling = HEAD_DIM ** (-0.5)
    scores = masked_scores(query_seq, key_seq, seg_row)
    probabilities = jnp.exp(scores - log_totals[..., None])
    probs_low = probabilities.astype(jnp.bfloat16)
    d_value = jnp.einsum("hqk,qhd->khd", probs_low, d_attended, preferred_element_type=jnp.float32)
    d_probs = jnp.einsum("qhd,khd->hqk", d_attended, value_seq, preferred_element_type=jnp.float32)
    inner_sums = jnp.sum(probabilities * d_probs, axis=-1, keepdims=True)
    d_scores = (probabilities * (d_probs - inner_sums)).astype(jnp.bfloat16)
    d_query = jnp.einsum("hqk,khd->qhd", d_scores, key_seq, preferred_element_type=jnp.float32)
    d_key = jnp.einsum("hqk,qhd->khd", d_scores, query_seq, preferred_element_type=jnp.float32)
    return (
        (d_query * scaling).astype(jnp.bfloat16),
        d_key.astype(jnp.bfloat16),
        d_value.astype(jnp.bfloat16),
    )


def on_device(
    inputs,
    segments,
    cotangent,
    norm1_gain,
    norm1_bias,
    query_weight,
    query_bias,
    key_weight,
    value_weight,
    value_bias,
    output_weight,
    output_bias,
    norm2_gain,
    norm2_bias,
    up_weight,
    up_bias,
    down_weight,
    down_bias,
):
    groups = lax.axis_size("tensor")
    all_rows = inputs.shape[0]
    row_share = all_rows // groups
    row_start = lax.axis_index("tensor") * row_share
    scaling = HEAD_DIM ** (-0.5)
    local_heads = query_weight.shape[1] // HEAD_DIM
    blocked = (segments.shape[0], segments.shape[1], local_heads, HEAD_DIM)
    rows_in = inputs.astype(jnp.float32)
    cot_float = cotangent.astype(jnp.float32)
    normed = layer_norm(rows_in, norm1_gain, norm1_bias).astype(jnp.bfloat16)
    query_low = (
        (jnp.dot(normed, query_weight, preferred_element_type=jnp.float32) + query_bias) * scaling
    ).astype(jnp.bfloat16)
    key_low = jnp.dot(normed, key_weight, preferred_element_type=jnp.float32).astype(jnp.bfloat16)
    value_low = (
        jnp.dot(normed, value_weight, preferred_element_type=jnp.float32) + value_bias
    ).astype(jnp.bfloat16)
    query_blocks = query_low.reshape(blocked)
    key_blocks = key_low.reshape(blocked)
    value_blocks = value_low.reshape(blocked)
    attended_blocks, log_totals = lax.map(
        attend_forward, (query_blocks, key_blocks, value_blocks, segments)
    )
    attended = attended_blocks.reshape(all_rows, -1)
    middle = rows_in + (
        lax.psum(jnp.dot(attended, output_weight, preferred_element_type=jnp.float32), "tensor")
        + output_bias
    )
    normed_two_f, norm2_pull = jax.vjp(layer_norm, middle, norm2_gain, norm2_bias)
    normed_two_rows = normed_two_f.astype(jnp.bfloat16)
    up_value = jnp.dot(normed_two_rows, up_weight, preferred_element_type=jnp.float32) + up_bias
    hidden_f, gelu_pull = jax.vjp(gelu_exact, up_value)
    hidden = hidden_f.astype(jnp.bfloat16)
    output_full = middle + (
        lax.psum(jnp.dot(hidden, down_weight, preferred_element_type=jnp.float32), "tensor")
        + down_bias
    )
    output = take_rows(output_full, row_start, row_share).astype(jnp.bfloat16)
    d_hidden = times_trans(cotangent, down_weight)
    d_up = gelu_pull(d_hidden)[0].astype(jnp.bfloat16)
    down_weight_grad = trans_times(hidden, cotangent)
    down_bias_grad = column_sums(cotangent)
    up_weight_grad = trans_times(normed_two_rows, d_up)
    up_bias_grad = column_sums(d_up)
    d_normed_two = lax.psum(times_trans(d_up, up_weight), "tensor")
    d_middle = cot_float
    d_middle_norm, norm2_gain_grad, norm2_bias_grad = norm2_pull(d_normed_two)
    d_middle = d_middle + d_middle_norm
    d_branch_rows = d_middle.astype(jnp.bfloat16)
    output_weight_grad = trans_times(attended, d_branch_rows)
    output_bias_grad = column_sums(d_branch_rows)
    d_attended = times_trans(d_branch_rows, output_weight).astype(jnp.bfloat16)
    d_query_blocks, d_key_blocks, d_value_blocks = lax.map(
        attend_backward,
        (query_blocks, key_blocks, value_blocks, segments, log_totals, d_attended.reshape(blocked)),
    )
    d_query = d_query_blocks.reshape(all_rows, -1)
    d_key = d_key_blocks.reshape(all_rows, -1)
    d_value = d_value_blocks.reshape(all_rows, -1)
    query_weight_grad = trans_times(normed, d_query)
    query_bias_grad = column_sums(d_query)
    key_weight_grad = trans_times(normed, d_key)
    value_weight_grad = trans_times(normed, d_value)
    value_bias_grad = column_sums(d_value)
    part_query = times_trans(take_rows(d_query, 0, all_rows), query_weight)
    part_key = times_trans(take_rows(d_key, 0, all_rows), key_weight)
    part_value = times_trans(take_rows(d_value, 0, all_rows), value_weight)
    d_normed = lax.psum(part_query + part_key + part_value, "tensor")
    norm1_unused, norm1_pull = jax.vjp(layer_norm, rows_in, norm1_gain, norm1_bias)
    d_input_norm, norm1_gain_grad, norm1_bias_grad = norm1_pull(d_normed)
    input_rows = d_middle + d_input_norm
    input_grad = take_rows(input_rows, row_start, row_share)
    (
        norm1_gain_grad,
        norm1_bias_grad,
        query_weight_grad,
        query_bias_grad,
        key_weight_grad,
        value_weight_grad,
        value_bias_grad,
        output_weight_grad,
        output_bias_grad,
        norm2_gain_grad,
        norm2_bias_grad,
        up_weight_grad,
        up_bias_grad,
        down_weight_grad,
        down_bias_grad,
    ) = (
        lax.psum_scatter(norm1_gain_grad, "dp", scatter_dimension=0, tiled=True),
        lax.psum_scatter(norm1_bias_grad, "dp", scatter_dimension=0, tiled=True),
        lax.psum_scatter(query_weight_grad, "dp", scatter_dimension=0, tiled=True),
        lax.psum_scatter(query_bias_grad, "dp", scatter_dimension=0, tiled=True),
        lax.psum_scatter(key_weight_grad, "dp", scatter_dimension=0, tiled=True),
        lax.psum_scatter(value_weight_grad, "dp", scatter_dimension=0, tiled=True),
        lax.psum_scatter(value_bias_grad, "dp", scatter_dimension=0, tiled=True),
        lax.psum_scatter(output_weight_grad, "dp", scatter_dimension=1, tiled=True),
        lax.psum_scatter(output_bias_grad, "dp", scatter_dimension=0, tiled=True),
        lax.psum_scatter(norm2_gain_grad, "dp", scatter_dimension=0, tiled=True),
        lax.psum_scatter(norm2_bias_grad, "dp", scatter_dimension=0, tiled=True),
        lax.psum_scatter(up_weight_grad, "dp", scatter_dimension=0, tiled=True),
        lax.psum_scatter(up_bias_grad, "dp", scatter_dimension=0, tiled=True),
        lax.psum_scatter(down_weight_grad, "dp", scatter_dimension=1, tiled=True),
        lax.psum_scatter(down_bias_grad, "dp", scatter_dimension=0, tiled=True),
    )
    return (
        output,
        input_grad,
        norm1_gain_grad,
        norm1_bias_grad,
        query_weight_grad,
        query_bias_grad,
        key_weight_grad,
        value_weight_grad,
        value_bias_grad,
        output_weight_grad,
        output_bias_grad,
        norm2_gain_grad,
        norm2_bias_grad,
        up_weight_grad,
        up_bias_grad,
        down_weight_grad,
        down_bias_grad,
    )


def solution(mesh):
    return jax.shard_map(
        on_device,
        mesh=mesh,
        in_specs=(
            P("dp", None),
            P("dp", None),
            P("dp", None),
            P(),
            P(),
            P(None, "tensor"),
            P("tensor"),
            P(None, "tensor"),
            P(None, "tensor"),
            P("tensor"),
            P("tensor", None),
            P(),
            P(),
            P(),
            P(None, "tensor"),
            P("tensor"),
            P("tensor", None),
            P(),
        ),
        out_specs=(
            P(("dp", "tensor"), None),
            P(("dp", "tensor"), None),
            P("dp"),
            P("dp"),
            P("dp", "tensor"),
            P(("tensor", "dp")),
            P("dp", "tensor"),
            P("dp", "tensor"),
            P(("tensor", "dp")),
            P("tensor", "dp"),
            P("dp"),
            P("dp"),
            P("dp"),
            P("dp", "tensor"),
            P(("tensor", "dp")),
            P("tensor", "dp"),
            P("dp"),
        ),
        check_vma=False,
    )
```

profile of v0, /device:TPU:0, one launch (start us, length us, event | category | flops | bytes accessed | tf_op | source)
XLA Modules:
  0.0 1815.7 jit_solution(14379121048515848170)
XLA Ops:
  25.5 7.6 select_reduce_fusion
  33.2 8.8 fusion
  42.0 8.5 fusion.27
  57.2 293.6 %all-reduce.15.cloned.1.call-done = f32[1024,2048]{1,0:T(8,128)} async-done(((f32[1024,2048]{1,0:T(8,128)}), f32[1024,2048]{1,0:T(8,128)}) %all-reduce.15.cloned.1.call-update) | async-done | bytes 8388624 | tf_op jit(solution)/shard_map/psum | solution.py:131
  357.6 23.1 %fusion.39 = f32[1024,2048]{1,0:T(8,128)S(1)} fusion(bf16[2048,2048]{1,0:T(8,128)(2,1)} %param.32, f32[1024,2048]{1,0:T(8,128)S(1)} %get-tuple-element.95, f32[2048]{0:T(1024)S(1)} %copy-done.52, f32[2048]{0:T(1024)S(1)} %copy-done.40, f32[1024]{0:T(1024)S(1)} %fusion.32, f32[1024]{0:T(1024)S(1)} %broadcast_multiply_fusion), kind=kOutput, calls=%fused_computation.89 | convolution fusion | flops 8600420352 | bytes 25190400 | tf_op jit(solution)/shard_map/dot_general | solution.py:136
  380.8 33.5 %convert_reduce_fusion.2 = (f32[2048]{0:T(1024)}, bf16[1024,2048]{1,0:T(8,128)(2,1)}, f32[1024,2048]{1,0:T(8,128)}) fusion(f32[1024,2048]{1,0:T(8,128)S(1)} %fusion.39, f32[2048]{0:T(1024)S(1)} %copy-done.45, bf16[1024,2048]{1,0:T(8,128)(2,1)S(1)} %copy-done.12, bf16[2048,2048]{1,0:T(8,128)(2,1)} %param.34), kind=kOutput, calls=%fused_computation.29 | convolution fusion | flops 8747218944 | bytes 33570816 | tf_op jit(solution)/shard_map/dot_general | solution.py:25
  414.3 14.6 fusion.46
  429.6 8.8 multiply_convert_fusion.1
  440.4 13.7 fusion.45
  454.1 264.8 %all-reduce.17.cloned.1.call-done = f32[1024,2048]{1,0:T(8,128)} async-done(((f32[1024,2048]{1,0:T(8,128)}), f32[1024,2048]{1,0:T(8,128)}) %all-reduce.17.cloned.1.call-update) | async-done | bytes 8388624 | tf_op jit(solution)/shard_map/psum | solution.py:150
  718.9 7.5 multiply_reduce_fusion.1
  738.1 8.3 convert_reduce_fusion.4
  746.4 12.3 multiply_reduce_fusion
  758.8 12.1 multiply_convert_fusion
  786.2 8.0 fusion.33
  815.2 16.4 fusion.38
  831.7 15.3 fusion.52
  849.5 498.8 %all-reduce.19.cloned.1.call-done = (f32[1024,2048]{1,0:T(8,128)}, f32[1024,2048]{1,0:T(8,128)}) async-done(((f32[1024,2048]{1,0:T(8,128)}, f32[1024,2048]{1,0:T(8,128)}), (f32[1024,2048]{1,0:T(8,128)}, f32[1024,2048]{1,0:T(8,128)})) %all-reduce.19.cloned.1.call-update) | async-done | bytes 16777232 | tf_op jit(solution)/shard_map/psum | solution.py:140
  1354.6 25.1 %all-reduce.9 = (f32[2048]{0:T(1024)S(1)}, f32[2048]{0:T(1024)S(1)}, f32[512]{0:T(512)S(1)}, f32[512]{0:T(512)S(1)}, f32[2048]{0:T(1024)S(1)}, /*index=5*/f32[20...) all-reduce(f32[2048]{0:T(1024)S(1)} %get-tuple-element.70, ...), channel_id=2, replica_groups=mesh['dp'=8,'tensor'=4] {'dp'}, use_global_device_ids=true, to_apply=%region_16.17.clone | all-reduce | flops 15360 | bytes 122880
  1402.5 55.5 %reduce-scatter.11.cloned.1.call-done = f32[256,512]{1,0:T(8,128)} async-done(((f32[2048,512]{1,0:T(8,128)}), f32[256,512]{1,0:T(8,128)}) %reduce-scatter.11.cloned.1.call-update) | async-done | bytes 524304 | tf_op jit(solution)/shard_map/reduce_scatter | solution.py:200
  1458.0 55.1 %reduce-scatter.9.cloned.1.call-done = f32[256,512]{1,0:T(8,128)} async-done(((f32[2048,512]{1,0:T(8,128)}), f32[256,512]{1,0:T(8,128)}) %reduce-scatter.9.cloned.1.call-update) | async-done | bytes 524304 | tf_op jit(solution)/shard_map/reduce_scatter | solution.py:199
  1513.1 55.6 %reduce-scatter.7.cloned.1.call-done = f32[256,512]{1,0:T(8,128)} async-done(((f32[2048,512]{1,0:T(8,128)}), f32[256,512]{1,0:T(8,128)}) %reduce-scatter.7.cloned.1.call-update) | async-done | bytes 524304 | tf_op jit(solution)/shard_map/reduce_scatter | solution.py:197
  1568.7 120.1 %reduce-scatter.15.cloned.1.call-done = f32[256,2048]{1,0:T(8,128)} async-done(((f32[2048,2048]{1,0:T(8,128)}), f32[256,2048]{1,0:T(8,128)}) %reduce-scatter.15.cloned.1.call-update) | async-done | bytes 2097168 | tf_op jit(solution)/shard_map/reduce_scatter | solution.py:206
  1688.9 120.1 %reduce-scatter.17.cloned.1.call-done = f32[2048,256]{1,0:T(8,128)} async-done(((f32[2048,2048]{1,0:T(8,128)}), f32[2048,256]{1,0:T(8,128)}) %reduce-scatter.17.cloned.1.call-update) | async-done | bytes 2097168 | tf_op jit(solution)/shard_map/reduce_scatter | solution.py:208
  (179 shorter events, 112.2 us)
Async XLA Ops:
  7.2 44.3 %copy-start = (bf16[512,2048]{1,0:T(8,128)(2,1)S(1)}, bf16[512,2048]{1,0:T(8,128)(2,1)}, u32[]{:S(2)}) copy-start(bf16[512,2048]{1,0:T(8,128)(2,1)} %param.28) | copy-start | bytes 6291460
  7.2 343.5 %all-reduce.15.cloned.1.call-start = ((), (), s32[]{:S(2)}) async-start(), calls=%async_computation.6 | async-start | bytes 16777216 | tf_op jit(solution)/shard_map/psum | solution.py:131
  14.6 27.4 %copy-start.3 = (pred[1024,1024]{0,1:T(8,128)(4,1)}, pred[1024,1024]{0,1:T(8,128)(4,1)S(1)}, u32[]{:S(2)}) copy-start(pred[1024,1024]{0,1:T(8,128)(4,1)S(1)} %fusion.25) | copy-start | bytes 3145732
  51.5 299.3 %copy-start.44 = (f32[2048]{0:T(1024)S(1)}, f32[2048]{0:T(1024)}, u32[]{:S(2)}) copy-start(f32[2048]{0:T(1024)} %param.29) | copy-start | bytes 24580
  57.1 661.8 %all-reduce.17.cloned.1.call-start = ((), (), s32[]{:S(2)}) async-start(), calls=%async_computation.7 | async-start | bytes 16777216 | tf_op jit(solution)/shard_map/psum | solution.py:150
  356.5 24.2 %copy-start.1 = (f32[1024,2048]{1,0:T(8,128)}, f32[1024,2048]{1,0:T(8,128)S(1)}, u32[]{:S(2)}) copy-start(f32[1024,2048]{1,0:T(8,128)S(1)} %get-tuple-element.95) | copy-start | bytes 25165828
  356.6 24.1 %copy-start.28 = (f32[1024]{0:T(1024)}, f32[1024]{0:T(1024)S(1)}, u32[]{:S(2)}) copy-start(f32[1024]{0:T(1024)S(1)} %broadcast_multiply_fusion) | copy-start | bytes 12292
  380.7 33.5 %copy-start.7 = (f32[1024,2048]{1,0:T(8,128)}, f32[1024,2048]{1,0:T(8,128)S(1)}, u32[]{:S(2)}) copy-start(f32[1024,2048]{1,0:T(8,128)S(1)} %fusion.39) | copy-start | bytes 25165828
  428.9 919.5 %all-reduce.19.cloned.1.call-start = ((), (), s32[]{:S(2)}) async-start(), calls=%async_computation.14 | async-start | bytes 33554432 | tf_op jit(solution)/shard_map/psum | solution.py:140
  440.4 278.5 %copy-start.29 = (f32[1024]{0:T(1024)S(1)}, f32[1024]{0:T(1024)}, u32[]{:S(2)}) copy-start(f32[1024]{0:T(1024)} %copy-done.28) | copy-start | bytes 12292
  440.4 278.5 %copy-start.37 = (f32[1024]{0:T(1024)S(1)}, f32[1024]{0:T(1024)}, u32[]{:S(2)}) copy-start(f32[1024]{0:T(1024)} %copy-done.36) | copy-start | bytes 12292
  440.4 278.5 %copy-start.41 = (f32[2048]{0:T(1024)S(1)}, f32[2048]{0:T(1024)}, u32[]{:S(2)}) copy-start(f32[2048]{0:T(1024)} %param.30) | copy-start | bytes 24580
  454.1 272.3 %copy-start.35 = (f32[1024]{0:T(1024)S(1)}, f32[1024]{0:T(1024)}, u32[]{:S(2)}) copy-start(f32[1024]{0:T(1024)} %copy-done.34) | copy-start | bytes 12292
  785.9 616.6 %reduce-scatter.13.cloned.1.call-start = ((), (), s32[]{:S(2)}) async-start(), calls=%async_computation.11 | async-start | bytes 4718592 | tf_op jit(solution)/shard_map/reduce_scatter | solution.py:202
  794.2 663.7 %reduce-scatter.11.cloned.1.call-start = ((), (), s32[]{:S(2)}) async-start(), calls=%async_computation.10 | async-start | bytes 4718592 | tf_op jit(solution)/shard_map/reduce_scatter | solution.py:200
  800.9 712.2 %reduce-scatter.9.cloned.1.call-start = ((), (), s32[]{:S(2)}) async-start(), calls=%async_computation.9 | async-start | bytes 4718592 | tf_op jit(solution)/shard_map/reduce_scatter | solution.py:199
  808.0 760.7 %reduce-scatter.7.cloned.1.call-start = ((), (), s32[]{:S(2)}) async-start(), calls=%async_computation.8 | async-start | bytes 4718592 | tf_op jit(solution)/shard_map/reduce_scatter | solution.py:197
  814.7 874.2 %reduce-scatter.15.cloned.1.call-start = ((), (), s32[]{:S(2)}) async-start(), calls=%async_computation.12 | async-start | bytes 18874368 | tf_op jit(solution)/shard_map/reduce_scatter | solution.py:206
  831.6 977.4 %reduce-scatter.17.cloned.1.call-start = ((), (), s32[]{:S(2)}) async-start(), calls=%async_computation.13 | async-start | bytes 18874368 | tf_op jit(solution)/shard_map/reduce_scatter | solution.py:208
  847.0 501.4 %copy-start.25 = (f32[1024]{0:T(1024)S(1)}, f32[1024]{0:T(1024)}, u32[]{:S(2)}) copy-start(f32[1024]{0:T(1024)} %copy-done.24) | copy-start | bytes 12292
  847.0 501.4 %copy-start.27 = (f32[2048]{0:T(1024)S(1)}, f32[2048]{0:T(1024)}, u32[]{:S(2)}) copy-start(f32[2048]{0:T(1024)} %param.21) | copy-start | bytes 24580
  847.0 501.4 %copy-start.31 = (f32[1024]{0:T(1024)S(1)}, f32[1024]{0:T(1024)}, u32[]{:S(2)}) copy-start(f32[1024]{0:T(1024)} %copy-done.30) | copy-start | bytes 12292
  847.0 507.6 %copy-start.46 = (f32[2048]{0:T(1024)S(1)}, f32[2048]{0:T(1024)}, u32[]{:S(2)}) copy-start(f32[2048]{0:T(1024)} %get-tuple-element.85) | copy-start | bytes 24580
  847.0 538.3 %copy-start.39 = (f32[1024]{0:T(1024)S(1)}, f32[1024]{0:T(1024)}, u32[]{:S(2)}) copy-start(f32[1024]{0:T(1024)} %copy-done.38) | copy-start | bytes 12292
  (43 other events, 274.1 us)
Sparse Core Ops, SparseCore 0:
  57.2 293.5 all-reduce.14
  429.0 289.8 all-reduce.16
  786.0 562.2 all-reduce.18
  1352.1 50.2 reduce-scatter.12
  1406.6 51.2 reduce-scatter.10
  1461.7 51.3 reduce-scatter.8
  1517.4 51.2 reduce-scatter.6
  1572.9 115.9 reduce-scatter.14
  1693.0 115.9 reduce-scatter.16
where the time goes:
time: 1820 us
  waiting for transfers between devices  1470 us (81%)
  matrix products  213 us (12%)
  other arithmetic  78.9 us (4%)
  blocking collectives  25.1 us (1%)
    psum x1, waiting for transfers between devices, on_device(): lax.psum(jnp.dot(hidden, down_weight, preferred_element_type=jnp.float32)...  499 us
    psum x1, waiting for transfers between devices, on_device(): lax.psum(jnp.dot(attended, output_weight, preferred_element_type=jnp.floa...  294 us
    psum x1, waiting for transfers between devices, on_device(): d_normed_two = lax.psum(times_trans(d_up, up_weight), 'tensor')  265 us
    reduce_scatter x1, waiting for transfers between devices, on_device(): lax.psum_scatter(down_weight_grad, 'dp', scatter_dimension=1, tiled=True)  120 us
    reduce_scatter x1, waiting for transfers between devices, on_device(): lax.psum_scatter(up_weight_grad, 'dp', scatter_dimension=0, tiled=True)  120 us
    dot_general x6, matrix products, times_trans(): lax.dot_general(left_side, right_side, (((1,), (1,)), ((), ())), preferre...  61.1 us
    dot_general x6, matrix products, trans_times(): lax.dot_general(left_side, right_side, (((0,), (0,)), ((), ())), preferre...  60 us
    reduce_scatter x1, waiting for transfers between devices, on_device(): lax.psum_scatter(query_weight_grad, 'dp', scatter_dimension=0, tiled=True)  55.6 us
  transfers between devices with their start and end apart: 9, of which 9 were waited for; matrix products, arithmetic and copies ran while one was open for 6% of the time, Pallas kernels for 0%

commit v1 on v0

v1 whole, which is shorter than its diff:
```python
import functools

import jax
import jax.numpy as jnp
from jax import lax
from jax.experimental import pallas as pl
from jax.experimental.pallas import tpu as pltpu
from jax.sharding import PartitionSpec as P

HEAD_DIM = 128
LONGEST = 512
EPSILON = 1e-05
MASKED_SCORE = -1e30
SCALING = HEAD_DIM ** (-0.5)
F32 = jnp.float32
BF16 = jnp.bfloat16
PARTS = 2


def mm(left_side, right_side):
    return lax.dot_general(
        left_side, right_side, (((1,), (0,)), ((), ())), preferred_element_type=F32
    )


def times_trans(left_side, right_side):
    return lax.dot_general(
        left_side, right_side, (((1,), (1,)), ((), ())), preferred_element_type=F32
    )


def trans_times(left_side, right_side):
    return lax.dot_general(
        left_side, right_side, (((0,), (0,)), ((), ())), preferred_element_type=F32
    )


def column_sums(values):
    return jnp.sum(values.astype(F32), axis=0)


def row_stats(rows):
    average = jnp.mean(rows, axis=-1, keepdims=True)
    centred = rows - average
    spread = jnp.mean(centred * centred, axis=-1, keepdims=True)
    return average, lax.rsqrt(spread + EPSILON)


def norm_back(d_normed, gain, xhat, inverse):
    scaled = d_normed * gain
    first = jnp.mean(scaled, axis=-1, keepdims=True)
    second = jnp.mean(scaled * xhat, axis=-1, keepdims=True)
    return inverse * (scaled - first - xhat * second)


def cost(flops):
    return pl.CostEstimate(flops=flops, bytes_accessed=16 * 2**20, transcendentals=0)


def key_start(block, size):
    return max(0, (block * size - (LONGEST - 1)) // size * size)


def probabilities(seg_row, seg_col, query, keys, block, size):
    low, high = key_start(block, size), (block + 1) * size
    scores = times_trans(keys[low:high, :], query)
    shape = (high - low, size)
    key_place = lax.broadcasted_iota(jnp.int32, shape, 0) + low
    query_place = lax.broadcasted_iota(jnp.int32, shape, 1) + block * size
    same = seg_col[low:high, :] == seg_row[:, block * size : high]
    scores = jnp.where(same & (key_place <= query_place), scores, MASKED_SCORE)
    weights = jnp.exp(scores - jnp.max(scores, axis=0, keepdims=True))
    return weights * (1.0 / jnp.sum(weights, axis=0, keepdims=True))


def forward_kernel(size, seg_row, seg_col, query, key, value, attended):
    for block in range(query.shape[0] // size):
        low, high = key_start(block, size), (block + 1) * size
        rows = slice(block * size, high)
        probs = probabilities(seg_row, seg_col, query[rows, :], key, block, size)
        attended[rows, :] = trans_times(probs.astype(BF16), value[low:high, :]).astype(BF16)


def backward_kernel(size, pieces, here_ref, seg_row, seg_col, query, key, value, *refs):
    count = len(pieces) * len(pieces[0])
    got = refs[:count]
    d_query, d_key, d_value, d_attended, key_sum, value_sum = refs[count:]
    groups = len(pieces[0])
    part = got[0].shape[0]
    share = len(pieces) * part
    for c in range(len(pieces)):
        for m in range(groups):
            start = lax.rem(here_ref[1] + m, groups) * share + c * part
            rows = pl.ds(pl.multiple_of(start, part), part)
            d_attended[rows, :] = got[c * groups + m][...]
    key_sum[...] = jnp.zeros_like(key_sum)
    value_sum[...] = jnp.zeros_like(value_sum)
    for block in range(query.shape[0] // size):
        low, high = key_start(block, size), (block + 1) * size
        rows = slice(block * size, high)
        probs = probabilities(seg_row, seg_col, query[rows, :], key, block, size)
        value_sum[low:high, :] += mm(probs.astype(BF16), d_attended[rows, :])
        d_probs = times_trans(value[low:high, :], d_attended[rows, :])
        inner = jnp.sum(probs * d_probs, axis=0, keepdims=True)
        d_scores = (probs * (d_probs - inner)).astype(BF16)
        d_query[rows, :] = (trans_times(d_scores, key[low:high, :]) * SCALING).astype(BF16)
        key_sum[low:high, :] += mm(d_scores, query[rows, :])
    d_key[...] = key_sum[...].astype(BF16)
    d_value[...] = value_sum[...].astype(BF16)


def segment_views(segments):
    seqs, length = segments.shape
    return segments.reshape(seqs, 1, length), segments.reshape(seqs, length, 1)


def attend(segments, query, key, value):
    seqs, length = segments.shape
    tall = pl.BlockSpec((length, HEAD_DIM), lambda s, h: (s, h))
    return pl.pallas_call(
        functools.partial(forward_kernel, min(256, length)),
        grid=(seqs, query.shape[1] // HEAD_DIM),
        in_specs=[
            pl.BlockSpec((None, 1, length), lambda s, h: (s, 0, 0)),
            pl.BlockSpec((None, length, 1), lambda s, h: (s, 0, 0)),
        ]
        + [tall] * 3,
        out_specs=tall,
        out_shape=jax.ShapeDtypeStruct(query.shape, BF16),
        compiler_params=pltpu.CompilerParams(vmem_limit_bytes=48 * 2**20),
        cost_estimate=cost(4 * query.shape[0] * length * query.shape[1]),
    )(*segment_views(segments), query, key, value)


def attend_back(segments, query, key, value, pieces, me):
    length = query.shape[0]
    tall = pl.BlockSpec((length, HEAD_DIM), lambda h, m: (0, h))
    flat = [piece for row in pieces for piece in row]
    kernel = functools.partial(backward_kernel, min(256, length), pieces)
    return pl.pallas_call(
        kernel,
        grid_spec=pltpu.PrefetchScalarGridSpec(
            num_scalar_prefetch=1,
            grid=(query.shape[1] // HEAD_DIM,),
            in_specs=[
                pl.BlockSpec((None, 1, length), lambda h, m: (0, 0, 0)),
                pl.BlockSpec((None, length, 1), lambda h, m: (0, 0, 0)),
            ]
            + [tall] * 3
            + [pl.BlockSpec((p.shape[0], HEAD_DIM), lambda h, m: (0, h)) for p in flat],
            out_specs=[tall] * 3,
            scratch_shapes=[
                pltpu.VMEM((length, HEAD_DIM), BF16),
                pltpu.VMEM((length, HEAD_DIM), F32),
                pltpu.VMEM((length, HEAD_DIM), F32),
            ],
        ),
        out_shape=[jax.ShapeDtypeStruct(query.shape, BF16)] * 3,
        compiler_params=pltpu.CompilerParams(vmem_limit_bytes=48 * 2**20),
        cost_estimate=cost(10 * query.shape[0] * length * query.shape[1]),
    )(me, *segment_views(segments), query, key, value, *flat)


def place_bits(blocks):
    return blocks.bit_length() - 1


def xor_source(place, me, bits):
    distance = 0
    for bit in range(bits):
        distance = distance + (((place >> (bits - 1 - bit)) & 1) << bit)
    return distance ^ me


def norm_rows(values, gain, bias):
    average = jnp.mean(values, axis=-1, keepdims=True)
    centred = values - average
    inverse = lax.rsqrt(jnp.mean(centred * centred, axis=-1, keepdims=True) + EPSILON)
    return centred * inverse * gain + bias


def project_kernel(x, gain, bias, wq, bq, wk, wv, bv, normed, query, key, value):
    low = norm_rows(x[...].astype(F32), gain[...], bias[...]).astype(BF16)
    normed[...] = low
    query[...] = ((mm(low, wq[...]) + bq[...]) * SCALING).astype(BF16)
    key[...] = mm(low, wk[...]).astype(BF16)
    value[...] = (mm(low, wv[...]) + bv[...]).astype(BF16)


def whole_spec(array):
    return pl.BlockSpec(array.shape, lambda *_: (0,) * array.ndim)


def project(x, gain, bias, wq, bq, wk, wv, bv):
    rows, width = x.shape
    local = wq.shape[1]
    size = min(512, rows)
    args = [x] + [v.reshape(1, -1) if v.ndim == 1 else v for v in (gain, bias, wq, bq, wk, wv, bv)]
    tall = pl.BlockSpec((size, width), lambda i: (i, 0))
    thin = pl.BlockSpec((size, local), lambda i: (i, 0))
    shape = jax.ShapeDtypeStruct((rows, local), BF16)
    return pl.pallas_call(
        project_kernel,
        grid=(rows // size,),
        in_specs=[tall] + [whole_spec(a) for a in args[1:]],
        out_specs=[tall] + [thin] * 3,
        out_shape=[jax.ShapeDtypeStruct(x.shape, BF16)] + [shape] * 3,
        compiler_params=pltpu.CompilerParams(vmem_limit_bytes=56 * 2**20),
        cost_estimate=cost(6 * rows * width * local),
    )(*args)


def middle_kernel(
    steps, here_ref, near, far, wo, x, bo, gain, bias, wup, bup, d_hid, wup_rows,
    own_mid, low_out, hidden, d_up, term, mid, low, d_low,
):
    first, second = steps
    step = pl.program_id(0)
    block = wo.shape[1]
    here, side = here_ref[0], here_ref[1]
    half = near.shape[1]

    @pl.when(step < first)
    def _():
        offset = pl.multiple_of(side * half, half)
        other = pl.multiple_of((1 - side) * half, half)
        branch = mm(near[...], wo[pl.ds(offset, half), :])
        branch = branch + mm(far[...], wo[pl.ds(other, half), :])
        values = x[...].reshape(branch.shape).astype(F32)
        columns = pl.ds(pl.multiple_of(step * block, block), block)
        mid[:, columns] = values + (branch + bo[...])

    @pl.when(step == first)
    def _():
        low[...] = norm_rows(mid[...], gain[...], bias[...]).astype(BF16)
        part = own_mid.shape[0]
        own_mid[...] = mid[pl.ds(pl.multiple_of(here * part, part), part), :]

    @pl.when((step >= first) & (step < first + second))
    def _():
        piece = 256
        for start in range(0, wup.shape[1], piece):
            columns = slice(start, start + piece)
            up_value = mm(low[...], wup[:, columns]) + bup[:, columns]
            below = 0.5 + 0.5 * lax.erf(up_value * (0.5**0.5))
            density = jnp.exp(-0.5 * up_value * up_value) * 0.3989422804014327
            hidden[:, columns] = (up_value * below).astype(BF16)
            slope = ((below + up_value * density) * d_hid[:, columns].astype(F32)).astype(BF16)
            d_up[:, columns] = slope
            place = pl.multiple_of((step - first) * wup.shape[1] + start, piece)
            d_low[:, pl.ds(place, piece)] = slope

    @pl.when(step >= first + second)
    def _():
        term[...] = times_trans(d_low[...], wup_rows[...]).astype(BF16)
        columns = pl.ds(pl.multiple_of((step - first - second) * block, block), block)
        low_out[...] = low[:, columns]


def middle_call(c, here, near, far, wo, x, bo, gain, bias, wup, bup, d_hid):
    groups, _, part, width = x.shape
    rows = groups * part
    hidden = wup.shape[1]
    block = 512
    first, second = width // block, hidden // block
    bo, gain, bias, bup = (v.reshape(1, -1) for v in (bo, gain, bias, bup))

    def at(index, low, count):
        return jnp.clip(index - low, 0, count - 1)

    def columns(tall, low, count):
        return pl.BlockSpec((tall, block), lambda i, h: (0, at(i, low, count)))

    third = first + second
    return pl.pallas_call(
        functools.partial(middle_kernel, (first, second)),
        grid_spec=pltpu.PrefetchScalarGridSpec(
            num_scalar_prefetch=1,
            grid=(first + second + first,),
            in_specs=[
                whole_spec(near),
                whole_spec(far),
                columns(width, 0, first),
                pl.BlockSpec(
                    (groups, None, part, block), lambda i, h: (0, c, 0, at(i, 0, first))
                ),
                columns(1, 0, first),
                whole_spec(gain),
                whole_spec(bias),
                columns(width, first, second),
                columns(1, first, second),
                pl.BlockSpec((None, rows, block), lambda i, h: (c, 0, at(i, first, second))),
                pl.BlockSpec((block, hidden), lambda i, h: (at(i, third, first), 0)),
            ],
            out_specs=[
                pl.BlockSpec((part, width), lambda i, h: (0, 0)),
                columns(rows, third, first),
                columns(rows, first, second),
                columns(rows, first, second),
                columns(rows, third, first),
            ],
            scratch_shapes=[
                pltpu.VMEM((rows, width), F32),
                pltpu.VMEM((rows, width), BF16),
                pltpu.VMEM((rows, hidden), BF16),
            ],
        ),
        out_shape=[
            jax.ShapeDtypeStruct((part, width), F32),
            jax.ShapeDtypeStruct((rows, width), BF16),
            jax.ShapeDtypeStruct((rows, hidden), BF16),
            jax.ShapeDtypeStruct((rows, hidden), BF16),
            jax.ShapeDtypeStruct((rows, width), BF16),
        ],
        compiler_params=pltpu.CompilerParams(vmem_limit_bytes=56 * 2**20),
        cost_estimate=cost(2 * rows * width * (width + 2 * hidden)),
    )(here, near, far, wo, x, bo, gain, bias, wup, bup, d_hid, wup)


def middle_back_kernel(count, here_ref, *refs):
    pieces, (mid, cot, gain, wo), outs = refs[:count], refs[count : count + 4], refs[count + 4 :]
    d_mid, d_branch, sums, d_att = outs

    @pl.when(pl.program_id(0) == 0)
    def _():
        d_normed = pieces[0][...].astype(F32)
        for piece in pieces[1:]:
            d_normed = d_normed + piece[...].astype(F32)
        values = mid[...]
        centred = values - jnp.mean(values, axis=-1, keepdims=True)
        inverse = lax.rsqrt(jnp.mean(centred * centred, axis=-1, keepdims=True) + EPSILON)
        xhat = centred * inverse
        total = cot[...].astype(F32) + norm_back(d_normed, gain[...], xhat, inverse)
        low = total.astype(BF16)
        d_mid[...] = total
        d_branch[...] = low
        sums[0:1, :] = jnp.sum(d_normed * xhat, axis=0, keepdims=True)
        sums[1:2, :] = jnp.sum(d_normed, axis=0, keepdims=True)
        sums[2:3, :] = jnp.sum(low.astype(F32), axis=0, keepdims=True)

    d_att[...] = times_trans(d_branch[...], wo[...]).astype(BF16)


def middle_back(c, me, pieces, mid, cotangent, gain, wo):
    part, width = mid.shape
    block = 512
    whole_rows = pl.BlockSpec((part, width), lambda j, m: (0, 0))
    specs = []
    for array, which in pieces:
        if which is None:
            specs.append(whole_rows)
        else:
            specs.append(
                pl.BlockSpec((None, part, width), lambda j, m, which=which: (which(m), 0, 0))
            )
    cot_spec = pl.BlockSpec((part, width), lambda j, m: (m[1] * PARTS + c, 0))
    return pl.pallas_call(
        functools.partial(middle_back_kernel, len(pieces)),
        grid_spec=pltpu.PrefetchScalarGridSpec(
            num_scalar_prefetch=1,
            grid=(width // block,),
            in_specs=specs
            + [whole_rows, cot_spec, pl.BlockSpec((1, width), lambda j, m: (0, 0))]
            + [pl.BlockSpec((block, width), lambda j, m: (j, 0))],
            out_specs=[
                whole_rows,
                whole_rows,
                pl.BlockSpec((8, width), lambda j, m: (0, 0)),
                pl.BlockSpec((part, block), lambda j, m: (0, j)),
            ],
        ),
        out_shape=[
            jax.ShapeDtypeStruct((part, width), F32),
            jax.ShapeDtypeStruct((part, width), BF16),
            jax.ShapeDtypeStruct((8, width), F32),
            jax.ShapeDtypeStruct((part, width), BF16),
        ],
        compiler_params=pltpu.CompilerParams(vmem_limit_bytes=48 * 2**20),
        cost_estimate=cost(2 * part * width * width),
    )(me, *[array for array, _ in pieces], mid, cotangent, gain.reshape(1, -1), wo)


def gradient_terms(pairs, me, blocks, core_only=False):
    half = blocks // 2
    bits = place_bits(blocks)
    lefts = [left for pair in pairs for left in pair[0]]
    part_of = [left[1] if isinstance(left, tuple) else None for left in lefts]
    lefts = [left[0] if isinstance(left, tuple) else left for left in lefts]
    rights = [right for pair in pairs for right in pair[1]]
    width = lefts[0].shape[-1] // blocks
    total = sum(pair[1][0].shape[1] for pair in pairs)

    def source(j, m):
        if core_only:
            return 2 * (j % half) + ((m[0] & 1) ^ (j < half).astype(jnp.int32))
        return xor_source(jnp.where(j < half, j + half, j - half), m[0], bits)

    def left_spec(left, c):
        if c is None:
            return pl.BlockSpec((left.shape[0], width), lambda j, m: (0, source(j, m)))
        shape = (left.shape[0], None, left.shape[2], width)
        return pl.BlockSpec(shape, lambda j, m: (0, c, 0, source(j, m)))

    def kernel(me_ref, *refs):
        left_refs, right_refs = refs[: len(lefts)], refs[len(lefts) : len(lefts) + len(rights)]
        send, keep = refs[-2:]
        step = pl.program_id(0)

        def fill(target):
            place = at = 0
            for ls, rs in pairs:
                count = len(ls)
                value = None
                for i in range(count):
                    left = left_refs[at + i][...].reshape(-1, width)
                    more = trans_times(left, right_refs[at + i][...])
                    value = more if value is None else value + more
                columns = value.shape[1]
                target[:, place : place + columns] = value.astype(BF16)
                place += columns
                at += count

        @pl.when(step < half)
        def _():
            fill(send)

        @pl.when(step >= half)
        def _():
            fill(keep)

    shape = jax.ShapeDtypeStruct((half, width, total), BF16)
    return pl.pallas_call(
        kernel,
        grid_spec=pltpu.PrefetchScalarGridSpec(
            num_scalar_prefetch=1,
            grid=(blocks,),
            in_specs=[left_spec(left, c) for left, c in zip(lefts, part_of)]
            + [whole_spec(right) for right in rights],
            out_specs=[
                pl.BlockSpec((None, width, total), lambda j, m: (jnp.minimum(j, half - 1), 0, 0)),
                pl.BlockSpec((None, width, total), lambda j, m: (jnp.maximum(j - half, 0), 0, 0)),
            ],
        ),
        out_shape=[shape, shape],
        compiler_params=pltpu.CompilerParams(vmem_limit_bytes=56 * 2**20),
        cost_estimate=cost(2 * blocks * width * sum(r.size for r in rights)),
    )(me, *lefts, *rights)


def normed_back_kernel(dq, dk, dv, wq, wk, wv, x, terms, gain_sum, bias_sum):
    total = times_trans(dq[...], wq[...]) + times_trans(dk[...], wk[...])
    total = total + times_trans(dv[...], wv[...])
    terms[...] = total.astype(BF16)
    values = x[...].astype(F32)
    centred = values - jnp.mean(values, axis=-1, keepdims=True)
    inverse = lax.rsqrt(jnp.mean(centred * centred, axis=-1, keepdims=True) + EPSILON)

    @pl.when(pl.program_id(0) == 0)
    def _():
        gain_sum[...] = jnp.zeros_like(gain_sum)
        bias_sum[...] = jnp.zeros_like(bias_sum)

    gain_sum[...] += jnp.sum(total * (centred * inverse), axis=0, keepdims=True)
    bias_sum[...] += jnp.sum(total, axis=0, keepdims=True)


def normed_back(dq, dk, dv, wq, wk, wv, x):
    rows, width = x.shape
    size = min(512, rows)
    thin = pl.BlockSpec((size, dq.shape[1]), lambda i: (i, 0))
    tall = pl.BlockSpec((size, width), lambda i: (i, 0))
    line = pl.BlockSpec((1, width), lambda i: (0, 0))
    return pl.pallas_call(
        normed_back_kernel,
        grid=(rows // size,),
        in_specs=[thin] * 3 + [whole_spec(w) for w in (wq, wk, wv)] + [tall],
        out_specs=[tall, line, line],
        out_shape=[
            jax.ShapeDtypeStruct((rows, width), BF16),
            jax.ShapeDtypeStruct((1, width), F32),
            jax.ShapeDtypeStruct((1, width), F32),
        ],
        compiler_params=pltpu.CompilerParams(vmem_limit_bytes=56 * 2**20),
        cost_estimate=cost(6 * rows * width * dq.shape[1]),
    )(dq, dk, dv, wq, wk, wv, x)


def both_parts(lefts, weight, transposed, columns):
    block = min(512, columns)
    part_of = [left[1] if isinstance(left, tuple) else None for left in lefts]
    lefts = [left[0] if isinstance(left, tuple) else left for left in lefts]
    depth = lefts[0].shape[-1]
    rows = lefts[0].shape[0] * (1 if part_of[0] is None else lefts[0].shape[2])

    def kernel(*refs):
        weight_ref, out = refs[-2:]
        for c in range(len(lefts)):
            left = refs[c][...].reshape(-1, depth)
            product = times_trans if transposed else mm
            out[c] = product(left, weight_ref[...]).astype(BF16)

    def left_spec(left, c):
        if c is None:
            return whole_spec(left)
        return pl.BlockSpec((left.shape[0], None) + left.shape[2:], lambda j: (0, c, 0, 0))

    if transposed:
        weight_spec = pl.BlockSpec((block, depth), lambda j: (j, 0))
    else:
        weight_spec = pl.BlockSpec((depth, block), lambda j: (0, j))
    return pl.pallas_call(
        kernel,
        grid=(columns // block,),
        in_specs=[left_spec(left, c) for left, c in zip(lefts, part_of)] + [weight_spec],
        out_specs=pl.BlockSpec((len(lefts), rows, block), lambda j: (0, 0, j)),
        out_shape=jax.ShapeDtypeStruct((len(lefts), rows, columns), BF16),
        compiler_params=pltpu.CompilerParams(vmem_limit_bytes=56 * 2**20),
        cost_estimate=cost(2 * len(lefts) * rows * depth * columns),
    )(*lefts, weight)


def swap_bit(values, axis, bit):
    size = lax.axis_size(axis)
    return lax.ppermute(values, axis, [(i, i ^ (1 << bit)) for i in range(size)])


def third(k, steps):
    return range((k - 1) * steps // 3 + 1, k * steps // 3 + 1)


def fence(things, arrays=()):
    lists = [thing.live for thing in things]
    flat = lax.optimization_barrier(tuple(v for values in lists for v in values) + tuple(arrays))
    place = 0
    for thing, values in zip(things, lists):
        thing.live = list(flat[place : place + len(values)])
        place += len(values)
    return flat[place:]


class Gather:
    def __init__(self, own):
        self.live = [own]
        self.size = lax.axis_size("tensor")
        self.here = lax.axis_index("tensor")

    def advance(self, k):
        if self.size != 4:
            if k == 1:
                every = lax.all_gather(self.live[0], "tensor", axis=1, tiled=True)
                half = every.shape[1] // 2
                side = self.here // (self.size // 2)
                self.live = [
                    lax.dynamic_slice_in_dim(every, where * half, half, 1)
                    for where in (side, 1 - side)
                ]
            return
        if k == 1:
            self.live.append(swap_bit(self.live[0], "tensor", 0))
        elif k == 2:
            own, other = self.live
            even = self.here % 2 == 0
            pair = [jnp.where(even, own, other), jnp.where(even, other, own)]
            near = jnp.concatenate(pair, axis=1)
            self.live = [near, lax.ppermute(near, "tensor", [(1, 2), (2, 1)])]
        else:
            near, far = self.live
            last = lax.ppermute(far, "tensor", [(1, 0), (2, 3)])
            self.live = [near, far, last]

    def pair(self):
        if self.size != 4:
            return self.live
        near, far, last = self.live
        inner = (self.here == 1) | (self.here == 2)
        return [near, jnp.where(inner, far, last)]


class PairReduce:
    def __init__(self, parts):
        self.live = [parts]
        self.size = lax.axis_size("tensor")
        self.here = lax.axis_index("tensor")

    def advance(self, k):
        parts = self.live[0]
        if self.size != 4:
            if k == 1:
                self.live = [lax.psum_scatter(parts, "tensor", scatter_dimension=0)]
            return
        side = self.here // 2
        away = lax.dynamic_slice_in_dim(parts, 2 - 2 * side, 2, 0)
        if k == 1:
            self.live.append(lax.ppermute(away, "tensor", [(0, 1), (3, 2)]))
        elif k == 2:
            total = (self.live[1].astype(F32) + away.astype(F32)).astype(BF16)
            self.live[1] = lax.ppermute(total, "tensor", [(1, 2), (2, 1)])
        else:
            got = self.live[1]
            other = lax.dynamic_index_in_dim(parts, self.here ^ 1, 0, False).astype(F32)
            more = lax.dynamic_index_in_dim(got, 1 - self.here % 2, 0, False).astype(F32)
            self.live.append(swap_bit((other + more).astype(BF16), "tensor", 0))

    def pieces(self):
        if self.size != 4:
            return [(self.live[0], None)]
        parts, got, last = self.live
        return [(parts, lambda m: m[1]), (got, lambda m: m[1] % 2), (last, None)]


class LineReduce:
    def __init__(self, parts, axis=0):
        self.live = [parts]
        self.axis = axis
        self.size = lax.axis_size("tensor")
        self.here = lax.axis_index("tensor")

    def term(self, which):
        which = jnp.clip(which, 0, self.size - 1)
        return lax.dynamic_index_in_dim(self.live[0], which, self.axis, keepdims=False)

    def advance(self, k):
        size = self.size
        for step in third(k, size - 1):
            ahead = self.term(self.here + size - step)
            behind = self.term(self.here - size + step)
            if step > 1:
                ahead = (self.live[1].astype(F32) + ahead.astype(F32)).astype(BF16)
                behind = (self.live[2].astype(F32) + behind.astype(F32)).astype(BF16)
            up = lax.ppermute(ahead, "tensor", [(i, i + 1) for i in range(step)])
            down = lax.ppermute(behind, "tensor", [(i, i - 1) for i in range(size - step, size)])
            self.live[1:] = [up, down]

    def total(self):
        own = self.term(self.here).astype(F32)
        return own + self.live[1].astype(F32) + self.live[2].astype(F32)


class DpSum:
    def __init__(self, send, keep, cuts):
        self.base = [send, keep]
        self.bits = place_bits(lax.axis_size("dp"))
        self.edges = [keep.shape[-1] * c // cuts for c in range(cuts + 1)]
        self.state = [[] for _ in range(cuts)]
        self.left = [list(range(1, self.bits)) for _ in range(cuts)]

    @property
    def live(self):
        return self.base + [v for values in self.state for v in values]

    @live.setter
    def live(self, values):
        values = list(values)
        self.base = [values.pop(0) for _ in self.base]
        self.state = [[values.pop(0) for _ in state] for state in self.state]

    def core(self):
        self.base = [self.base[1], swap_bit(self.base[0], "dp", 0)]

    def move(self, values, cut):
        left = self.left[cut]
        bit = left[0] if cut % 2 == 0 else left[-1]
        dim = left.index(bit)
        keep = lax.index_in_dim(values, 0, dim, keepdims=False)
        send = lax.index_in_dim(values, 1, dim, keepdims=False)
        left.remove(bit)
        self.state[cut] = [keep, swap_bit(send, "dp", bit)]

    def first(self, *cuts):
        keep, got = self.base
        for cut in cuts:
            columns = slice(self.edges[cut], self.edges[cut + 1])
            total = keep[..., columns].astype(F32) + got[..., columns].astype(F32)
            total = total.astype(BF16).reshape((2,) * (self.bits - 1) + keep.shape[1:-1] + (-1,))
            self.move(total, cut)
        if all(self.state):
            self.base = []

    def second(self, *cuts):
        for cut in cuts:
            while self.left[cut]:
                self.move(self.sum(cut).astype(BF16), cut)

    def sum(self, cut):
        keep, got = self.state[cut]
        return keep.astype(F32) + got.astype(F32)

    def total(self):
        return [self.sum(cut) for cut in range(len(self.state))]


class WeightGather:
    def __init__(self, own, me):
        self.blocks = lax.axis_size("dp")
        self.size = lax.axis_size("tensor")
        self.usual = (self.size, self.blocks) == (4, 8)
        self.me = me
        share = own.shape[1 if self.usual else 0] // self.blocks
        axis = 1 if self.usual else 0
        self.live = [lax.dynamic_slice_in_dim(own, me[0] * share, share, axis)]

    def advance(self, k):
        if not self.usual:
            if k == 0:
                self.live = [lax.all_gather(self.live[0], ("tensor", "dp"), axis=0, tiled=True)]
            return
        if k == 0:
            own = self.live[0]
            self.live += [
                lax.ppermute(own, "tensor", [(i, (i + m) % self.size) for i in range(self.size)])
                for m in range(1, self.size)
            ]
        elif k == 1:
            own, one, two, three = self.live
            even = lax.axis_index("tensor") % 2 == 0
            near = jnp.concatenate([jnp.where(even, own, one), jnp.where(even, three, own)])
            far = jnp.concatenate([jnp.where(even, two, three), jnp.where(even, one, two)])
            self.live = [near, swap_bit(near, "dp", 1), far, swap_bit(far, "dp", 2)]
            self.live += [swap_bit(near, "dp", 0), swap_bit(far, "dp", 0)]
        elif k == 2:
            near, near_one, far, far_one, near_core, far_core = self.live
            self.live = [jnp.stack([near, near_one]), jnp.stack([far, far_one])]
            self.live += [swap_bit(self.live[0], "dp", 2), swap_bit(self.live[1], "dp", 1)]
            self.live += [near_core[None], far_core[None], far_one]
            self.live += [swap_bit(near_one, "dp", 0)[None]]
        else:
            near, far, near_two, far_two, near_core, far_core, far_one, near_one_core = self.live
            self.half = self.place([near, near_two, far, far_two], 0, None)
            self.live = [near_core, near_one_core, swap_bit(near_two, "dp", 0)]
            self.live += [far_core, swap_bit(far_one, "dp", 0)[None], swap_bit(far_two, "dp", 0)]
            self.live += [self.half]

    def place(self, arrays, core, half):
        rows, width = arrays[0].shape[1:]
        starts = [0]
        for array in arrays:
            starts.append(starts[-1] + array.shape[0])

        def kernel(me_ref, *refs):
            step = pl.program_id(0)
            for q in range(len(arrays)):

                @pl.when((step >= starts[q]) & (step < starts[q + 1]))
                def _():
                    refs[-1][...] = refs[q][...]

        def source(q):
            last = arrays[q].shape[0] - 1
            return pl.BlockSpec(
                (None, rows, width), lambda s, m: (jnp.clip(s - starts[q], 0, last), 0, 0)
            )

        def target(s, m):
            one, two = s & 1, (s >> 1) & 1
            low = jnp.where(s < 4, 2 * one + 4 * two, 4 * one + 2 * two)
            return (jnp.where(s < 4, m[2], 1 - m[2]), (low + core) ^ m[0])

        more = [] if half is None else [half]
        return pl.pallas_call(
            kernel,
            grid_spec=pltpu.PrefetchScalarGridSpec(
                num_scalar_prefetch=1,
                grid=(8,),
                in_specs=[source(q) for q in range(len(arrays))]
                + [pl.BlockSpec(memory_space=pl.ANY)] * len(more),
                out_specs=pl.BlockSpec((rows, width), target),
            ),
            out_shape=jax.ShapeDtypeStruct((2 * rows, 8 * width), BF16),
            input_output_aliases={1 + len(arrays): 0} if more else {},
            compiler_params=pltpu.CompilerParams(vmem_limit_bytes=32 * 2**20),
            cost_estimate=cost(2**20),
        )(self.me, *arrays, *more)

    def whole(self):
        if not self.usual:
            return self.live[0]
        return self.place(self.live[:6], 1, self.live[6])


class SmallSum:
    def __init__(self, vectors, me):
        self.vectors = vectors
        self.blocks = blocks = lax.axis_size("dp")
        self.bits = place_bits(blocks)
        places = jnp.stack([xor_source(p, me, self.bits) for p in range(blocks)]).reshape(-1)
        self.ordered = sorted(range(len(vectors)), key=lambda i: not vectors[i][1])
        wide = [vectors[i][0].reshape(blocks, -1) for i in self.ordered]
        wide = jnp.take(jnp.concatenate(wide, axis=1), places, axis=0)
        self.live = [wide.reshape((2,) * self.bits + wide.shape[1:])]

    def move(self):
        values = self.live[0]
        self.live = [values[0] + swap_bit(values[1], "dp", self.bits - values.ndim + 1)]

    def finish(self):
        while self.live[0].ndim > 1:
            self.move()
        values = self.live[0]
        both = sum(v[0].shape[0] // self.blocks for v in self.vectors if v[1])
        summed, alone = values[:both], values[both:]
        for bit in range(place_bits(lax.axis_size("tensor"))):
            summed = summed + swap_bit(summed, "tensor", bit)
        self.live = [jnp.concatenate([summed, alone])]

    def total(self):
        out, start = [None] * len(self.vectors), 0
        for i in self.ordered:
            size = self.vectors[i][0].shape[0] // self.blocks
            out[i] = self.live[0][start : start + size]
            start += size
        return out


def on_device(
    inputs,
    segments,
    cotangent,
    norm1_gain,
    norm1_bias,
    query_weight,
    query_bias,
    key_weight,
    value_weight,
    value_bias,
    output_weight,
    output_bias,
    norm2_gain,
    norm2_bias,
    up_weight,
    up_bias,
    down_weight,
    down_bias,
):
    groups = lax.axis_size("tensor")
    blocks = lax.axis_size("dp")
    here = lax.axis_index("tensor").astype(jnp.int32)
    side = here // (groups // 2)
    me = lax.axis_index("dp").astype(jnp.int32)
    me = jnp.stack([me, here, side])
    place = jnp.stack([here, side])
    rows, width = inputs.shape
    share = rows // groups
    part = share // PARTS
    local = query_weight.shape[1]
    size = width // blocks

    def by_part(values):
        return values.reshape(groups, PARTS, part, values.shape[1])

    def own(values):
        return lax.dynamic_slice_in_dim(values, here * share, share, 0)

    def own_heads(values):
        values = values.reshape(groups, part, values.shape[1])
        return lax.dynamic_index_in_dim(values, here, 0, keepdims=False)

    def all_to_all(d_att):
        got = []
        for m in range(groups):
            to = (here - m) % groups
            piece = lax.dynamic_slice_in_dim(d_att, to * local, local, 1)
            if m > 0:
                ring = [(i, (i - m) % groups) for i in range(groups)]
                piece = lax.ppermute(piece, "tensor", ring)
            got.append(piece)
        return got

    weight = WeightGather(output_weight, me)
    weight.advance(0)
    normed, query, key, value = project(
        inputs,
        norm1_gain,
        norm1_bias,
        query_weight,
        query_bias,
        key_weight,
        value_weight,
        value_bias,
    )
    attended = attend(segments, query, key, value)
    gather = [
        Gather(by_part(attended)[:, c].reshape(groups * part, local)) for c in range(PARTS)
    ]
    (cot,) = fence([weight] + gather, (cotangent,))

    gather[0].advance(1)
    weight.advance(1)
    cot_parts = by_part(cot)
    cots = [(cot_parts, c) for c in range(PARTS)]
    d_hidden = both_parts(cots, down_weight, True, down_weight.shape[0])
    (d_hidden, cot) = fence([weight] + gather, (d_hidden, cot))

    gather[0].advance(2)
    gather[1].advance(1)
    weight.advance(2)
    cot_sum = column_sums(cot)
    (cot_sum,) = fence([weight] + gather, (cot_sum,))

    gather[0].advance(3)
    gather[1].advance(2)
    weight.advance(3)
    fence([weight] + gather)

    own_mid, low, hidden, d_up, pairs, heads = ([None] * PARTS for _ in range(6))

    def middle(c):
        pairs[c] = gather[c].pair()
        own_mid[c], low[c], hidden[c], d_up[c], terms = middle_call(
            c,
            place,
            *pairs[c],
            whole,
            by_part(inputs),
            output_bias,
            norm2_gain,
            norm2_bias,
            up_weight,
            up_bias,
            d_hidden,
        )
        return PairReduce(terms.reshape(groups, part, width))

    gather[1].advance(3)
    whole = weight.whole()
    reduce_up = [middle(0), None]
    (whole,) = fence([gather[1], reduce_up[0]], (whole,))

    reduce_up[0].advance(1)
    reduce_up[1] = middle(1)
    hidden[0], hidden[1], d_up[0], d_up[1], *heads = fence(
        reduce_up, (*hidden, *d_up, *pairs[0], *pairs[1])
    )

    reduce_up[0].advance(2)
    reduce_up[1].advance(1)
    out_terms = both_parts(hidden, down_weight, False, width)
    reduce_out = LineReduce(out_terms.reshape(PARTS, groups, part, width), 1)
    heads = [own_heads(v) for v in heads]
    attended_own = [jnp.concatenate(heads[k::2], axis=0) for k in range(2)]
    d_up[0], d_up[1], *attended_own = fence(reduce_up + [reduce_out], (*d_up, *attended_own))

    reduce_up[0].advance(3)
    reduce_up[1].advance(2)
    reduce_out.advance(1)
    mlp_terms = gradient_terms([(low, d_up), (cots, hidden)], me, blocks, True)
    up_sum = column_sums(d_up[0]) + column_sums(d_up[1])
    *mlp_terms, up_sum = fence(reduce_up + [reduce_out], (*mlp_terms, up_sum))

    d_mids, d_branches, sums, got = ([None] * PARTS for _ in range(4))
    reduce_up[1].advance(3)
    mlp_got = swap_bit(mlp_terms[0], "dp", 0)

    def back(c):
        d_mids[c], d_branches[c], sums[c], d_att = middle_back(
            c, me, reduce_up[c].pieces(), own_mid[c], cotangent, norm2_gain, whole
        )
        got[c] = all_to_all(d_att)

    back(0)
    *got[0], d_branches[0], mlp_got = fence(
        [reduce_up[1], reduce_out], (*got[0], d_branches[0], mlp_got)
    )

    back(1)
    reduce_out.advance(2)
    mlp_sum = (mlp_terms[1].astype(F32) + mlp_got.astype(F32)).astype(BF16)
    wo_sum = DpSum(
        *gradient_terms(
            [([d_branches[c] for c in range(PARTS)], [v[c * part : (c + 1) * part] for c in range(PARTS)]) for v in attended_own],
            me,
            blocks,
        ),
        2,
    )
    *got[1], mlp_sum = fence([reduce_out, wo_sum], (*got[1], mlp_sum))

    reduce_out.advance(3)
    wo_sum.core()
    same_core = [list(range(c, blocks, 2)) for c in range(2)]
    mlp_sum = lax.psum_scatter(
        mlp_sum, "dp", scatter_dimension=0, axis_index_groups=same_core
    )
    d_query, d_key, d_value = attend_back(segments, query, key, value, got, me)
    d_query, d_key, d_value = fence([reduce_out, wo_sum], (d_query, d_key, d_value))

    wo_sum.first(0, 1)
    terms_in, gain1, bias1 = normed_back(
        d_query, d_key, d_value, query_weight, key_weight, value_weight, inputs
    )
    reduce_in = LineReduce(terms_in.reshape(groups, share, width))
    d_query, d_key, d_value, normed, gain1, bias1 = fence(
        [reduce_in, wo_sum], (d_query, d_key, d_value, normed, gain1, bias1)
    )

    reduce_in.advance(1)
    wo_sum.second(0, 1)
    qkv_sum = DpSum(
        *gradient_terms([([normed], [d]) for d in (d_query, d_key, d_value)], me, blocks), 2
    )
    two = sums[0] + sums[1]
    small = SmallSum(
        [
            (gain1[0], True),
            (bias1[0], True),
            (two[0], True),
            (two[1], True),
            (two[2], True),
            (cot_sum, False),
            (column_sums(d_query), False),
            (column_sums(d_value), False),
            (up_sum, False),
        ],
        me[:1],
    )
    fence([reduce_in, wo_sum, qkv_sum, small])

    reduce_in.advance(2)
    qkv_sum.core()
    small.move()
    total = reduce_out.total()
    outputs = [(own_mid[c] + (total[c] + down_bias)).astype(BF16) for c in range(PARTS)]
    output = jnp.concatenate(outputs, axis=0)
    average, inverse = row_stats(own(inputs).astype(F32))
    wo_terms = jnp.concatenate(wo_sum.total(), axis=1).T
    wo_terms = wo_terms.astype(BF16).reshape(groups, local, size)
    wo_terms, output, average, inverse = fence(
        [reduce_in, qkv_sum, small], (wo_terms, output, average, inverse)
    )

    reduce_in.advance(3)
    qkv_sum.first(0, 1)
    small.move()
    (mlp_sum,) = fence([reduce_in, qkv_sum, small], (mlp_sum,))

    qkv_sum.second(0, 1)
    small.finish()
    output_weight_grad = 0.0
    for m in range(groups):
        to = (here - m) % groups
        away = jnp.where(to // (groups // 2) == side, 0, groups // 2)
        piece = lax.dynamic_index_in_dim(wo_terms, away + to % (groups // 2), 0, keepdims=False)
        if m > 0:
            ring = [(i, (i - m) % groups) for i in range(groups)]
            piece = lax.ppermute(piece, "tensor", ring)
        output_weight_grad = output_weight_grad + piece.astype(F32)
    xhat = (own(inputs).astype(F32) - average) * inverse
    d_mid = jnp.concatenate(d_mids, axis=0)
    input_grad = d_mid + norm_back(reduce_in.total(), norm1_gain, xhat, inverse)
    hidden_width = up_weight.shape[1]
    mlp_sum = mlp_sum.astype(F32)
    qkv_grad = jnp.concatenate(qkv_sum.total(), axis=1)
    (
        norm1_gain_grad,
        norm1_bias_grad,
        norm2_gain_grad,
        norm2_bias_grad,
        output_bias_grad,
        down_bias_grad,
        query_bias_grad,
        value_bias_grad,
        up_bias_grad,
    ) = small.total()
    return (
        output,
        input_grad,
        norm1_gain_grad,
        norm1_bias_grad,
        qkv_grad[:, :local],
        query_bias_grad,
        qkv_grad[:, local : 2 * local],
        qkv_grad[:, 2 * local :],
        value_bias_grad,
        output_weight_grad,
        output_bias_grad,
        norm2_gain_grad,
        norm2_bias_grad,
        mlp_sum[:, :hidden_width],
        up_bias_grad,
        mlp_sum[:, hidden_width:].T,
        down_bias_grad,
    )


def solution(mesh):
    return jax.shard_map(
        on_device,
        mesh=mesh,
        in_specs=(
            P("dp", None),
            P("dp", None),
            P("dp", None),
            P(),
            P(),
            P(None, "tensor"),
            P("tensor"),
            P(None, "tensor"),
            P(None, "tensor"),
            P("tensor"),
            P("tensor", None),
            P(),
            P(),
            P(),
            P(None, "tensor"),
            P("tensor"),
            P("tensor", None),
            P(),
        ),
        out_specs=(
            P(("dp", "tensor"), None),
            P(("dp", "tensor"), None),
            P("dp"),
            P("dp"),
            P("dp", "tensor"),
            P(("tensor", "dp")),
            P("dp", "tensor"),
            P("dp", "tensor"),
            P(("tensor", "dp")),
            P("tensor", "dp"),
            P("dp"),
            P("dp"),
            P("dp"),
            P("dp", "tensor"),
            P(("tensor", "dp")),
            P("tensor", "dp"),
            P("dp"),
        ),
        check_vma=False,
    )
```

time: 1820 us -> 602 us (0.33)
  waiting for transfers between devices: 1470 us -> 119 us
  matrix products: 213 us -> 0 us
  Pallas kernels: 0 us -> 213 us
  starting transfers between devices: 0.99 us -> 117 us
  local copies, waits for them, and re-layouts: 12.9 us -> 52.7 us
  blocking collectives: 25.1 us -> 0 us
    psum x3 -> x0, waiting for transfers between devices: 1060 us -> none  [the longest x1 499 us: on_device(): lax.psum(jnp.dot(hidden, down_weight, preferred_element_type=jnp.float32)...]
    reduce_scatter x6 -> x0, waiting for transfers between devices: 412 us -> none  [the longest x1 120 us: on_device(): lax.psum_scatter(down_weight_grad, 'dp', scatter_dimension=1, tiled=True)]
    pallas_call x0 -> x15, Pallas kernels: none -> 213 us  [the longest x2 54.3 us: middle_call(): pl.pallas_call(functools.partial(middle_kernel, (first, second)), grid_sp...]
    dot_general x24 -> x0, matrix products: 213 us -> none  [the longest x6 61.1 us: times_trans(): lax.dot_general(left_side, right_side, (((1,), (1,)), ((), ())), preferre...]
    ppermute x0 -> x62, waiting for transfers between devices: none -> 119 us  [the longest x30 39.4 us: swap_bit(): return lax.ppermute(values, axis, [(i, i ^ 1 << bit) for i in range(size)])]
    ppermute x0 -> x62, starting transfers between devices: none -> 117 us  [the longest x6 28.8 us: advance(): up = lax.ppermute(ahead, 'tensor', [(i, i + 1) for i in range(step)])]
    reduce_sum x10 -> x8, other arithmetic: 49.7 us -> 6.43 us  [the longest x5 2.39 us: column_sums(): return jnp.sum(values.astype(F32), axis=0)]
    unnamed x1 -> x0, blocking collectives: 25.1 us -> none
  transfers between devices with their start and end apart: 9 -> 63, of which waited for: 9 -> 16; matrix products, arithmetic and copies ran while one was open for 6% -> 17% of each run, Pallas kernels for 0% -> 34%
where the time goes in v1:
time: 602 us; the launch traced here: 596 us
  Pallas kernels  213 us (35%)
  waiting for transfers between devices  119 us (20%)
  starting transfers between devices  117 us (19%)
  other arithmetic  78.4 us (13%)
  local copies, waits for them, and re-layouts  52.7 us (9%)
  between operations  15.9 us (3%)
    pallas_call x2, Pallas kernels, middle_call(): pl.pallas_call(functools.partial(middle_kernel, (first, second)), grid_sp...  54.3 us
    pallas_call x3, Pallas kernels, gradient_terms(): pl.pallas_call(kernel, grid_spec=pltpu.PrefetchScalarGridSpec(num_scalar_...  52.7 us
    ppermute x30, waiting for transfers between devices, swap_bit(): return lax.ppermute(values, axis, [(i, i ^ 1 << bit) for i in range(size)])  39.4 us
    ppermute x6, starting transfers between devices, advance(): up = lax.ppermute(ahead, 'tensor', [(i, i + 1) for i in range(step)])  28.8 us
    pallas_call x2, Pallas kernels, both_parts(): pl.pallas_call(kernel, grid=(columns // block,), in_specs=[left_spec(left...  26.9 us
    ppermute x30, starting transfers between devices, swap_bit(): return lax.ppermute(values, axis, [(i, i ^ 1 << bit) for i in range(size)])  26.3 us
    ppermute x2, waiting for transfers between devices, advance(): last = lax.ppermute(far, 'tensor', [(1, 0), (2, 3)])  22.8 us
    ppermute x6, waiting for transfers between devices, advance(): up = lax.ppermute(ahead, 'tensor', [(i, i + 1) for i in range(step)])  19.8 us
  transfers between devices with their start and end apart: 63, of which 16 were waited for; matrix products, arithmetic and copies ran while one was open for 17% of the time, Pallas kernels for 34%

profile of v1, /device:TPU:0, one launch (start us, length us, event | category | flops | bytes accessed | tf_op | source)
XLA Modules:
  0.0 595.9 jit_solution(14134520390250839938)
XLA Ops:
  16.8 13.5 %shard_map.305 = (bf16[1024,2048]{1,0:T(8,128)(2,1)}, bf16[1024,512]{1,0:T(8,128)(2,1)}, bf16[1024,512]{1,0:T(8,128)(2,1)}, bf16[1024,512]{1,0:T(8,128)(2,1)}) custom-call(bf16[1024,2048]{1,0:T(8,128)(2,1)} %x.3, f32[1,2048]{1,0:T(1,128)} %bitcast.238, f32[1,2048]{1,0:T(1,128)} %bitcast.239, bf16[2048,512]{1,0:T(8,128)(2,1)} %wq.3, f32[1,512]{1,0:T(1,128)} %bitcast.246, ...), custom_call_target="tpu_custom_call" | custom-call | flops 6442450944 | bytes 16777216 | tf_op jit(solution)/shard_map/pallas_call | solution.py:202
  34.0 7.4 %shard_map.306 = bf16[1024,512]{1,0:T(8,128)(2,1)S(1)} custom-call(s32[1,1,1024]{2,1,0:T(1,128)S(1)} %bitcast.196, s32[1,1024,1]{2,1,0:T(8,128)S(1)} %copy.70.seg_col, bf16[1024,512]{1,0:T(8,128)(2,1)S(1)} %copy-done.34, bf16[1024,512]{1,0:T(8,128)(2,1)S(1)} %copy-done.36, bf16[1024,512]{1,0:T(8,128)(2,1)S(1)} %copy-done.37), custom_call_target="tpu_custom_call" | custom-call | flops 2147483648 | bytes 16777216 | tf_op jit(solution)/shard_map/pallas_call | solution.py:120
  45.7 13.4 %shard_map.307.d_hid = bf16[2,512,2048]{2,1,0:T(8,128)(2,1)} custom-call(bf16[4,2,128,2048]{3,2,1,0:T(8,128)(2,1)} %bitcast.198, bf16[4,2,128,2048]{3,2,1,0:T(8,128)(2,1)} %bitcast.199, bf16[2048,2048]{1,0:T(8,128)(2,1)} %refs_2_.3), custom_call_target="tpu_custom_call" | custom-call | flops 8589934592 | bytes 16777216 | tf_op jit(solution)/shard_map/pallas_call | solution.py:511
  68.4 11.5 %collective-permute-done.12 = bf16[512,512]{1,0:T(8,128)(2,1)S(1)} collective-permute-done((bf16[512,512]{1,0:T(8,128)(2,1)S(1)}, bf16[512,512]{1,0:T(8,128)(2,1)S(1)}, u32[]{:S(2)}, u32[]{:S(2)}) %collective-permute-start.12) | collective-permute-done | bytes 524320 | tf_op jit(solution)/shard_map/ppermute | solution.py:524
  79.9 8.5 %collective-permute-done.9.refs_3_ = bf16[2,1024,256]{2,1,0:T(8,128)(2,1)S(1)} collective-permute-done((bf16[2,1024,256]{2,1,0:T(8,128)(2,1)S(1)}, bf16[2,1024,256]{2,1,0:T(8,128)(2,1)S(1)}, u32[]{:S(2)}, u32[]{:S(2)}) %collective-permute-start.9) | collective-permute-done | bytes 1048608 | tf_op jit(solution)/shard_map/ppermute | solution.py:524
  99.2 22.8 %collective-permute-done.16 = bf16[512,1024]{1,0:T(8,128)(2,1)} collective-permute-done((bf16[512,1024]{1,0:T(8,128)(2,1)}, bf16[512,1024]{1,0:T(8,128)(2,1)}, u32[]{:S(2)}, u32[]{:S(2)}) %collective-permute-start.16) | collective-permute-done | bytes 1048608 | tf_op jit(solution)/shard_map/ppermute | solution.py:568
  134.2 27.1 %shard_map.310 = (f32[128,2048]{1,0:T(8,128)}, bf16[512,2048]{1,0:T(8,128)(2,1)}, bf16[512,2048]{1,0:T(8,128)(2,1)}, bf16[512,2048]{1,0:T(8,128)(2,1)}, bf16[512,2048]{1,0:T(8,128)(2,1)}) custom-call(s32[2]{0:T(128)} %pad_add_fusion.1.here_ref, bf16[512,1024]{1,0:T(8,128)(2,1)} %copy-done.59, bf16[512,1024]{1,0:T(8,128)(2,1)} %broadcast_select_fusion.1.far, ...), custom_call_target="tpu_custom_call" | custom-call | flops 12884901888 | bytes 16777216 | tf_op jit(solution)/shard_map/pallas_call | solution.py:275
  168.5 27.2 %shard_map.311 = (f32[128,2048]{1,0:T(8,128)}, bf16[512,2048]{1,0:T(8,128)(2,1)}, bf16[512,2048]{1,0:T(8,128)(2,1)}, bf16[512,2048]{1,0:T(8,128)(2,1)}, bf16[512,2048]{1,0:T(8,128)(2,1)}) custom-call(s32[2]{0:T(128)} %pad_add_fusion.1.here_ref, bf16[512,1024]{1,0:T(8,128)(2,1)} %pad_maximum_fusion.3.near, bf16[512,1024]{1,0:T(8,128)(2,1)} %broadcast_select_fusion.far, ...), custom_call_target="tpu_custom_call" | custom-call | flops 12884901888 | bytes 16777216 | tf_op jit(solution)/shard_map/pallas_call | solution.py:275
  205.6 13.5 %shard_map.312 = bf16[2,512,2048]{2,1,0:T(8,128)(2,1)} custom-call(bf16[512,2048]{1,0:T(8,128)(2,1)} %get-tuple-element.259.refs_0_.refs_6_, bf16[512,2048]{1,0:T(8,128)(2,1)} %get-tuple-element.260.refs_1_.refs_7_, bf16[2048,2048]{1,0:T(8,128)(2,1)} %refs_2_.3), custom_call_target="tpu_custom_call" | custom-call | flops 8589934592 | bytes 16777216 | tf_op jit(solution)/shard_map/pallas_call | solution.py:511
  222.9 11.0 %collective-permute-start.23 = (bf16[2,128,2048]{2,1,0:T(8,128)(2,1)}, bf16[2,128,2048]{2,1,0:T(8,128)(2,1)S(1)}, u32[]{:S(2)}, u32[]{:S(2)}) collective-permute-start(bf16[2,128,2048]{2,1,0:T(8,128)(2,1)} %add_convert_fusion.7), channel_id=1, source_target_pairs={{1,2},{2,1},{5,6},{6,5},{9,10},{10,9},{13,14},{14,13},{17,18},{18,... | collective-permute-start | bytes 3145736 | tf_op jit(solution)/shard_map/ppermute | solution.py:597
  237.1 9.7 %collective-permute-start.24 = (bf16[2,128,2048]{2,1,0:T(8,128)(2,1)}, bf16[2,128,2048]{2,1,0:T(8,128)(2,1)}, u32[]{:S(2)}, u32[]{:S(2)}) collective-permute-start(bf16[2,128,2048]{2,1,0:T(8,128)(2,1)} %get-tuple-element.456), channel_id=1, source_target_pairs={{0,1},{4,5},{8,9},{12,13},{16,17},{20,21},{24,25},{28,29}} | collective-permute-start | bytes 3145736 | tf_op jit(solution)/shard_map/ppermute | solution.py:630
  249.4 26.4 %shard_map.313 = (bf16[4,256,4096]{2,1,0:T(8,128)(2,1)}, bf16[4,256,4096]{2,1,0:T(8,128)(2,1)}) custom-call(s32[3]{0:T(128)} %copy-done.24, bf16[512,2048]{1,0:T(8,128)(2,1)} %get-tuple-element.272.refs_0_, bf16[512,2048]{1,0:T(8,128)(2,1)} %get-tuple-element.273.refs_1_, bf16[4,2,128,2048]{3,2,1,0:T(8,128)(2,1)} %bitcast.200, ...), custom_call_target="tpu_custom_call" | custom-call | flops 17179869184 | bytes 16777216 | tf_op jit(solution)/shard_map/pallas_call | solution.py:432
  284.6 8.2 %shard_map.314 = (f32[128,2048]{1,0:T(8,128)S(1)}, bf16[128,2048]{1,0:T(8,128)(2,1)S(1)}, f32[8,2048]{1,0:T(8,128)S(1)}, bf16[128,2048]{1,0:T(8,128)(2,1)S(1)}) custom-call(s32[3]{0:T(128)S(1)} %copy-done.25, bf16[4,128,2048]{2,1,0:T(8,128)(2,1)} %bitcast.216, bf16[2,128,2048]{2,1,0:T(8,128)(2,1)S(1)} %collective-permute-done.20.refs_1_, ...), custom_call_target="tpu_custom_call" | custom-call | flops 1073741824 | bytes 16777216 | tf_op jit(solution)/shard_map/pallas_call | solution.py:357
  302.1 7.8 %collective-permute-done.28.refs_2_ = bf16[128,512]{1,0:T(8,128)(2,1)S(1)} collective-permute-done((bf16[128,512]{1,0:T(8,128)(2,1)S(1)}, bf16[128,512]{1,0:T(8,128)(2,1)S(1)}, u32[]{:S(2)}, u32[]{:S(2)}) %collective-permute-start.28) | collective-permute-done | bytes 131104 | tf_op jit(solution)/shard_map/ppermute | solution.py:864
  311.2 8.4 %shard_map.315 = (f32[128,2048]{1,0:T(8,128)S(1)}, bf16[128,2048]{1,0:T(8,128)(2,1)S(1)}, f32[8,2048]{1,0:T(8,128)S(1)}, bf16[128,2048]{1,0:T(8,128)(2,1)S(1)}) custom-call(s32[3]{0:T(128)S(1)} %copy-done.25, bf16[4,128,2048]{2,1,0:T(8,128)(2,1)} %bitcast.213, bf16[2,128,2048]{2,1,0:T(8,128)(2,1)S(1)} %collective-permute-done.23.refs_1_, ...), custom_call_target="tpu_custom_call" | custom-call | flops 1073741824 | bytes 16777216 | tf_op jit(solution)/shard_map/pallas_call | solution.py:357
  332.7 10.1 %add_convert_fusion = bf16[4,256,4096]{2,1,0:T(8,128)(2,1)} fusion(bf16[4,256,4096]{2,1,0:T(8,128)(2,1)} %collective-permute-done.30, bf16[4,256,4096]{2,1,0:T(8,128)(2,1)} %get-tuple-element.304), kind=kLoop, calls=%fused_computation.1 | loop fusion | flops 16777216 | bytes 25165824 | tf_op jit(solution)/shard_map/convert_element_type | solution.py:966
  342.9 11.2 %shard_map.316 = (bf16[4,256,2048]{2,1,0:T(8,128)(2,1)}, bf16[4,256,2048]{2,1,0:T(8,128)(2,1)}) custom-call(s32[3]{0:T(128)} %copy-done.24, bf16[128,2048]{1,0:T(8,128)(2,1)} %copy-done.28, bf16[128,2048]{1,0:T(8,128)(2,1)} %copy-done.29, bf16[128,2048]{1,0:T(8,128)(2,1)} %copy-done.28, bf16[128,2048]{1,0:T(8,128)(2,1)} %copy-done.29, ...), custom_call_target="tpu_custom_call" | custom-call | flops 2147483648 | bytes 16777216 | tf_op jit(solution)/shard_map/pallas_call | solution.py:432
  367.5 17.4 %shard_map.317 = (bf16[1024,512]{1,0:T(8,128)(2,1)S(1)}, bf16[1024,512]{1,0:T(8,128)(2,1)S(1)}, bf16[1024,512]{1,0:T(8,128)(2,1)S(1)}) custom-call(s32[3]{0:T(128)S(1)} %copy-done.26, s32[1,1,1024]{2,1,0:T(1,128)S(1)} %bitcast.197, s32[1,1024,1]{2,1,0:T(8,128)S(1)} %copy-done.22, bf16[1024,512]{1,0:T(8,128)(2,1)S(1)} %copy-done.35, ...), custom_call_target="tpu_custom_call" | custom-call | flops 5368709120 | bytes 16777216 | tf_op jit(solution)/shard_map/pallas_call | solution.py:140
  401.0 15.4 %shard_map.318 = (bf16[1024,2048]{1,0:T(8,128)(2,1)}, f32[1,2048]{1,0:T(1,128)}, f32[1,2048]{1,0:T(1,128)}) custom-call(bf16[1024,512]{1,0:T(8,128)(2,1)} %copy-done.11, bf16[1024,512]{1,0:T(8,128)(2,1)} %copy-done.38, bf16[1024,512]{1,0:T(8,128)(2,1)} %copy-done.9, bf16[2048,512]{1,0:T(8,128)(2,1)} %wq.3, bf16[2048,512]{1,0:T(8,128)(2,1)} %wk.3, ...), custom_call_target="tpu_custom_call" | custom-call | flops 6442450944 | bytes 16777216 | tf_op jit(solution)/shard_map/pallas_call | solution.py:473
  416.5 15.5 %collective-permute-done.39 = bf16[2,256,1024]{2,1,0:T(8,128)(2,1)} collective-permute-done((bf16[2,256,1024]{2,1,0:T(8,128)(2,1)}, bf16[2,256,1024]{2,1,0:T(8,128)(2,1)}, u32[]{:S(2)}, u32[]{:S(2)}) %collective-permute-start.39) | collective-permute-done | bytes 1048608 | tf_op jit(solution)/shard_map/ppermute | solution.py:524
  447.5 15.1 %shard_map.319 = (bf16[4,256,1536]{2,1,0:T(8,128)(2,1)}, bf16[4,256,1536]{2,1,0:T(8,128)(2,1)}) custom-call(s32[3]{0:T(128)} %copy-done.24, bf16[1024,2048]{1,0:T(8,128)(2,1)} %get-tuple-element.336.refs_0_.refs_1_.refs_2_, bf16[1024,2048]{1,0:T(8,128)(2,1)} %get-tuple-element.336.refs_0_.refs_1_.refs_2_, ...), custom_call_target="tpu_custom_call" | custom-call | flops 6442450944 | bytes 16777216 | tf_op jit(solution)/shard_map/pallas_call | solution.py:432
  483.2 18.4 %collective-permute-done.45 = bf16[256,2048]{1,0:T(8,128)(2,1)} collective-permute-done((bf16[256,2048]{1,0:T(8,128)(2,1)}, bf16[256,2048]{1,0:T(8,128)(2,1)}, u32[]{:S(2)}, u32[]{:S(2)}) %collective-permute-start.45) | collective-permute-done | bytes 1048608 | tf_op jit(solution)/shard_map/ppermute | solution.py:630
  505.2 5.5 collective-permute-start.59
  536.4 18.2 %collective-permute-done.61 = bf16[512,256]{1,0:T(8,128)(2,1)S(1)} collective-permute-done((bf16[512,256]{1,0:T(8,128)(2,1)S(1)}, bf16[512,256]{1,0:T(8,128)(2,1)S(1)}, u32[]{:S(2)}, u32[]{:S(2)}) %collective-permute-start.61) | collective-permute-done | bytes 262176 | tf_op jit(solution)/shard_map/ppermute | solution.py:1044
  (382 shorter events, 236.8 us)
Async XLA Ops:
  7.2 551.0 %reduce-scatter.4.cloned.1.call-start = ((), (), s32[]{:S(2)}) async-start(), calls=%async_computation.1 | async-start | bytes 10485760
  8.8 32.6 %collective-permute-start = (bf16[512,256]{1,0:T(8,128)(2,1)S(1)}, bf16[512,256]{1,0:T(8,128)(2,1)S(1)}, u32[]{:S(2)}, u32[]{:S(2)}) collective-permute-start(bf16[512,256]{1,0:T(8,128)(2,1)S(1)} %constant_dynamic-slice_fusion.13), channel_id=1, source_target_pairs={{0,1},{1,2},{2,3},{3,0},{4,5},{5,6},{6,7},{7,4},{8,9},{9,10},{10,1... | collective-permute-start | bytes 786440 | tf_op jit(solution)/shard_map/ppermute | solution.py:710
  11.9 29.6 %collective-permute-start.1 = (bf16[512,256]{1,0:T(8,128)(2,1)S(1)}, bf16[512,256]{1,0:T(8,128)(2,1)S(1)}, u32[]{:S(2)}, u32[]{:S(2)}) collective-permute-start(bf16[512,256]{1,0:T(8,128)(2,1)S(1)} %constant_dynamic-slice_fusion.13), channel_id=1, source_target_pairs={{0,2},{1,3},{2,0},{3,1},{4,6},{5,7},{6,4},{7,5},{8,10},{9,11},{10,... | collective-permute-start | bytes 786440 | tf_op jit(solution)/shard_map/ppermute | solution.py:710
  93.3 28.7 %collective-permute-start.16 = (bf16[512,1024]{1,0:T(8,128)(2,1)}, bf16[512,1024]{1,0:T(8,128)(2,1)}, u32[]{:S(2)}, u32[]{:S(2)}) collective-permute-start(bf16[512,1024]{1,0:T(8,128)(2,1)} %collective-permute-done.11), channel_id=1, source_target_pairs={{1,0},{2,3},{5,4},{6,7},{9,8},{10,11},{13,12},{14,15},{17,16},{18,... | collective-permute-start | bytes 3145736 | tf_op jit(solution)/shard_map/ppermute | solution.py:568
  122.0 39.4 %collective-permute-start.18 = (bf16[512,1024]{1,0:T(8,128)(2,1)}, bf16[512,1024]{1,0:T(8,128)(2,1)S(1)}, u32[]{:S(2)}, u32[]{:S(2)}) collective-permute-start(bf16[512,1024]{1,0:T(8,128)(2,1)} %collective-permute-done.17), channel_id=1, source_target_pairs={{1,0},{2,3},{5,4},{6,7},{9,8},{10,11},{13,12},{14,15},{17,16},{18,... | collective-permute-start | bytes 3145736 | tf_op jit(solution)/shard_map/ppermute | solution.py:568
  162.7 33.0 %collective-permute-start.19 = (bf16[2,128,2048]{2,1,0:T(8,128)(2,1)S(1)}, bf16[2,128,2048]{2,1,0:T(8,128)(2,1)S(1)}, u32[]{:S(2)}, u32[]{:S(2)}) collective-permute-start(bf16[2,128,2048]{2,1,0:T(8,128)(2,1)S(1)} %constant_dynamic-slice_fusion.12), channel_id=1, source_target_pairs={{0,1},{3,2},{4,5},{7,6},{8,9},{11,10},{12,13},{15,14},{16,17},{19,... | collective-permute-start | bytes 3145736 | tf_op jit(solution)/shard_map/ppermute | solution.py:594
  222.9 56.3 %collective-permute-start.23 = (bf16[2,128,2048]{2,1,0:T(8,128)(2,1)}, bf16[2,128,2048]{2,1,0:T(8,128)(2,1)S(1)}, u32[]{:S(2)}, u32[]{:S(2)}) collective-permute-start(bf16[2,128,2048]{2,1,0:T(8,128)(2,1)} %add_convert_fusion.7), channel_id=1, source_target_pairs={{1,2},{2,1},{5,6},{6,5},{9,10},{10,9},{13,14},{14,13},{17,18},{18,... | collective-permute-start | bytes 3145736 | tf_op jit(solution)/shard_map/ppermute | solution.py:597
  237.1 42.1 %collective-permute-start.24 = (bf16[2,128,2048]{2,1,0:T(8,128)(2,1)}, bf16[2,128,2048]{2,1,0:T(8,128)(2,1)}, u32[]{:S(2)}, u32[]{:S(2)}) collective-permute-start(bf16[2,128,2048]{2,1,0:T(8,128)(2,1)} %get-tuple-element.456), channel_id=1, source_target_pairs={{0,1},{4,5},{8,9},{12,13},{16,17},{20,21},{24,25},{28,29}} | collective-permute-start | bytes 3145736 | tf_op jit(solution)/shard_map/ppermute | solution.py:630
  246.8 32.3 %collective-permute-start.25 = (bf16[2,128,2048]{2,1,0:T(8,128)(2,1)}, bf16[2,128,2048]{2,1,0:T(8,128)(2,1)}, u32[]{:S(2)}, u32[]{:S(2)}) collective-permute-start(bf16[2,128,2048]{2,1,0:T(8,128)(2,1)} %get-tuple-element.455), channel_id=1, source_target_pairs={{3,2},{7,6},{11,10},{15,14},{19,18},{23,22},{27,26},{31,30}} | collective-permute-start | bytes 3145736 | tf_op jit(solution)/shard_map/ppermute | solution.py:631
  249.4 29.0 %collective-permute-start.22 = (bf16[128,2048]{1,0:T(8,128)(2,1)}, bf16[128,2048]{1,0:T(8,128)(2,1)S(1)}, u32[]{:S(2)}, u32[]{:S(2)}) collective-permute-start(bf16[128,2048]{1,0:T(8,128)(2,1)} %fusion.26), channel_id=1, source_target_pairs={{0,1},{1,0},{2,3},{3,2},{4,5},{5,4},{6,7},{7,6},{8,9},{9,8},{10,11... | collective-permute-start | bytes 1572872 | tf_op jit(solution)/shard_map/ppermute | solution.py:524
  279.2 32.0 %collective-permute-start.30 = (bf16[4,256,4096]{2,1,0:T(8,128)(2,1)}, bf16[4,256,4096]{2,1,0:T(8,128)(2,1)}, u32[]{:S(2)}, u32[]{:S(2)}) collective-permute-start(bf16[4,256,4096]{2,1,0:T(8,128)(2,1)} %get-tuple-element.289), channel_id=1, source_target_pairs={{0,4},{4,0},{8,12},{12,8},{16,20},{20,16},{24,28},{28,24},{1,5},{5... | collective-permute-start | bytes 25165832 | tf_op jit(solution)/shard_map/ppermute | solution.py:524
  280.6 30.6 %collective-permute-start.26 = (bf16[128,2048]{1,0:T(8,128)(2,1)S(1)}, bf16[128,2048]{1,0:T(8,128)(2,1)S(1)}, u32[]{:S(2)}, u32[]{:S(2)}) collective-permute-start(bf16[128,2048]{1,0:T(8,128)(2,1)S(1)} %fusion.27), channel_id=1, source_target_pairs={{0,1},{1,0},{2,3},{3,2},{4,5},{5,4},{6,7},{7,6},{8,9},{9,8},{10,11... | collective-permute-start | bytes 1572872 | tf_op jit(solution)/shard_map/ppermute | solution.py:524
  319.7 34.3 %collective-permute-start.33 = (bf16[128,512]{1,0:T(8,128)(2,1)S(1)}, bf16[128,512]{1,0:T(8,128)(2,1)S(1)}, u32[]{:S(2)}, u32[]{:S(2)}) collective-permute-start(bf16[128,512]{1,0:T(8,128)(2,1)S(1)} %get-tuple-element.485), channel_id=1, source_target_pairs={{0,3},{1,0},{2,1},{3,2},{4,7},{5,4},{6,5},{7,6},{8,11},{9,8},{10,9... | collective-permute-start | bytes 393224 | tf_op jit(solution)/shard_map/ppermute | solution.py:864
  321.0 33.1 %collective-permute-start.34 = (bf16[128,512]{1,0:T(8,128)(2,1)S(1)}, bf16[128,512]{1,0:T(8,128)(2,1)S(1)}, u32[]{:S(2)}, u32[]{:S(2)}) collective-permute-start(bf16[128,512]{1,0:T(8,128)(2,1)S(1)} %get-tuple-element.484), channel_id=1, source_target_pairs={{0,2},{1,3},{2,0},{3,1},{4,6},{5,7},{6,4},{7,5},{8,10},{9,11},{10,... | collective-permute-start | bytes 393224 | tf_op jit(solution)/shard_map/ppermute | solution.py:864
  321.5 32.6 %collective-permute-start.35 = (bf16[128,512]{1,0:T(8,128)(2,1)S(1)}, bf16[128,512]{1,0:T(8,128)(2,1)S(1)}, u32[]{:S(2)}, u32[]{:S(2)}) collective-permute-start(bf16[128,512]{1,0:T(8,128)(2,1)S(1)} %get-tuple-element.483), channel_id=1, source_target_pairs={{0,1},{1,2},{2,3},{3,0},{4,5},{5,6},{6,7},{7,4},{8,9},{9,10},{10,1... | collective-permute-start | bytes 393224 | tf_op jit(solution)/shard_map/ppermute | solution.py:864
  354.1 36.5 %collective-permute-start.38 = (bf16[4,256,2048]{2,1,0:T(8,128)(2,1)}, bf16[4,256,2048]{2,1,0:T(8,128)(2,1)}, u32[]{:S(2)}, u32[]{:S(2)}) collective-permute-start(bf16[4,256,2048]{2,1,0:T(8,128)(2,1)} %get-tuple-element.310), channel_id=1, source_target_pairs={{0,4},{4,0},{8,12},{12,8},{16,20},{20,16},{24,28},{28,24},{1,5},{5... | collective-permute-start | bytes 12582920 | tf_op jit(solution)/shard_map/ppermute | solution.py:524
  359.2 27.2 %collective-permute-start.36 = (bf16[2,128,2048]{2,1,0:T(8,128)(2,1)S(1)}, bf16[2,128,2048]{2,1,0:T(8,128)(2,1)S(1)}, u32[]{:S(2)}, u32[]{:S(2)}) collective-permute-start(bf16[2,128,2048]{2,1,0:T(8,128)(2,1)S(1)} %get-tuple-element.452), channel_id=1, source_target_pairs={{0,1},{1,2},{2,3},{4,5},{5,6},{6,7},{8,9},{9,10},{10,11},{12,13},{... | collective-permute-start | bytes 3145736 | tf_op jit(solution)/shard_map/ppermute | solution.py:630
  397.4 34.6 %collective-permute-start.39 = (bf16[2,256,1024]{2,1,0:T(8,128)(2,1)}, bf16[2,256,1024]{2,1,0:T(8,128)(2,1)}, u32[]{:S(2)}, u32[]{:S(2)}) collective-permute-start(bf16[2,256,1024]{2,1,0:T(8,128)(2,1)} %get-tuple-element.461), channel_id=1, source_target_pairs={{0,8},{4,12},{8,0},{12,4},{16,24},{20,28},{24,16},{28,20},{1,9},{5... | collective-permute-start | bytes 3145736 | tf_op jit(solution)/shard_map/ppermute | solution.py:524
  400.3 31.8 %collective-permute-start.40 = (bf16[2,256,1024]{2,1,0:T(8,128)(2,1)}, bf16[2,256,1024]{2,1,0:T(8,128)(2,1)}, u32[]{:S(2)}, u32[]{:S(2)}) collective-permute-start(bf16[2,256,1024]{2,1,0:T(8,128)(2,1)} %get-tuple-element.459), channel_id=1, source_target_pairs={{0,16},{4,20},{8,24},{12,28},{16,0},{20,4},{24,8},{28,12},{1,17},{... | collective-permute-start | bytes 3145736 | tf_op jit(solution)/shard_map/ppermute | solution.py:524
  434.8 30.9 %collective-permute-start.44 = (bf16[256,1024]{1,0:T(8,128)(2,1)}, bf16[256,1024]{1,0:T(8,128)(2,1)}, u32[]{:S(2)}, u32[]{:S(2)}) collective-permute-start(bf16[256,1024]{1,0:T(8,128)(2,1)} %get-tuple-element.470), channel_id=1, source_target_pairs={{0,8},{4,12},{8,0},{12,4},{16,24},{20,28},{24,16},{28,20},{1,9},{5... | collective-permute-start | bytes 1572872 | tf_op jit(solution)/shard_map/ppermute | solution.py:524
  465.8 35.9 %collective-permute-start.47 = (bf16[4,256,1536]{2,1,0:T(8,128)(2,1)}, bf16[4,256,1536]{2,1,0:T(8,128)(2,1)}, u32[]{:S(2)}, u32[]{:S(2)}) collective-permute-start(bf16[4,256,1536]{2,1,0:T(8,128)(2,1)} %get-tuple-element.352), channel_id=1, source_target_pairs={{0,4},{4,0},{8,12},{12,8},{16,20},{20,16},{24,28},{28,24},{1,5},{5... | collective-permute-start | bytes 9437192 | tf_op jit(solution)/shard_map/ppermute | solution.py:524
  520.3 36.3 %collective-permute-start.49 = (bf16[256,2048]{1,0:T(8,128)(2,1)}, bf16[256,2048]{1,0:T(8,128)(2,1)S(1)}, u32[]{:S(2)}, u32[]{:S(2)}) collective-permute-start(bf16[256,2048]{1,0:T(8,128)(2,1)} %get-tuple-element.446), channel_id=1, source_target_pairs={{0,1},{1,2},{2,3},{4,5},{5,6},{6,7},{8,9},{9,10},{10,11},{12,13},{... | collective-permute-start | bytes 3145736 | tf_op jit(solution)/shard_map/ppermute | solution.py:630
  522.0 36.2 %collective-permute-start.50 = (bf16[256,2048]{1,0:T(8,128)(2,1)}, bf16[256,2048]{1,0:T(8,128)(2,1)S(1)}, u32[]{:S(2)}, u32[]{:S(2)}) collective-permute-start(bf16[256,2048]{1,0:T(8,128)(2,1)} %get-tuple-element.445), channel_id=1, source_target_pairs={{1,0},{2,1},{3,2},{5,4},{6,5},{7,6},{9,8},{10,9},{11,10},{13,12},{... | collective-permute-start | bytes 3145736 | tf_op jit(solution)/shard_map/ppermute | solution.py:631
  528.7 28.0 %collective-permute-start.51 = (bf16[2,256,768]{2,1,0:T(8,128)(2,1)}, bf16[2,256,768]{2,1,0:T(8,128)(2,1)}, u32[]{:S(2)}, u32[]{:S(2)}) collective-permute-start(bf16[2,256,768]{2,1,0:T(8,128)(2,1)} %get-tuple-element.465), channel_id=1, source_target_pairs={{0,8},{4,12},{8,0},{12,4},{16,24},{20,28},{24,16},{28,20},{1,9},{5... | collective-permute-start | bytes 2359304 | tf_op jit(solution)/shard_map/ppermute | solution.py:524
  (111 other events, 1314.6 us)
Sparse Core Ops, SparseCore 0:
  354.3 110.5 reduce-scatter.3

commit v2 on v1

v2 whole, which is shorter than its diff:
```python
import functools

import jax
import jax.numpy as jnp
from jax import lax
from jax.experimental import pallas as pl
from jax.experimental.pallas import tpu as pltpu
from jax.sharding import PartitionSpec as P

HEAD_DIM = 128
LONGEST = 512
EPSILON = 1e-05
MASKED_SCORE = -1e30
SCALING = HEAD_DIM ** (-0.5)
F32 = jnp.float32
BF16 = jnp.bfloat16
PARTS = 2
COST = 0
VMEM = 60 * 2**20


def mm(left_side, right_side):
    return lax.dot_general(
        left_side, right_side, (((1,), (0,)), ((), ())), preferred_element_type=F32
    )


def times_trans(left_side, right_side):
    return lax.dot_general(
        left_side, right_side, (((1,), (1,)), ((), ())), preferred_element_type=F32
    )


def trans_times(left_side, right_side):
    return lax.dot_general(
        left_side, right_side, (((0,), (0,)), ((), ())), preferred_element_type=F32
    )


def column_sums(values):
    return jnp.sum(values.astype(F32), axis=0)


def row_stats(rows):
    average = jnp.mean(rows, axis=-1, keepdims=True)
    centred = rows - average
    spread = jnp.mean(centred * centred, axis=-1, keepdims=True)
    return average, lax.rsqrt(spread + EPSILON)


def norm_back(d_normed, gain, xhat, inverse):
    scaled = d_normed * gain
    first = jnp.mean(scaled, axis=-1, keepdims=True)
    second = jnp.mean(scaled * xhat, axis=-1, keepdims=True)
    return inverse * (scaled - first - xhat * second)


def cost(flops):
    return pl.CostEstimate(flops=COST and flops, bytes_accessed=2**10, transcendentals=0)


def key_start(block, size):
    return max(0, (block * size - (LONGEST - 1)) // size * size)


def probabilities(seg_row, seg_col, query, keys, block, size):
    low, high = key_start(block, size), (block + 1) * size
    scores = times_trans(keys[low:high, :], query)
    shape = (high - low, size)
    key_place = lax.broadcasted_iota(jnp.int32, shape, 0) + low
    query_place = lax.broadcasted_iota(jnp.int32, shape, 1) + block * size
    same = seg_col[low:high, :] == seg_row[:, block * size : high]
    scores = jnp.where(same & (key_place <= query_place), scores, MASKED_SCORE)
    weights = jnp.exp(scores - jnp.max(scores, axis=0, keepdims=True))
    return weights * (1.0 / jnp.sum(weights, axis=0, keepdims=True))


def forward_kernel(size, seg_row, seg_col, query, key, value, *outs):
    part = outs[0].shape[1]
    for block in range(query.shape[0] // size):
        low, high = key_start(block, size), (block + 1) * size
        rows = slice(block * size, high)
        probs = probabilities(seg_row, seg_col, query[rows, :], key, block, size)
        attended = trans_times(probs.astype(BF16), value[low:high, :]).astype(BF16)
        for piece in range(size // part):
            share, c = divmod(block * (size // part) + piece, PARTS)
            outs[c][share] = attended[piece * part : (piece + 1) * part, :]


def backward_kernel(size, seg_row, seg_col, query, key, value, got, *refs):
    d_query, d_key, d_value, d_attended, key_sum, value_sum = refs
    groups, parts, part = got.shape[:3]
    for t in range(groups):
        for c in range(parts):
            start = (t * parts + c) * part
            d_attended[start : start + part, :] = got[t, c]
    key_sum[...] = jnp.zeros_like(key_sum)
    value_sum[...] = jnp.zeros_like(value_sum)
    for block in range(query.shape[0] // size):
        low, high = key_start(block, size), (block + 1) * size
        rows = slice(block * size, high)
        probs = probabilities(seg_row, seg_col, query[rows, :], key, block, size)
        value_sum[low:high, :] += mm(probs.astype(BF16), d_attended[rows, :])
        d_probs = times_trans(value[low:high, :], d_attended[rows, :])
        inner = jnp.sum(probs * d_probs, axis=0, keepdims=True)
        d_scores = (probs * (d_probs - inner)).astype(BF16)
        d_query[rows, :] = (trans_times(d_scores, key[low:high, :]) * SCALING).astype(BF16)
        key_sum[low:high, :] += mm(d_scores, query[rows, :])
    d_key[...] = key_sum[...].astype(BF16)
    d_value[...] = value_sum[...].astype(BF16)


def segment_views(segments):
    seqs, length = segments.shape
    return segments.reshape(seqs, 1, length), segments.reshape(seqs, length, 1)


def attend(segments, query, key, value, groups):
    length, local = query.shape
    part = length // groups // PARTS
    tall = pl.BlockSpec((length, HEAD_DIM), lambda h: (0, h))
    out = jax.ShapeDtypeStruct((groups, part, local), BF16)
    return pl.pallas_call(
        functools.partial(forward_kernel, min(256, length)),
        grid=(local // HEAD_DIM,),
        in_specs=[
            pl.BlockSpec((None, 1, length), lambda h: (0, 0, 0)),
            pl.BlockSpec((None, length, 1), lambda h: (0, 0, 0)),
        ]
        + [tall] * 3,
        out_specs=[pl.BlockSpec((groups, part, HEAD_DIM), lambda h: (0, 0, h))] * PARTS,
        out_shape=[out] * PARTS,
        compiler_params=pltpu.CompilerParams(vmem_limit_bytes=VMEM),
        cost_estimate=cost(4 * length * length * local),
    )(*segment_views(segments), query, key, value)


def attend_back(segments, query, key, value, got):
    length = query.shape[0]
    tall = pl.BlockSpec((length, HEAD_DIM), lambda h: (0, h))
    return pl.pallas_call(
        functools.partial(backward_kernel, min(256, length)),
        grid=(query.shape[1] // HEAD_DIM,),
        in_specs=[
            pl.BlockSpec((None, 1, length), lambda h: (0, 0, 0)),
            pl.BlockSpec((None, length, 1), lambda h: (0, 0, 0)),
        ]
        + [tall] * 3
        + [pl.BlockSpec(got.shape[:3] + (HEAD_DIM,), lambda h: (0, 0, 0, h))],
        out_specs=[tall] * 3,
        scratch_shapes=[
            pltpu.VMEM((length, HEAD_DIM), BF16),
            pltpu.VMEM((length, HEAD_DIM), F32),
            pltpu.VMEM((length, HEAD_DIM), F32),
        ],
        out_shape=[jax.ShapeDtypeStruct(query.shape, BF16)] * 3,
        compiler_params=pltpu.CompilerParams(vmem_limit_bytes=VMEM),
        cost_estimate=cost(10 * query.shape[0] * length * query.shape[1]),
    )(*segment_views(segments), query, key, value, got)


def place_bits(blocks):
    return blocks.bit_length() - 1


def xor_source(place, me, bits):
    distance = 0
    for bit in range(bits):
        distance = distance + (((place >> (bits - 1 - bit)) & 1) << bit)
    return distance ^ me


def norm_rows(values, gain, bias):
    average = jnp.mean(values, axis=-1, keepdims=True)
    centred = values - average
    inverse = lax.rsqrt(jnp.mean(centred * centred, axis=-1, keepdims=True) + EPSILON)
    return centred * inverse * gain + bias


def project_kernel(x, gain, bias, wq, bq, wk, wv, bv, normed, query, key, value):
    low = norm_rows(x[...].astype(F32), gain[...], bias[...]).astype(BF16)
    normed[...] = low
    query[...] = ((mm(low, wq[...]) + bq[...]) * SCALING).astype(BF16)
    key[...] = mm(low, wk[...]).astype(BF16)
    value[...] = (mm(low, wv[...]) + bv[...]).astype(BF16)


def whole_spec(array):
    return pl.BlockSpec(array.shape, lambda *_: (0,) * array.ndim)


def project(x, gain, bias, wq, bq, wk, wv, bv):
    rows, width = x.shape
    local = wq.shape[1]
    size = min(512, rows)
    args = [x] + [v.reshape(1, -1) if v.ndim == 1 else v for v in (gain, bias, wq, bq, wk, wv, bv)]
    tall = pl.BlockSpec((size, width), lambda i: (i, 0))
    thin = pl.BlockSpec((size, local), lambda i: (i, 0))
    shape = jax.ShapeDtypeStruct((rows, local), BF16)
    return pl.pallas_call(
        project_kernel,
        grid=(rows // size,),
        in_specs=[tall] + [whole_spec(a) for a in args[1:]],
        out_specs=[tall] + [thin] * 3,
        out_shape=[jax.ShapeDtypeStruct(x.shape, BF16)] + [shape] * 3,
        compiler_params=pltpu.CompilerParams(vmem_limit_bytes=VMEM),
        cost_estimate=cost(6 * rows * width * local),
    )(*args)


def middle_kernel(
    steps, here_ref, heads, wo, x, bo, gain, bias, wup, bup, d_hid, wup_rows,
    own_mid, low_out, hidden, d_up, *rest,
):
    first, second = steps
    *terms, mid, low, d_low = rest
    step = pl.program_id(0)
    block = wo.shape[1]
    here = here_ref[1]
    local = heads.shape[2]

    @pl.when(step == 0)
    def _():
        for t in range(heads.shape[0]):
            low[:, t * local : (t + 1) * local] = heads[t]

    @pl.when(step < first)
    def _():
        branch = mm(low[...], wo[...])
        values = x[...].reshape(branch.shape).astype(F32)
        columns = pl.ds(pl.multiple_of(step * block, block), block)
        mid[:, columns] = values + (branch + bo[...])

    @pl.when(step == first)
    def _():
        low[...] = norm_rows(mid[...], gain[...], bias[...]).astype(BF16)
        part = own_mid.shape[0]
        own_mid[...] = mid[pl.ds(pl.multiple_of(here * part, part), part), :]

    @pl.when((step >= first) & (step < first + second))
    def _():
        piece = 256
        for start in range(0, wup.shape[1], piece):
            columns = slice(start, start + piece)
            up_value = mm(low[...], wup[:, columns]) + bup[:, columns]
            below = 0.5 + 0.5 * lax.erf(up_value * (0.5**0.5))
            density = jnp.exp(-0.5 * up_value * up_value) * 0.3989422804014327
            hidden[:, columns] = (up_value * below).astype(BF16)
            slope = ((below + up_value * density) * d_hid[:, columns].astype(F32)).astype(BF16)
            d_up[:, columns] = slope
            place = pl.multiple_of((step - first) * wup.shape[1] + start, piece)
            d_low[:, pl.ds(place, piece)] = slope

    @pl.when(step >= first + second)
    def _():
        value = times_trans(d_low[...], wup_rows[...]).astype(BF16)

        for k, term in enumerate(terms):
            start = first + second + k * first // len(terms)

            @pl.when((step >= start) & (step < start + first // len(terms)))
            def _():
                term[...] = value

        columns = pl.ds(pl.multiple_of((step - first - second) * block, block), block)
        low_out[...] = low[:, columns]


def middle_call(split, c, here, heads, wo, x, bo, gain, bias, wup, bup, d_hid):
    groups, _, part, width = x.shape
    rows = groups * part
    hidden = wup.shape[1]
    block = 512
    first, second = width // block, hidden // block
    bo, gain, bias, bup = (v.reshape(1, -1) for v in (bo, gain, bias, bup))

    def at(index, low, count):
        return jnp.clip(index - low, 0, count - 1)

    def columns(tall, low, count):
        return pl.BlockSpec((tall, block), lambda i, h: (0, at(i, low, count)))

    third = first + second
    return pl.pallas_call(
        functools.partial(middle_kernel, (first, second)),
        grid_spec=pltpu.PrefetchScalarGridSpec(
            num_scalar_prefetch=1,
            grid=(first + second + first,),
            in_specs=[
                whole_spec(heads),
                columns(width, 0, first),
                pl.BlockSpec(
                    (groups, None, part, block), lambda i, h: (0, c, 0, at(i, 0, first))
                ),
                columns(1, 0, first),
                whole_spec(gain),
                whole_spec(bias),
                columns(width, first, second),
                columns(1, first, second),
                pl.BlockSpec((None, rows, block), lambda i, h: (c, 0, at(i, first, second))),
                pl.BlockSpec((block, hidden), lambda i, h: (at(i, third, first), 0)),
            ],
            out_specs=[
                pl.BlockSpec((part, width), lambda i, h: (0, 0)),
                columns(rows, third, first),
                columns(rows, first, second),
                columns(rows, first, second),
            ]
            + [columns(rows, third + k * first // split, first // split) for k in range(split)],
            scratch_shapes=[
                pltpu.VMEM((rows, width), F32),
                pltpu.VMEM((rows, width), BF16),
                pltpu.VMEM((rows, hidden), BF16),
            ],
        ),
        out_shape=[
            jax.ShapeDtypeStruct((part, width), F32),
            jax.ShapeDtypeStruct((rows, width), BF16),
            jax.ShapeDtypeStruct((rows, hidden), BF16),
            jax.ShapeDtypeStruct((rows, hidden), BF16),
        ]
        + [jax.ShapeDtypeStruct((rows, width // split), BF16)] * split,
        compiler_params=pltpu.CompilerParams(vmem_limit_bytes=VMEM),
        cost_estimate=cost(2 * rows * width * (width + 2 * hidden)),
    )(here, heads, wo, x, bo, gain, bias, wup, bup, d_hid, wup)


def middle_back_kernel(count, *refs):
    (terms, mid, cot, gain, wo), before = refs[:5], refs[5 : 5 + count]
    d_mid, d_branch, sums, d_att = refs[5 + count :]

    @pl.when(pl.program_id(0) == 0)
    def _():
        d_normed = terms[...].astype(F32)
        values = mid[...]
        centred = values - jnp.mean(values, axis=-1, keepdims=True)
        inverse = lax.rsqrt(jnp.mean(centred * centred, axis=-1, keepdims=True) + EPSILON)
        xhat = centred * inverse
        total = cot[...].astype(F32) + norm_back(d_normed, gain[...], xhat, inverse)
        low = total.astype(BF16)
        d_mid[...] = total
        d_branch[...] = low
        sums[0:1, :] = jnp.sum(d_normed * xhat, axis=0, keepdims=True)
        sums[1:2, :] = jnp.sum(d_normed, axis=0, keepdims=True)
        sums[2:3, :] = jnp.sum(low.astype(F32), axis=0, keepdims=True)

    for c in range(count):
        d_att[c] = before[c][...]
    d_att[count] = times_trans(d_branch[...], wo[...]).astype(BF16)


def middle_back(terms, mid, cot, gain, wo, before):
    part, width = mid.shape
    groups = lax.axis_size("tensor")
    block = width // groups
    count = len(before) + 1
    rows = pl.BlockSpec((part, width), lambda j: (0, 0))
    return pl.pallas_call(
        functools.partial(middle_back_kernel, len(before)),
        grid=(groups,),
        in_specs=[
            rows,
            rows,
            rows,
            pl.BlockSpec((1, width), lambda j: (0, 0)),
            pl.BlockSpec((block, width), lambda j: (j, 0)),
        ]
        + [pl.BlockSpec((None, None, part, block), lambda j: (j, 0, 0, 0))] * len(before),
        out_specs=[
            rows,
            rows,
            pl.BlockSpec((8, width), lambda j: (0, 0)),
            pl.BlockSpec((None, count, part, block), lambda j: (j, 0, 0, 0)),
        ],
        out_shape=[
            jax.ShapeDtypeStruct((part, width), F32),
            jax.ShapeDtypeStruct((part, width), BF16),
            jax.ShapeDtypeStruct((8, width), F32),
            jax.ShapeDtypeStruct((groups, count, part, block), BF16),
        ],
        compiler_params=pltpu.CompilerParams(vmem_limit_bytes=VMEM),
        cost_estimate=cost(2 * part * width * width),
    )(terms, mid, cot, gain.reshape(1, -1), wo, *before)


def gradient_terms(lefts, groups, me, blocks):
    half = blocks // 2
    bits = place_bits(blocks)
    part_of = [left[1] if isinstance(left, tuple) else None for left in lefts]
    lefts = [left[0] if isinstance(left, tuple) else left for left in lefts]
    count = len(lefts)
    rights = [right for group in groups for right in group]
    entry_of = [right[1] if isinstance(right, tuple) else None for right in rights]
    rights = [right[0] if isinstance(right, tuple) else right for right in rights]
    width = lefts[0].shape[-1] // blocks
    total = sum(right.shape[-1] for right in rights[::count])

    def source(j, m):
        return xor_source(jnp.where(j < half, j + half, j - half), m[0], bits)

    def right_spec(right, t):
        if t is None:
            return whole_spec(right)
        return pl.BlockSpec((None, None) + right.shape[2:], lambda j, m: (t, m[1], 0, 0))

    def left_spec(left, c):
        if c is None:
            return pl.BlockSpec((left.shape[0], width), lambda j, m: (0, source(j, m)))
        shape = (left.shape[0], None, left.shape[2], width)
        return pl.BlockSpec(shape, lambda j, m: (0, c, 0, source(j, m)))

    def kernel(me_ref, *refs):
        left_refs, right_refs = refs[:count], refs[count:]
        send, keep = refs[-2:]
        step = pl.program_id(0)

        def fill(target):
            place = 0
            turned = [ref[...].reshape(-1, width).T for ref in left_refs]
            for g in range(len(groups)):
                value = None
                for i in range(count):
                    more = mm(turned[i], right_refs[g * count + i][...])
                    value = more if value is None else value + more
                columns = value.shape[1]
                target[:, place : place + columns] = value.astype(BF16)
                place += columns

        @pl.when(step < half)
        def _():
            fill(send)

        @pl.when(step >= half)
        def _():
            fill(keep)

    shape = jax.ShapeDtypeStruct((half, width, total), BF16)
    return pl.pallas_call(
        kernel,
        grid_spec=pltpu.PrefetchScalarGridSpec(
            num_scalar_prefetch=1,
            grid=(blocks,),
            in_specs=[left_spec(left, c) for left, c in zip(lefts, part_of)]
            + [right_spec(right, t) for right, t in zip(rights, entry_of)],
            out_specs=[
                pl.BlockSpec((None, width, total), lambda j, m: (jnp.minimum(j, half - 1), 0, 0)),
                pl.BlockSpec((None, width, total), lambda j, m: (jnp.maximum(j - half, 0), 0, 0)),
            ],
        ),
        out_shape=[shape, shape],
        compiler_params=pltpu.CompilerParams(vmem_limit_bytes=VMEM),
        cost_estimate=cost(2**20),
    )(me, *lefts, *rights)


def normed_back_kernel(dq, dk, dv, wq, wk, wv, x, terms, gain_sum, bias_sum):
    total = times_trans(dq[...], wq[...]) + times_trans(dk[...], wk[...])
    total = total + times_trans(dv[...], wv[...])
    terms[...] = total.astype(BF16)
    values = x[...].astype(F32)
    centred = values - jnp.mean(values, axis=-1, keepdims=True)
    inverse = lax.rsqrt(jnp.mean(centred * centred, axis=-1, keepdims=True) + EPSILON)

    @pl.when(pl.program_id(0) == 0)
    def _():
        gain_sum[...] = jnp.zeros_like(gain_sum)
        bias_sum[...] = jnp.zeros_like(bias_sum)

    gain_sum[...] += jnp.sum(total * (centred * inverse), axis=0, keepdims=True)
    bias_sum[...] += jnp.sum(total, axis=0, keepdims=True)


def normed_back(dq, dk, dv, wq, wk, wv, x):
    rows, width = x.shape
    size = min(512, rows)
    thin = pl.BlockSpec((size, dq.shape[1]), lambda i: (i, 0))
    tall = pl.BlockSpec((size, width), lambda i: (i, 0))
    line = pl.BlockSpec((1, width), lambda i: (0, 0))
    return pl.pallas_call(
        normed_back_kernel,
        grid=(rows // size,),
        in_specs=[thin] * 3 + [whole_spec(w) for w in (wq, wk, wv)] + [tall],
        out_specs=[tall, line, line],
        out_shape=[
            jax.ShapeDtypeStruct((rows, width), BF16),
            jax.ShapeDtypeStruct((1, width), F32),
            jax.ShapeDtypeStruct((1, width), F32),
        ],
        compiler_params=pltpu.CompilerParams(vmem_limit_bytes=VMEM),
        cost_estimate=cost(6 * rows * width * dq.shape[1]),
    )(dq, dk, dv, wq, wk, wv, x)


def input_back(d_normed, x, d_mid, gain):
    rows, width = x.shape
    size = min(64, rows)

    def kernel(terms, x_ref, mid, gain_ref, out):
        values = x_ref[...].astype(F32)
        centred = values - jnp.mean(values, axis=-1, keepdims=True)
        inverse = lax.rsqrt(jnp.mean(centred * centred, axis=-1, keepdims=True) + EPSILON)
        back = norm_back(terms[...].astype(F32), gain_ref[...], centred * inverse, inverse)
        out[...] = mid[...] + back

    tall = pl.BlockSpec((size, width), lambda i: (i, 0))
    return pl.pallas_call(
        kernel,
        grid=(rows // size,),
        in_specs=[tall, tall, tall, pl.BlockSpec((1, width), lambda i: (0, 0))],
        out_specs=tall,
        out_shape=jax.ShapeDtypeStruct((rows, width), F32),
        compiler_params=pltpu.CompilerParams(vmem_limit_bytes=VMEM),
        cost_estimate=cost(2**20),
    )(d_normed, x, d_mid, gain.reshape(1, -1))


def both_parts(lefts, weight, transposed, columns, groups=None):
    block = min(512, columns)
    part_of = [left[1] if isinstance(left, tuple) else None for left in lefts]
    lefts = [left[0] if isinstance(left, tuple) else left for left in lefts]
    depth = lefts[0].shape[-1]
    rows = lefts[0].shape[0] * (1 if part_of[0] is None else lefts[0].shape[2])

    def kernel(*refs):
        weight_ref, out = refs[-2:]
        for c in range(len(lefts)):
            left = refs[c][...].reshape(-1, depth)
            product = times_trans if transposed else mm
            value = product(left, weight_ref[...]).astype(BF16)
            if groups is None:
                out[c] = value
            else:
                out[:, c] = value.reshape(groups, rows // groups, block)

    def left_spec(left, c):
        if c is None:
            return whole_spec(left)
        return pl.BlockSpec((left.shape[0], None) + left.shape[2:], lambda j: (0, c, 0, 0))

    shape = (len(lefts), rows)
    if groups is not None:
        shape = (groups, len(lefts), rows // groups)
    if transposed:
        weight_spec = pl.BlockSpec((block, depth), lambda j: (j, 0))
    else:
        weight_spec = pl.BlockSpec((depth, block), lambda j: (0, j))
    return pl.pallas_call(
        kernel,
        grid=(columns // block,),
        in_specs=[left_spec(left, c) for left, c in zip(lefts, part_of)] + [weight_spec],
        out_specs=pl.BlockSpec(shape + (block,), lambda j: (0,) * len(shape) + (j,)),
        out_shape=jax.ShapeDtypeStruct(shape + (columns,), BF16),
        compiler_params=pltpu.CompilerParams(vmem_limit_bytes=VMEM),
        cost_estimate=cost(2 * len(lefts) * rows * depth * columns),
    )(*lefts, weight)


def swap_bit(values, axis, bit):
    size = lax.axis_size(axis)
    return lax.ppermute(values, axis, [(i, i ^ (1 << bit)) for i in range(size)])


def third(k, steps):
    return range((k - 1) * steps // 3 + 1, k * steps // 3 + 1)


def fence(things, arrays=()):
    lists = [thing.live for thing in things]
    flat = lax.optimization_barrier(tuple(v for values in lists for v in values) + tuple(arrays))
    place = 0
    for thing, values in zip(things, lists):
        thing.live = list(flat[place : place + len(values)])
        place += len(values)
    return flat[place:]


def exchange(values):
    return lax.all_to_all(values, "tensor", 0, 0)


def add_and_split(sources, outs, dims):
    places = 2**dims
    rows = sources[0][0].shape[1]
    size = min(64, rows)
    widths = [sum(stop - start for _, start, stop in picks) for picks, _ in outs]

    def kernel(*refs):
        target = 2 * len(sources)
        for picks, dim in outs:
            shift = dims - 1 - dim
            for half in range(2):
                chosen = [p for p in range(places) if (p >> shift) & 1 == half]
                at = 0
                for source, start, stop in picks:
                    keep, got = refs[2 * source : 2 * source + 2]
                    for q, p in enumerate(chosen):
                        value = keep[p, :, start:stop].astype(F32) + got[p, :, start:stop].astype(F32)
                        refs[target][q, :, at : at + stop - start] = value.astype(BF16)
                    at += stop - start
                target += 1

    def block(count, columns):
        return pl.BlockSpec((count, size, columns), lambda i: (0, i, 0))

    flat = [v for pair in sources for v in pair]
    return pl.pallas_call(
        kernel,
        grid=(rows // size,),
        in_specs=[block(places, v.shape[2]) for v in flat],
        out_specs=[block(places // 2, w) for w in widths for _ in range(2)],
        out_shape=[
            jax.ShapeDtypeStruct((places // 2, rows, w), BF16) for w in widths for _ in range(2)
        ],
        compiler_params=pltpu.CompilerParams(vmem_limit_bytes=VMEM),
        cost_estimate=cost(2**20),
    )(*flat)


class DpSum:
    def __init__(self, send, keep, cuts):
        self.live = [send, keep]
        self.cuts = cuts
        self.rest = place_bits(lax.axis_size("dp")) - 1
        self.width = keep.shape[-1] // cuts
        self.left = [list(range(1, self.rest + 1)) for _ in range(2)]

    def core(self):
        self.live = [self.live[1], swap_bit(self.live[0], "dp", 0)]

    def dim(self, odd):
        return len(self.left[odd]) - 1 if odd else 0

    def split(self):
        outs = [
            ([(0, c * self.width, (c + 1) * self.width)], self.dim(c % 2)) for c in range(self.cuts)
        ]
        self.live = list(add_and_split([tuple(self.live)], outs, self.rest))

    def first(self, *cuts):
        for c in cuts:
            values = self.live[2 * c + 1]
            self.live[2 * c + 1] = swap_bit(values, "dp", self.left[c % 2][self.dim(c % 2)])

    def add(self):
        bits = [left[self.dim(odd)] for odd, left in enumerate(self.left)]
        for odd in range(2):
            self.left[odd].remove(bits[odd])
        count = len(self.live) // 2
        sources = [(self.live[2 * k], self.live[2 * k + 1]) for k in range(count)]
        outs = [
            ([(k, 0, sources[k][0].shape[2]) for k in range(odd, count, 2)], self.dim(odd))
            for odd in range(2)
        ]
        self.live = list(add_and_split(sources, outs, len(self.left[0])))

    def send(self):
        for odd in range(2):
            bit = self.left[odd][self.dim(odd)]
            self.live[2 * odd + 1] = swap_bit(self.live[2 * odd + 1], "dp", bit)
        while len(self.left[0]) > 1:
            self.add()
            self.send()

    def total(self):
        sums = [
            self.live[2 * odd][0].astype(F32) + self.live[2 * odd + 1][0].astype(F32)
            for odd in range(2)
        ]
        size = self.width
        return [
            sums[c % 2][:, c // 2 * size : (c // 2 + 1) * size] for c in range(self.cuts)
        ]


class WeightGather:
    def __init__(self, own, me):
        self.blocks = lax.axis_size("dp")
        self.size = lax.axis_size("tensor")
        self.usual = (self.size, self.blocks) == (4, 8)
        self.me = me
        share = own.shape[1 if self.usual else 0] // self.blocks
        axis = 1 if self.usual else 0
        self.live = [lax.dynamic_slice_in_dim(own, me[0] * share, share, axis)]

    def advance(self, k):
        if not self.usual:
            if k == 0:
                self.live = [lax.all_gather(self.live[0], ("tensor", "dp"), axis=0, tiled=True)]
            return
        if k == 0:
            own = self.live[0]
            self.live += [
                lax.ppermute(own, "tensor", [(i, (i + m) % self.size) for i in range(self.size)])
                for m in range(1, self.size)
            ]
        elif k == 1:
            own, one, two, three = self.live
            even = lax.axis_index("tensor") % 2 == 0
            near = jnp.concatenate([jnp.where(even, own, one), jnp.where(even, three, own)])
            far = jnp.concatenate([jnp.where(even, two, three), jnp.where(even, one, two)])
            self.live = [near, swap_bit(near, "dp", 1), far, swap_bit(far, "dp", 2)]
            self.live += [swap_bit(near, "dp", 0), swap_bit(far, "dp", 0)]
        elif k == 2:
            near, near_one, far, far_one, near_core, far_core = self.live
            near, far = jnp.stack([near, near_one]), jnp.stack([far, far_one])
            self.live = [near, far, near_core[None], far_core[None]]
            self.live += [swap_bit(near, "dp", 2), swap_bit(far, "dp", 1)]
            self.live += [swap_bit(near_one, "dp", 0)[None], swap_bit(far_one, "dp", 0)[None]]
        elif k == 3:
            near, far, near_core, far_core, near_two, far_two, near_one_core, far_one_core = self.live
            own = [(near, 0), (near, 1), (far, 0), (far, 1)]
            other = [(v, 0) for v in (near_core, near_one_core, far_core, far_one_core)]
            self.live = [near_two, far_two, self.place(own, other, 0, None)]
        else:
            near_two, far_two, half = self.live
            self.live = [near_two, swap_bit(near_two, "dp", 0)]
            self.live += [far_two, swap_bit(far_two, "dp", 0), half]

    def place(self, own, other, late, half):
        rows, width = own[0][0].shape[1:]
        blocks = own + other

        def kernel(me_ref, *refs):
            out = refs[-1]
            step, odd = pl.program_id(0), me_ref[0] & 1
            for k in range(4):
                for flip in range(2):

                    @pl.when((step == k) & (odd == flip))
                    def _():
                        out[:, flip * width : (flip + 1) * width] = refs[k][...]
                        out[:, (1 - flip) * width : (2 - flip) * width] = refs[k + 4][...]

        def source(entry):
            return pl.BlockSpec((None, rows, width), lambda s, m: (entry, 0, 0))

        def target(s, m):
            top, one = s < 2, s & 1
            low = jnp.where(top, 2 * one + 4 * late, 4 * one + 2 * late)
            return (jnp.where(top, m[2], 1 - m[2]), (low ^ m[0]) >> 1)

        more = [] if half is None else [half]
        return pl.pallas_call(
            kernel,
            grid_spec=pltpu.PrefetchScalarGridSpec(
                num_scalar_prefetch=1,
                grid=(4,),
                in_specs=[source(entry) for _, entry in blocks]
                + [pl.BlockSpec(memory_space=pl.ANY)] * len(more),
                out_specs=pl.BlockSpec((rows, 2 * width), target),
            ),
            out_shape=jax.ShapeDtypeStruct((2 * rows, 8 * width), BF16),
            input_output_aliases={9: 0} if more else {},
            compiler_params=pltpu.CompilerParams(vmem_limit_bytes=VMEM),
            cost_estimate=cost(2**20),
        )(self.me, *[array for array, _ in blocks], *more)

    def whole(self):
        if not self.usual:
            return self.live[0]
        near, near_core, far, far_core, half = self.live
        own = [(near, 0), (near, 1), (far, 0), (far, 1)]
        other = [(near_core, 0), (near_core, 1), (far_core, 0), (far_core, 1)]
        return self.place(own, other, 1, half)


class SmallSum:
    def __init__(self, vectors, me):
        self.vectors = vectors
        self.blocks = blocks = lax.axis_size("dp")
        self.bits = place_bits(blocks)
        places = jnp.stack([xor_source(p, me, self.bits) for p in range(blocks)]).reshape(-1)
        self.ordered = sorted(range(len(vectors)), key=lambda i: not vectors[i][1])
        wide = [vectors[i][0].reshape(blocks, -1) for i in self.ordered]
        wide = jnp.take(jnp.concatenate(wide, axis=1), places, axis=0)
        self.live = [wide.reshape((2,) * self.bits + wide.shape[1:])]

    def move(self):
        self.steps = getattr(self, "steps", 0) + 1
        while self.live[0].ndim > 1:
            values = self.live[0]
            self.live = [values[0] + swap_bit(values[1], "dp", self.bits - values.ndim + 1)]
            if self.steps < 3:
                return

    def tensor(self):
        values = self.live[0]
        both = sum(v[0].shape[0] // self.blocks for v in self.vectors if v[1])
        summed, alone = values[..., :both], values[..., both:]
        for bit in range(place_bits(lax.axis_size("tensor"))):
            summed = summed + swap_bit(summed, "tensor", bit)
        self.live = [jnp.concatenate([summed, alone], axis=-1)]

    def total(self):
        out, start = [None] * len(self.vectors), 0
        for i in self.ordered:
            size = self.vectors[i][0].shape[0] // self.blocks
            out[i] = self.live[0][start : start + size]
            start += size
        return out


def on_device(
    inputs,
    segments,
    cotangent,
    norm1_gain,
    norm1_bias,
    query_weight,
    query_bias,
    key_weight,
    value_weight,
    value_bias,
    output_weight,
    output_bias,
    norm2_gain,
    norm2_bias,
    up_weight,
    up_bias,
    down_weight,
    down_bias,
):
    groups = lax.axis_size("tensor")
    blocks = lax.axis_size("dp")
    here = lax.axis_index("tensor").astype(jnp.int32)
    side = here // (groups // 2)
    me = lax.axis_index("dp").astype(jnp.int32)
    me = jnp.stack([me, here, side])
    rows, width = inputs.shape
    share = rows // groups
    part = share // PARTS
    local = query_weight.shape[1]
    size = width // blocks

    def by_part(values):
        return values.reshape(groups, PARTS, part, values.shape[1])

    def own(values):
        return lax.dynamic_slice_in_dim(values, here * share, share, 0)

    weight = WeightGather(output_weight, me)
    weight.advance(0)
    normed, query, key, value = project(
        inputs,
        norm1_gain,
        norm1_bias,
        query_weight,
        query_bias,
        key_weight,
        value_weight,
        value_bias,
    )
    heads = attend(segments, query, key, value, groups)
    heads = [h.reshape(groups * part, local) for h in heads]
    cot, *heads = fence([weight], (cotangent, *heads))

    heads[0] = lax.all_gather(heads[0], "tensor", axis=0)
    weight.advance(1)
    cot, heads[1] = fence([weight], (cot, heads[1]))
    heads[1] = lax.all_gather(heads[1], "tensor", axis=0)
    weight.advance(2)
    cot_parts = by_part(cot)
    cots = [(cot_parts, c) for c in range(PARTS)]
    d_hidden = both_parts(cots, down_weight, True, down_weight.shape[0])
    d_hidden, cot = fence([], (d_hidden, cot))
    weight.advance(3)
    d_hidden, cot = fence([weight], (d_hidden, cot))
    weight.advance(4)
    fence([weight])
    whole = weight.whole()
    whole, heads[0] = fence([], (whole, heads[0]))

    own_mid, low, hidden, d_up, terms = ([None] * PARTS for _ in range(5))

    def middle(c):
        own_mid[c], low[c], hidden[c], d_up[c], *term = middle_call(
            1,
            c,
            me,
            heads[c],
            whole,
            by_part(inputs),
            output_bias,
            norm2_gain,
            norm2_bias,
            up_weight,
            up_bias,
            d_hidden,
        )
        terms[c] = term[0].reshape(groups, part, width)

    middle(0)
    terms[0], heads[1] = fence([], (terms[0], heads[1]))

    terms[0] = lax.psum_scatter(terms[0], "tensor", scatter_dimension=0)
    middle(1)
    cot_own = own(cot)
    terms[1], cot_own, low[0], low[1], d_up[0], d_up[1] = fence(
        [], (terms[1], cot_own, *low, *d_up)
    )

    terms[1] = lax.psum_scatter(terms[1], "tensor", scatter_dimension=0)
    up_terms = gradient_terms(low, [d_up], me, blocks)
    d_mids, d_branches, sums = ([None] * PARTS for _ in range(3))

    def back(c, before):
        d_mids[c], d_branches[c], sums[c], d_att = middle_back(
            terms[c], own_mid[c], cot_own[c * part : (c + 1) * part], norm2_gain, whole, before
        )
        return d_att

    terms[0], hidden[0], hidden[1], *up_terms = fence([], (terms[0], *hidden, *up_terms))
    d_att = back(0, [])
    d_att, hidden[0], hidden[1] = fence([], (d_att, *hidden))
    out_terms = both_parts(hidden, down_weight, False, width, groups)
    out_terms, hidden[0], hidden[1] = fence([], (out_terms, *hidden))
    down_terms = gradient_terms(cots, [hidden], me, blocks)
    cot_sum = column_sums(cot)
    up_bias_sum = column_sums(d_up[0]) + column_sums(d_up[1])
    up_sum = DpSum(*up_terms, 2)
    down_sum = DpSum(*down_terms, 2)
    terms[1], out_terms, d_branches[0], cot_sum, up_bias_sum, d_att = fence(
        [up_sum, down_sum], (terms[1], out_terms, d_branches[0], cot_sum, up_bias_sum, d_att)
    )

    d_att = back(1, [d_att])
    d_att, *d_branches = fence([up_sum, down_sum], (d_att, *d_branches))
    d_att = exchange(d_att)
    up_sum.core()
    down_sum.core()
    views = [h.reshape(groups, groups, part, local) for h in heads]
    wo_terms = gradient_terms(d_branches, [[(v, t) for v in views] for t in range(groups)], me, blocks)
    wo_sum = DpSum(*wo_terms, 2)
    up_sum.split()
    d_att, out_terms = fence([wo_sum, up_sum, down_sum], (d_att, out_terms))

    out_sum = lax.psum_scatter(out_terms, "tensor", scatter_dimension=0)
    up_sum.first(0, 1)
    wo_sum.core()
    d_query, d_key, d_value = attend_back(segments, query, key, value, d_att)
    wo_sum.split()
    d_query, d_key, d_value = fence([up_sum, wo_sum, down_sum], (d_query, d_key, d_value))
    wo_sum.first(0, 1)
    qkv_sum = DpSum(
        *gradient_terms([normed], [[d] for d in (d_query, d_key, d_value)], me, blocks), 2
    )
    down_sum.split()
    d_query, d_key, d_value = fence([wo_sum, qkv_sum, down_sum], (d_query, d_key, d_value))
    qkv_sum.core()
    down_sum.first(0, 1)
    terms_in, gain1, bias1 = normed_back(
        d_query, d_key, d_value, query_weight, key_weight, value_weight, inputs
    )
    gain1, bias1, terms_in, d_query, d_value = fence(
        [qkv_sum, wo_sum], (gain1, bias1, terms_in, d_query, d_value)
    )

    d_normed = lax.psum_scatter(
        terms_in.reshape(groups, share, width), "tensor", scatter_dimension=0
    )
    qkv_sum.split()
    wo_sum.add()
    gain1, bias1, d_query, d_value = fence(
        [qkv_sum, wo_sum, down_sum], (gain1, bias1, d_query, d_value)
    )
    qkv_sum.first(0, 1)
    wo_sum.send()
    two = sums[0] + sums[1]
    small = SmallSum(
        [
            (gain1[0], True),
            (bias1[0], True),
            (two[0], True),
            (two[1], True),
            (two[2], True),
            (cot_sum, False),
            (column_sums(d_query), False),
            (column_sums(d_value), False),
            (up_bias_sum, False),
        ],
        me[:1],
    )
    down_sum.add()
    out_sum, *_ = fence([qkv_sum, wo_sum, down_sum, small, up_sum], (out_sum,))
    qkv_sum.add()
    qkv_sum.send()
    down_sum.send()
    small.tensor()
    wo_terms = jnp.concatenate(wo_sum.total(), axis=1).T
    wo_terms = wo_terms.astype(BF16).reshape(groups, local, size)
    to_all = [
        lax.dynamic_index_in_dim(wo_terms, (here - m) % groups, 0, keepdims=False)
        for m in range(groups)
    ]
    up_sum.add()
    out_sum, *to_all = fence([qkv_sum, small, down_sum, up_sum], (out_sum, *to_all))
    output_weight_grad = to_all[0].astype(F32)
    for m in range(1, groups):
        ring = [(i, (i - m) % groups) for i in range(groups)]
        output_weight_grad = output_weight_grad + lax.ppermute(to_all[m], "tensor", ring).astype(F32)
    up_sum.send()
    small.move()
    small.move()
    small.move()
    total = [own_mid[c] + (out_sum[c].astype(F32) + down_bias) for c in range(PARTS)]
    output = jnp.concatenate([t.astype(BF16) for t in total], axis=0)
    qkv_grad = jnp.concatenate(qkv_sum.total(), axis=1)
    up_weight_grad = jnp.concatenate(up_sum.total(), axis=1)
    down_weight_grad = jnp.concatenate(down_sum.total(), axis=1).T
    up_weight_grad, down_weight_grad, qkv_grad, output_weight_grad = fence(
        [small], (up_weight_grad, down_weight_grad, qkv_grad, output_weight_grad)
    )
    (d_normed,) = fence([small], (d_normed,))
    input_grad = input_back(d_normed, own(inputs), jnp.concatenate(d_mids, axis=0), norm1_gain)
    (
        norm1_gain_grad,
        norm1_bias_grad,
        norm2_gain_grad,
        norm2_bias_grad,
        output_bias_grad,
        down_bias_grad,
        query_bias_grad,
        value_bias_grad,
        up_bias_grad,
    ) = small.total()
    return (
        output,
        input_grad,
        norm1_gain_grad,
        norm1_bias_grad,
        qkv_grad[:, :local],
        query_bias_grad,
        qkv_grad[:, local : 2 * local],
        qkv_grad[:, 2 * local :],
        value_bias_grad,
        output_weight_grad,
        output_bias_grad,
        norm2_gain_grad,
        norm2_bias_grad,
        up_weight_grad,
        up_bias_grad,
        down_weight_grad,
        down_bias_grad,
    )


def solution(mesh):
    return jax.shard_map(
        on_device,
        mesh=mesh,
        in_specs=(
            P("dp", None),
            P("dp", None),
            P("dp", None),
            P(),
            P(),
            P(None, "tensor"),
            P("tensor"),
            P(None, "tensor"),
            P(None, "tensor"),
            P("tensor"),
            P("tensor", None),
            P(),
            P(),
            P(),
            P(None, "tensor"),
            P("tensor"),
            P("tensor", None),
            P(),
        ),
        out_specs=(
            P(("dp", "tensor"), None),
            P(("dp", "tensor"), None),
            P("dp"),
            P("dp"),
            P("dp", "tensor"),
            P(("tensor", "dp")),
            P("dp", "tensor"),
            P("dp", "tensor"),
            P(("tensor", "dp")),
            P("tensor", "dp"),
            P("dp"),
            P("dp"),
            P("dp"),
            P("dp", "tensor"),
            P(("tensor", "dp")),
            P("tensor", "dp"),
            P("dp"),
        ),
        check_vma=False,
    )
```

time: 602 us -> 469 us (0.78)
  starting transfers between devices: 117 us -> 41.1 us
  other arithmetic: 78.4 us -> 22.6 us
  Pallas kernels: 213 us -> 265 us
  waiting for transfers between devices: 119 us -> 90.8 us
  local copies, waits for them, and re-layouts: 52.7 us -> 26.3 us
    ppermute x29 -> x3, starting transfers between devices: 84 us -> 3.08 us  [on_device(): lax.ppermute(to_all[m], 'tensor', ring).astype(F32)]
    ppermute x29 -> x3, waiting for transfers between devices: 79.2 us -> 15.3 us  [on_device(): lax.ppermute(to_all[m], 'tensor', ring).astype(F32)]
    convert_element_type x17 -> x1, other arithmetic: 46.5 us -> 0.34 us  [on_device(): output = jnp.concatenate([t.astype(BF16) for t in total], axis=0)]
    pallas_call x3 -> x12, Pallas kernels: 34 us -> 79.3 us  [the longest x8 40 us: add_and_split(): pl.pallas_call(kernel, grid=(rows // size,), in_specs=[block(places, v.sh...]
    ppermute x30 -> x35, waiting for transfers between devices: 39.4 us -> 54.2 us  [swap_bit(): return lax.ppermute(values, axis, [(i, i ^ 1 << bit) for i in range(size)])]
    squeeze x10 -> x0, local copies, waits for them, and re-layouts: 12.3 us -> none  [the longest x6 5.52 us: move(): send = lax.index_in_dim(values, 1, dim, keepdims=False)]
    all_to_all x0 -> x1, waiting for transfers between devices: none -> 9.48 us  [exchange(): return lax.all_to_all(values, 'tensor', 0, 0)]
    all_gather x0 -> x2, waiting for transfers between devices: none -> 8.77 us  [the longest x1 8.77 us: on_device(): heads[1] = lax.all_gather(heads[1], 'tensor', axis=0)]
  transfers between devices with their start and end apart: 63 -> 48, of which waited for: 16 -> 17; matrix products, arithmetic and copies ran while one was open for 17% -> 9% of each run, Pallas kernels for 34% -> 55%
where the time goes in v2:
time: 469 us; the launch traced here: 461 us
  Pallas kernels  265 us (57%)
  waiting for transfers between devices  90.8 us (19%)
  starting transfers between devices  41.1 us (9%)
  local copies, waits for them, and re-layouts  26.3 us (6%)
  other arithmetic  22.6 us (5%)
  between operations  15.2 us (3%)
    pallas_call x2, Pallas kernels, middle_call(): pl.pallas_call(functools.partial(middle_kernel, (first, second)), grid_sp...  55.3 us
    pallas_call x4, Pallas kernels, gradient_terms(): pl.pallas_call(kernel, grid_spec=pltpu.PrefetchScalarGridSpec(num_scalar_...  54.5 us
    ppermute x35, waiting for transfers between devices, swap_bit(): return lax.ppermute(values, axis, [(i, i ^ 1 << bit) for i in range(size)])  54.2 us
    pallas_call x8, Pallas kernels, add_and_split(): pl.pallas_call(kernel, grid=(rows // size,), in_specs=[block(places, v.sh...  40 us
    ppermute x35, starting transfers between devices, swap_bit(): return lax.ppermute(values, axis, [(i, i ^ 1 << bit) for i in range(size)])  27.4 us
    pallas_call x2, Pallas kernels, both_parts(): pl.pallas_call(kernel, grid=(columns // block,), in_specs=[left_spec(left...  26.9 us
    pallas_call x1, Pallas kernels, attend_back(): pl.pallas_call(functools.partial(backward_kernel, min(256, length)), grid...  17.7 us
    pallas_call x2, Pallas kernels, middle_back(): pl.pallas_call(functools.partial(middle_back_kernel, len(before)), grid=(...  16.7 us
  transfers between devices with their start and end apart: 48, of which 17 were waited for; matrix products, arithmetic and copies ran while one was open for 9% of the time, Pallas kernels for 55%

profile of v2, /device:TPU:0, one launch (start us, length us, event | category | flops | bytes accessed | tf_op | source)
XLA Modules:
  0.0 460.8 jit_solution(13311173194990204618)
XLA Ops:
  16.6 13.4 %shard_map.305 = (bf16[1024,2048]{1,0:T(8,128)(2,1)}, bf16[1024,512]{1,0:T(8,128)(2,1)}, bf16[1024,512]{1,0:T(8,128)(2,1)}, bf16[1024,512]{1,0:T(8,128)(2,1)}) custom-call(bf16[1024,2048]{1,0:T(8,128)(2,1)} %x.3, f32[1,2048]{1,0:T(1,128)} %bitcast.128, f32[1,2048]{1,0:T(1,128)} %bitcast.136, bf16[2048,512]{1,0:T(8,128)(2,1)} %wq.3, f32[1,512]{1,0:T(1,128)} %bitcast.137, ...), custom_call_target="tpu_custom_call" | custom-call | bytes 1024 | tf_op jit(solution)/shard_map/pallas_call | solution.py:200
  30.0 8.8 %shard_map.306 = (bf16[4,128,512]{2,1,0:T(8,128)(2,1)}, bf16[4,128,512]{2,1,0:T(8,128)(2,1)}) custom-call(s32[1,1,1024]{2,1,0:T(1,128)} %bitcast.126, s32[1,1024,1]{2,1,0:T(8,128)} %copy.41.seg_col, bf16[1024,512]{1,0:T(8,128)(2,1)} %get-tuple-element.258.query, bf16[1024,512]{1,0:T(8,128)(2,1)} %get-tuple-element.259.key, ...), custom_call_target="tpu_custom_call" | custom-call | bytes 1024 | tf_op jit(solution)/shard_map/pallas_call | solution.py:123
  42.5 11.1 %collective-permute-done.3 = bf16[1024,256]{1,0:T(8,128)(2,1)} collective-permute-done((bf16[1024,256]{1,0:T(8,128)(2,1)S(1)}, bf16[1024,256]{1,0:T(8,128)(2,1)}, u32[]{:S(2)}, u32[]{:S(2)}) %collective-permute-start.3) | collective-permute-done | bytes 524320 | tf_op jit(solution)/shard_map/ppermute | solution.py:560
  61.4 13.5 %shard_map.308.d_hid = bf16[2,512,2048]{2,1,0:T(8,128)(2,1)} custom-call(bf16[4,2,128,2048]{3,2,1,0:T(8,128)(2,1)} %bitcast.88, bf16[4,2,128,2048]{3,2,1,0:T(8,128)(2,1)} %bitcast.89, bf16[2048,2048]{1,0:T(8,128)(2,1)} %refs_2_.3), custom_call_target="tpu_custom_call" | custom-call | bytes 1024 | tf_op jit(solution)/shard_map/pallas_call | solution.py:547
  74.9 5.5 %shard_map.307.refs_8_ = bf16[2048,2048]{1,0:T(8,128)(2,1)} custom-call(s32[3]{0:T(128)} %pad_add_fusion.me_ref.here_ref, bf16[2,1024,256]{2,1,0:T(8,128)(2,1)} %copy-done.2, bf16[2,1024,256]{2,1,0:T(8,128)(2,1)} %copy-done.2, bf16[2,1024,256]{2,1,0:T(8,128)(2,1)} %copy-done.3, bf16[2,1024,256]{2,1,0:T(8,128)(2,1)} %copy-done.3, ...), custom_call_target="tpu_custom_call" | custom-call | bytes 1024 | tf_op jit(solution)/shard_map/pallas_call | solution.py:743
  90.3 5.6 %shard_map.309.wo.refs_4_ = bf16[2048,2048]{1,0:T(8,128)(2,1)} custom-call(s32[3]{0:T(128)} %pad_add_fusion.me_ref.here_ref, bf16[2,1024,256]{2,1,0:T(8,128)(2,1)} %copy-done.8, bf16[2,1024,256]{2,1,0:T(8,128)(2,1)} %copy-done.8, bf16[2,1024,256]{2,1,0:T(8,128)(2,1)} %collective-permute-done.8.refs_2_.refs_3_, ...), custom_call_target="tpu_custom_call", output_to_operand_aliasing={{}: (9, {})} | custom-call | bytes 1024 | tf_op jit(solution)/shard_map/pallas_call | solution.py:743
  95.9 27.6 %shard_map.310 = (f32[128,2048]{1,0:T(8,128)}, bf16[512,2048]{1,0:T(8,128)(2,1)}, bf16[512,2048]{1,0:T(8,128)(2,1)}, bf16[512,2048]{1,0:T(8,128)(2,1)}, bf16[512,2048]{1,0:T(8,128)(2,1)}) custom-call(s32[3]{0:T(128)} %pad_add_fusion.me_ref.here_ref, bf16[4,512,512]{2,1,0:T(8,128)(2,1)} %bitcast.94, bf16[2048,2048]{1,0:T(8,128)(2,1)} %shard_map.309.wo.refs_4_, ...), custom_call_target="tpu_custom_call" | custom-call | bytes 1024 | tf_op jit(solution)/shard_map/pallas_call | solution.py:284
  123.5 8.8 %all-gather.7.cloned.1.call-done = bf16[2048,512]{1,0:T(8,128)(2,1)} async-done(((bf16[512,512]{1,0:T(8,128)(2,1)}), bf16[2048,512]{1,0:T(8,128)(2,1)}) %all-gather.7.cloned.1.call-update) | async-done | bytes 2097168 | tf_op jit(solution)/shard_map/all_gather | solution.py:860
  134.2 27.7 %shard_map.311 = (f32[128,2048]{1,0:T(8,128)}, bf16[512,2048]{1,0:T(8,128)(2,1)}, bf16[512,2048]{1,0:T(8,128)(2,1)}, bf16[512,2048]{1,0:T(8,128)(2,1)}, bf16[512,2048]{1,0:T(8,128)(2,1)}) custom-call(s32[3]{0:T(128)} %pad_add_fusion.me_ref.here_ref, bf16[4,512,512]{2,1,0:T(8,128)(2,1)} %bitcast.99, bf16[2048,2048]{1,0:T(8,128)(2,1)} %shard_map.309.wo.refs_4_, ...), custom_call_target="tpu_custom_call" | custom-call | bytes 1024 | tf_op jit(solution)/shard_map/pallas_call | solution.py:284
  166.3 15.3 %shard_map.312 = (bf16[4,256,2048]{2,1,0:T(8,128)(2,1)}, bf16[4,256,2048]{2,1,0:T(8,128)(2,1)}) custom-call(s32[3]{0:T(128)} %pad_add_fusion.me_ref.here_ref, bf16[512,2048]{1,0:T(8,128)(2,1)} %get-tuple-element.303.refs_0_, bf16[512,2048]{1,0:T(8,128)(2,1)} %get-tuple-element.304.refs_1_, bf16[512,2048]{1,0:T(8,128)(2,1)} %get-tuple-element.305.refs_2_, ...), custom_call_target="tpu_custom_call" | custom-call | bytes 1024 | tf_op jit(solution)/shard_map/pallas_call | solution.py:438
  182.6 8.4 %shard_map.313 = (f32[128,2048]{1,0:T(8,128)}, bf16[128,2048]{1,0:T(8,128)(2,1)}, f32[8,2048]{1,0:T(8,128)}, bf16[4,1,128,512]{3,2,1,0:T(8,128)(2,1)}) custom-call(bf16[128,2048]{1,0:T(8,128)(2,1)} %bitcast.114, f32[128,2048]{1,0:T(8,128)} %get-tuple-element.290.refs_1_, bf16[128,2048]{1,0:T(8,128)(2,1)} %get-tuple-element.548.refs_2_, f32[1,2048]{1,0:T(1,128)} %bitcast.123, ...), custom_call_target="tpu_custom_call" | custom-call | bytes 1024 | tf_op jit(solution)/shard_map/pallas_call | solution.py:358
  191.0 13.4 %shard_map.314 = bf16[4,2,128,2048]{3,2,1,0:T(8,128)(2,1)} custom-call(bf16[512,2048]{1,0:T(8,128)(2,1)} %get-tuple-element.318.refs_0_.refs_2_, bf16[512,2048]{1,0:T(8,128)(2,1)} %get-tuple-element.319.refs_1_.refs_3_, bf16[2048,2048]{1,0:T(8,128)(2,1)} %refs_2_.3), custom_call_target="tpu_custom_call" | custom-call | bytes 1024 | tf_op jit(solution)/shard_map/pallas_call | solution.py:547
  204.4 15.4 %shard_map.315 = (bf16[4,256,2048]{2,1,0:T(8,128)(2,1)}, bf16[4,256,2048]{2,1,0:T(8,128)(2,1)}) custom-call(s32[3]{0:T(128)} %pad_add_fusion.me_ref.here_ref, bf16[4,2,128,2048]{3,2,1,0:T(8,128)(2,1)} %bitcast.90, bf16[4,2,128,2048]{3,2,1,0:T(8,128)(2,1)} %bitcast.91, bf16[512,2048]{1,0:T(8,128)(2,1)} %get-tuple-element.318.refs_0_.refs_2_, ...), custom_call_target="tpu_custom_call" | custom-call | bytes 1024 | tf_op jit(solution)/shard_map/pallas_call | solution.py:438
  222.7 8.3 %shard_map.316 = (f32[128,2048]{1,0:T(8,128)}, bf16[128,2048]{1,0:T(8,128)(2,1)}, f32[8,2048]{1,0:T(8,128)}, bf16[4,2,128,512]{3,2,1,0:T(8,128)(2,1)}) custom-call(bf16[128,2048]{1,0:T(8,128)(2,1)} %bitcast.115, f32[128,2048]{1,0:T(8,128)} %get-tuple-element.331.refs_1_, bf16[128,2048]{1,0:T(8,128)(2,1)} %get-tuple-element.547.refs_2_, f32[1,2048]{1,0:T(1,128)} %bitcast.124, ...), custom_call_target="tpu_custom_call" | custom-call | bytes 1024 | tf_op jit(solution)/shard_map/pallas_call | solution.py:358
  235.1 10.6 %shard_map.317 = (bf16[4,256,2048]{2,1,0:T(8,128)(2,1)}, bf16[4,256,2048]{2,1,0:T(8,128)(2,1)}) custom-call(s32[3]{0:T(128)} %pad_add_fusion.me_ref.here_ref, bf16[128,2048]{1,0:T(8,128)(2,1)} %get-tuple-element.336.refs_0_, bf16[128,2048]{1,0:T(8,128)(2,1)} %get-tuple-element.337.refs_1_, bf16[4,4,128,512]{3,2,1,0:T(8,128)(2,1)} %bitcast.95, ...), custom_call_target="tpu_custom_call" | custom-call | bytes 1024 | tf_op jit(solution)/shard_map/pallas_call | solution.py:438
  245.7 6.1 %shard_map.318 = (bf16[2,256,1024]{2,1,0:T(8,128)(2,1)}, bf16[2,256,1024]{2,1,0:T(8,128)(2,1)}, bf16[2,256,1024]{2,1,0:T(8,128)(2,1)}, bf16[2,256,1024]{2,1,0:T(8,128)(2,1)}) custom-call(bf16[4,256,2048]{2,1,0:T(8,128)(2,1)} %get-tuple-element.340.refs_0_, bf16[4,256,2048]{2,1,0:T(8,128)(2,1)} %collective-permute-done.13.refs_1_), custom_call_target="tpu_custom_call" | custom-call | bytes 1024 | tf_op jit(solution)/shard_map/pallas_call | solution.py:606
  251.8 9.5 %all-to-all-done.got = bf16[4,2,128,512]{3,2,1,0:T(8,128)(2,1)S(1)} async-done(((bf16[4,2,128,512]{3,2,1,0:T(8,128)(2,1)}), bf16[4,2,128,512]{3,2,1,0:T(8,128)(2,1)S(1)}, u32[]{:S(2)}, u32[]{:S(2)}) %all-to-all-start) | async-done | bytes 1048608 | tf_op jit(solution)/shard_map/all_to_all | solution.py:578
  264.8 17.7 %shard_map.320 = (bf16[1024,512]{1,0:T(8,128)(2,1)}, bf16[1024,512]{1,0:T(8,128)(2,1)}, bf16[1024,512]{1,0:T(8,128)(2,1)}) custom-call(s32[1,1,1024]{2,1,0:T(1,128)} %bitcast.127, s32[1,1024,1]{2,1,0:T(8,128)} %copy.41.seg_col, bf16[1024,512]{1,0:T(8,128)(2,1)} %get-tuple-element.258.query, bf16[1024,512]{1,0:T(8,128)(2,1)} %get-tuple-element.259.key, ...), custom_call_target="tpu_custom_call" | custom-call | bytes 1024 | tf_op jit(solution)/shard_map/pallas_call | solution.py:141
  282.5 6.1 %shard_map.319 = (bf16[2,256,1024]{2,1,0:T(8,128)(2,1)}, bf16[2,256,1024]{2,1,0:T(8,128)(2,1)}, bf16[2,256,1024]{2,1,0:T(8,128)(2,1)}, bf16[2,256,1024]{2,1,0:T(8,128)(2,1)}) custom-call(bf16[4,256,2048]{2,1,0:T(8,128)(2,1)} %get-tuple-element.354.refs_0_, bf16[4,256,2048]{2,1,0:T(8,128)(2,1)} %collective-permute-done.17.refs_1_), custom_call_target="tpu_custom_call" | custom-call | bytes 1024 | tf_op jit(solution)/shard_map/pallas_call | solution.py:606
  290.0 6.0 %shard_map.322 = (bf16[2,256,1024]{2,1,0:T(8,128)(2,1)}, bf16[2,256,1024]{2,1,0:T(8,128)(2,1)}, bf16[2,256,1024]{2,1,0:T(8,128)(2,1)}, bf16[2,256,1024]{2,1,0:T(8,128)(2,1)}) custom-call(bf16[4,256,2048]{2,1,0:T(8,128)(2,1)} %get-tuple-element.376.refs_0_, bf16[4,256,2048]{2,1,0:T(8,128)(2,1)} %collective-permute-done.14.refs_1_), custom_call_target="tpu_custom_call" | custom-call | bytes 1024 | tf_op jit(solution)/shard_map/pallas_call | solution.py:606
  296.1 13.2 %shard_map.321 = (bf16[4,256,1536]{2,1,0:T(8,128)(2,1)}, bf16[4,256,1536]{2,1,0:T(8,128)(2,1)}) custom-call(s32[3]{0:T(128)} %pad_add_fusion.me_ref.here_ref, bf16[1024,2048]{1,0:T(8,128)(2,1)} %get-tuple-element.370.refs_0_, bf16[1024,512]{1,0:T(8,128)(2,1)} %get-tuple-element.437.refs_1_.dq, bf16[1024,512]{1,0:T(8,128)(2,1)} %get-tuple-element.389.refs_2_.dk, ...), custom_call_target="tpu_custom_call" | custom-call | bytes 1024 | tf_op jit(solution)/shard_map/pallas_call | solution.py:438
  318.1 15.5 %shard_map.323 = (bf16[1024,2048]{1,0:T(8,128)(2,1)}, f32[1,2048]{1,0:T(1,128)}, f32[1,2048]{1,0:T(1,128)}) custom-call(bf16[1024,512]{1,0:T(8,128)(2,1)} %get-tuple-element.437.refs_1_.dq, bf16[1024,512]{1,0:T(8,128)(2,1)} %get-tuple-element.389.refs_2_.dk, bf16[1024,512]{1,0:T(8,128)(2,1)} %get-tuple-element.438.refs_3_.dv, bf16[2048,512]{1,0:T(8,128)(2,1)} %wq.3, ...), custom_call_target="tpu_custom_call" | custom-call | bytes 1024 | tf_op jit(solution)/shard_map/pallas_call | solution.py:479
  358.2 19.9 %collective-permute-done.25 = bf16[1,256,1024]{2,1,0:T(8,128)(2,1)S(1)} collective-permute-done((bf16[1,256,1024]{2,1,0:T(8,128)(2,1)}, bf16[1,256,1024]{2,1,0:T(8,128)(2,1)S(1)}, u32[]{:S(2)}, u32[]{:S(2)}) %collective-permute-start.25) | collective-permute-done | bytes 524320 | tf_op jit(solution)/shard_map/ppermute | solution.py:560
  425.2 15.3 %collective-permute-done.39 = bf16[512,256]{1,0:T(8,128)(2,1)S(1)} collective-permute-done((bf16[512,256]{1,0:T(8,128)(2,1)S(1)}, bf16[512,256]{1,0:T(8,128)(2,1)S(1)}, u32[]{:S(2)}, u32[]{:S(2)}) %collective-permute-start.39) | collective-permute-done | bytes 262176 | tf_op jit(solution)/shard_map/ppermute | solution.py:1000
  (261 shorter events, 143.1 us)
Async XLA Ops:
  7.2 88.7 %all-gather.5.cloned.1.call-start = ((), (), s32[]{:S(2)}) async-start(), calls=%async_computation.9 | async-start | bytes 2621440 | tf_op jit(solution)/shard_map/all_gather | solution.py:857
  8.8 30.0 %collective-permute-start.2 = (bf16[512,256]{1,0:T(8,128)(2,1)S(1)}, bf16[512,256]{1,0:T(8,128)(2,1)S(1)}, u32[]{:S(2)}, u32[]{:S(2)}) collective-permute-start(bf16[512,256]{1,0:T(8,128)(2,1)S(1)} %constant_dynamic-slice_fusion.6), channel_id=1, source_target_pairs={{0,3},{1,0},{2,1},{3,2},{4,7},{5,4},{6,5},{7,6},{8,11},{9,8},{10,9... | collective-permute-start | bytes 786440 | tf_op jit(solution)/shard_map/ppermute | solution.py:693
  13.9 24.9 %collective-permute-start.1 = (bf16[512,256]{1,0:T(8,128)(2,1)S(1)}, bf16[512,256]{1,0:T(8,128)(2,1)S(1)}, u32[]{:S(2)}, u32[]{:S(2)}) collective-permute-start(bf16[512,256]{1,0:T(8,128)(2,1)S(1)} %constant_dynamic-slice_fusion.6), channel_id=1, source_target_pairs={{0,2},{1,3},{2,0},{3,1},{4,6},{5,7},{6,4},{7,5},{8,10},{9,11},{10,... | collective-permute-start | bytes 786440 | tf_op jit(solution)/shard_map/ppermute | solution.py:693
  13.9 24.9 %collective-permute-start = (bf16[512,256]{1,0:T(8,128)(2,1)S(1)}, bf16[512,256]{1,0:T(8,128)(2,1)S(1)}, u32[]{:S(2)}, u32[]{:S(2)}) collective-permute-start(bf16[512,256]{1,0:T(8,128)(2,1)S(1)} %constant_dynamic-slice_fusion.6), channel_id=1, source_target_pairs={{0,1},{1,2},{2,3},{3,0},{4,5},{5,6},{6,7},{7,4},{8,9},{9,10},{10,1... | collective-permute-start | bytes 786440 | tf_op jit(solution)/shard_map/ppermute | solution.py:693
  38.9 93.4 %all-gather.7.cloned.1.call-start = ((), (), s32[]{:S(2)}) async-start(), calls=%async_computation.10 | async-start | bytes 2621440 | tf_op jit(solution)/shard_map/all_gather | solution.py:860
  55.3 127.3 %reduce-scatter.5.cloned.1.call-start = ((), (), s32[]{:S(2)}) async-start(), calls=%async_computation.5 | async-start | bytes 2621440 | tf_op jit(solution)/shard_map/reduce_scatter | solution.py:895
  56.8 24.7 %collective-permute-start.7 = (bf16[2,1024,256]{2,1,0:T(8,128)(2,1)S(1)}, bf16[2,1024,256]{2,1,0:T(8,128)(2,1)S(1)}, u32[]{:S(2)}, u32[]{:S(2)}) collective-permute-start(bf16[2,1024,256]{2,1,0:T(8,128)(2,1)S(1)} %pad_maximum_fusion.3.refs_0_.refs_1_), channel_id=1, source_target_pairs={{0,16},{4,20},{8,24},{12,28},{16,0},{20,4},{24,8},{28,12},{1,17},{... | collective-permute-start | bytes 3145736 | tf_op jit(solution)/shard_map/ppermute | solution.py:560
  59.7 24.5 %collective-permute-start.8 = (bf16[2,1024,256]{2,1,0:T(8,128)(2,1)S(1)}, bf16[2,1024,256]{2,1,0:T(8,128)(2,1)}, u32[]{:S(2)}, u32[]{:S(2)}) collective-permute-start(bf16[2,1024,256]{2,1,0:T(8,128)(2,1)S(1)} %pad_maximum_fusion.4.refs_2_.refs_3_), channel_id=1, source_target_pairs={{0,8},{4,12},{8,0},{12,4},{16,24},{20,28},{24,16},{28,20},{1,9},{5... | collective-permute-start | bytes 3145736 | tf_op jit(solution)/shard_map/ppermute | solution.py:560
  132.3 90.4 %reduce-scatter.7.cloned.1.call-start = ((), (), s32[]{:S(2)}) async-start(), calls=%async_computation.6 | async-start | bytes 2621440 | tf_op jit(solution)/shard_map/reduce_scatter | solution.py:902
  231.0 30.2 %collective-permute-start.14 = (bf16[4,256,2048]{2,1,0:T(8,128)(2,1)}, bf16[4,256,2048]{2,1,0:T(8,128)(2,1)}, u32[]{:S(2)}, u32[]{:S(2)}) collective-permute-start(bf16[4,256,2048]{2,1,0:T(8,128)(2,1)} %get-tuple-element.347), channel_id=1, source_target_pairs={{0,4},{4,0},{8,12},{12,8},{16,20},{20,16},{24,28},{28,24},{1,5},{5... | collective-permute-start | bytes 12582920 | tf_op jit(solution)/shard_map/ppermute | solution.py:560
  231.5 29.7 %all-to-all-start = ((bf16[4,2,128,512]{3,2,1,0:T(8,128)(2,1)}), bf16[4,2,128,512]{3,2,1,0:T(8,128)(2,1)S(1)}, u32[]{:S(2)}, u32[]{:S(2)}) async-start(bf16[4,2,128,512]{3,2,1,0:T(8,128)(2,1)} %get-tuple-element.348), calls=%async_computation.2 | async-start | bytes 2097152 | tf_op jit(solution)/shard_map/all_to_all | solution.py:578
  235.0 123.1 %reduce-scatter.9.cloned.1.call-start = ((), (), s32[]{:S(2)}) async-start(), calls=%async_computation.7 | async-start | bytes 5242880 | tf_op jit(solution)/shard_map/reduce_scatter | solution.py:937
  262.2 185.4 %reduce-scatter.11.cloned.1.call-start = ((), (), s32[]{:S(2)}) async-start(), calls=%async_computation.8 | async-start | bytes 5242880 | tf_op jit(solution)/shard_map/reduce_scatter | solution.py:958
  262.2 26.4 %collective-permute-start.15 = (bf16[2,256,1024]{2,1,0:T(8,128)(2,1)}, bf16[2,256,1024]{2,1,0:T(8,128)(2,1)S(1)}, u32[]{:S(2)}, u32[]{:S(2)}) collective-permute-start(bf16[2,256,1024]{2,1,0:T(8,128)(2,1)} %get-tuple-element.351), channel_id=1, source_target_pairs={{0,8},{4,12},{8,0},{12,4},{16,24},{20,28},{24,16},{28,20},{1,9},{5... | collective-permute-start | bytes 3145736 | tf_op jit(solution)/shard_map/ppermute | solution.py:560
  263.4 25.2 %collective-permute-start.16 = (bf16[2,256,1024]{2,1,0:T(8,128)(2,1)S(1)}, bf16[2,256,1024]{2,1,0:T(8,128)(2,1)S(1)}, u32[]{:S(2)}, u32[]{:S(2)}) collective-permute-start(bf16[2,256,1024]{2,1,0:T(8,128)(2,1)S(1)} %copy-done.38), channel_id=1, source_target_pairs={{0,16},{4,20},{8,24},{12,28},{16,0},{20,4},{24,8},{28,12},{1,17},{... | collective-permute-start | bytes 3145736 | tf_op jit(solution)/shard_map/ppermute | solution.py:560
  313.7 32.7 %collective-permute-start.21 = (bf16[2,256,1024]{2,1,0:T(8,128)(2,1)}, bf16[2,256,1024]{2,1,0:T(8,128)(2,1)}, u32[]{:S(2)}, u32[]{:S(2)}) collective-permute-start(bf16[2,256,1024]{2,1,0:T(8,128)(2,1)} %get-tuple-element.409), channel_id=1, source_target_pairs={{0,8},{4,12},{8,0},{12,4},{16,24},{20,28},{24,16},{28,20},{1,9},{5... | collective-permute-start | bytes 3145736 | tf_op jit(solution)/shard_map/ppermute | solution.py:560
  315.2 31.3 %collective-permute-start.22 = (bf16[2,256,1024]{2,1,0:T(8,128)(2,1)}, bf16[2,256,1024]{2,1,0:T(8,128)(2,1)}, u32[]{:S(2)}, u32[]{:S(2)}) collective-permute-start(bf16[2,256,1024]{2,1,0:T(8,128)(2,1)} %get-tuple-element.411), channel_id=1, source_target_pairs={{0,16},{4,20},{8,24},{12,28},{16,0},{20,4},{24,8},{28,12},{1,17},{... | collective-permute-start | bytes 3145736 | tf_op jit(solution)/shard_map/ppermute | solution.py:560
  346.5 31.6 %collective-permute-start.23 = (bf16[2,256,768]{2,1,0:T(8,128)(2,1)}, bf16[2,256,768]{2,1,0:T(8,128)(2,1)S(1)}, u32[]{:S(2)}, u32[]{:S(2)}) collective-permute-start(bf16[2,256,768]{2,1,0:T(8,128)(2,1)} %get-tuple-element.417), channel_id=1, source_target_pairs={{0,8},{4,12},{8,0},{12,4},{16,24},{20,28},{24,16},{28,20},{1,9},{5... | collective-permute-start | bytes 2359304 | tf_op jit(solution)/shard_map/ppermute | solution.py:560
  347.5 30.6 %collective-permute-start.24 = (bf16[2,256,768]{2,1,0:T(8,128)(2,1)}, bf16[2,256,768]{2,1,0:T(8,128)(2,1)}, u32[]{:S(2)}, u32[]{:S(2)}) collective-permute-start(bf16[2,256,768]{2,1,0:T(8,128)(2,1)} %get-tuple-element.419), channel_id=1, source_target_pairs={{0,16},{4,20},{8,24},{12,28},{16,0},{20,4},{24,8},{28,12},{1,17},{... | collective-permute-start | bytes 2359304 | tf_op jit(solution)/shard_map/ppermute | solution.py:560
  348.7 29.4 %collective-permute-start.25 = (bf16[1,256,1024]{2,1,0:T(8,128)(2,1)}, bf16[1,256,1024]{2,1,0:T(8,128)(2,1)S(1)}, u32[]{:S(2)}, u32[]{:S(2)}) collective-permute-start(bf16[1,256,1024]{2,1,0:T(8,128)(2,1)} %get-tuple-element.421), channel_id=1, source_target_pairs={{0,16},{4,20},{8,24},{12,28},{16,0},{20,4},{24,8},{28,12},{1,17},{... | collective-permute-start | bytes 1572872 | tf_op jit(solution)/shard_map/ppermute | solution.py:560
  349.7 28.3 %collective-permute-start.26 = (bf16[1,256,1024]{2,1,0:T(8,128)(2,1)}, bf16[1,256,1024]{2,1,0:T(8,128)(2,1)}, u32[]{:S(2)}, u32[]{:S(2)}) collective-permute-start(bf16[1,256,1024]{2,1,0:T(8,128)(2,1)} %get-tuple-element.423), channel_id=1, source_target_pairs={{0,8},{4,12},{8,0},{12,4},{16,24},{20,28},{24,16},{28,20},{1,9},{5... | collective-permute-start | bytes 1572872 | tf_op jit(solution)/shard_map/ppermute | solution.py:560
  406.7 33.8 %collective-permute-start.39 = (bf16[512,256]{1,0:T(8,128)(2,1)S(1)}, bf16[512,256]{1,0:T(8,128)(2,1)S(1)}, u32[]{:S(2)}, u32[]{:S(2)}) collective-permute-start(bf16[512,256]{1,0:T(8,128)(2,1)S(1)} %bitcast.119), channel_id=1, source_target_pairs={{0,2},{1,3},{2,0},{3,1},{4,6},{5,7},{6,4},{7,5},{8,10},{9,11},{10,... | collective-permute-start | bytes 786440 | tf_op jit(solution)/shard_map/ppermute | solution.py:1000
  407.6 32.8 %collective-permute-start.40 = (bf16[512,256]{1,0:T(8,128)(2,1)S(1)}, bf16[512,256]{1,0:T(8,128)(2,1)S(1)}, u32[]{:S(2)}, u32[]{:S(2)}) collective-permute-start(bf16[512,256]{1,0:T(8,128)(2,1)S(1)} %bitcast.118), channel_id=1, source_target_pairs={{0,1},{1,2},{2,3},{3,0},{4,5},{5,6},{6,7},{7,4},{8,9},{9,10},{10,1... | collective-permute-start | bytes 786440 | tf_op jit(solution)/shard_map/ppermute | solution.py:1000
  408.2 33.2 %collective-permute-start.36 = (bf16[1,256,1024]{2,1,0:T(8,128)(2,1)}, bf16[1,256,1024]{2,1,0:T(8,128)(2,1)S(1)}, u32[]{:S(2)}, u32[]{:S(2)}) collective-permute-start(bf16[1,256,1024]{2,1,0:T(8,128)(2,1)} %get-tuple-element.474), channel_id=1, source_target_pairs={{0,16},{4,20},{8,24},{12,28},{16,0},{20,4},{24,8},{28,12},{1,17},{... | collective-permute-start | bytes 1572872 | tf_op jit(solution)/shard_map/ppermute | solution.py:560
  (65 other events, 673.9 us)
Sparse Core Ops, SparseCore 0:
  39.0 46.3 all-gather.4
  87.6 44.6 all-gather.6
  134.6 42.5 reduce-scatter.4
  179.5 43.1 reduce-scatter.6
  261.5 75.6 reduce-scatter.8
  339.4 86.4 reduce-scatter.10

commit v3 on v2

--- a/solution.py
+++ b/solution.py
@@ -59,47 +59,52 @@
     return pl.CostEstimate(flops=COST and flops, bytes_accessed=2**10, transcendentals=0)
 
 
-def key_start(block, size):
-    return max(0, (block * size - (LONGEST - 1)) // size * size)
-
-
-def probabilities(seg_row, seg_col, query, keys, block, size):
-    low, high = key_start(block, size), (block + 1) * size
+def key_start(first):
+    return max(0, (first - (LONGEST - 1)) // 256 * 256)
+
+
+def segment_column(seg_row):
+    length = seg_row.shape[1]
+    return jnp.broadcast_to(seg_row[...], (128, length)).T[:, :1]
+
+
+def probabilities(seg_row, seg_col, query, keys, first, last):
+    low, high = key_start(first), last
     scores = times_trans(keys[low:high, :], query)
-    shape = (high - low, size)
+    shape = (high - low, last - first)
     key_place = lax.broadcasted_iota(jnp.int32, shape, 0) + low
-    query_place = lax.broadcasted_iota(jnp.int32, shape, 1) + block * size
-    same = seg_col[low:high, :] == seg_row[:, block * size : high]
+    query_place = lax.broadcasted_iota(jnp.int32, shape, 1) + first
+    same = seg_col[low:high, :] == seg_row[:, first:last]
     scores = jnp.where(same & (key_place <= query_place), scores, MASKED_SCORE)
     weights = jnp.exp(scores - jnp.max(scores, axis=0, keepdims=True))
     return weights * (1.0 / jnp.sum(weights, axis=0, keepdims=True))
 
 
-def forward_kernel(size, seg_row, seg_col, query, key, value, *outs):
-    part = outs[0].shape[1]
-    for block in range(query.shape[0] // size):
-        low, high = key_start(block, size), (block + 1) * size
-        rows = slice(block * size, high)
-        probs = probabilities(seg_row, seg_col, query[rows, :], key, block, size)
-        attended = trans_times(probs.astype(BF16), value[low:high, :]).astype(BF16)
-        for piece in range(size // part):
-            share, c = divmod(block * (size // part) + piece, PARTS)
-            outs[c][share] = attended[piece * part : (piece + 1) * part, :]
-
-
-def backward_kernel(size, seg_row, seg_col, query, key, value, got, *refs):
+def forward_kernel(c, seg_row, query, key, value, out):
+    groups, part = out.shape[:2]
+    seg_col = segment_column(seg_row)
+    for t in range(groups):
+        first = (t * PARTS + c) * part
+        last = first + part
+        low = key_start(first)
+        probs = probabilities(seg_row, seg_col, query[first:last, :], key, first, last)
+        out[t] = trans_times(probs.astype(BF16), value[low:last, :]).astype(BF16)
+
+
+def backward_kernel(size, seg_row, query, key, value, got, *refs):
     d_query, d_key, d_value, d_attended, key_sum, value_sum = refs
     groups, parts, part = got.shape[:3]
     for t in range(groups):
         for c in range(parts):
             start = (t * parts + c) * part
             d_attended[start : start + part, :] = got[t, c]
+    seg_col = segment_column(seg_row)
     key_sum[...] = jnp.zeros_like(key_sum)
     value_sum[...] = jnp.zeros_like(value_sum)
     for block in range(query.shape[0] // size):
-        low, high = key_start(block, size), (block + 1) * size
+        low, high = key_start(block * size), (block + 1) * size
         rows = slice(block * size, high)
-        probs = probabilities(seg_row, seg_col, query[rows, :], key, block, size)
+        probs = probabilities(seg_row, seg_col, query[rows, :], key, block * size, high)
         value_sum[low:high, :] += mm(probs.astype(BF16), d_attended[rows, :])
         d_probs = times_trans(value[low:high, :], d_attended[rows, :])
         inner = jnp.sum(probs * d_probs, axis=0, keepdims=True)
@@ -110,29 +115,19 @@
     d_value[...] = value_sum[...].astype(BF16)
 
 
-def segment_views(segments):
-    seqs, length = segments.shape
-    return segments.reshape(seqs, 1, length), segments.reshape(seqs, length, 1)
-
-
-def attend(segments, query, key, value, groups):
+def attend(c, segments, query, key, value, groups):
     length, local = query.shape
     part = length // groups // PARTS
     tall = pl.BlockSpec((length, HEAD_DIM), lambda h: (0, h))
-    out = jax.ShapeDtypeStruct((groups, part, local), BF16)
     return pl.pallas_call(
-        functools.partial(forward_kernel, min(256, length)),
+        functools.partial(forward_kernel, c),
         grid=(local // HEAD_DIM,),
-        in_specs=[
-            pl.BlockSpec((None, 1, length), lambda h: (0, 0, 0)),
-            pl.BlockSpec((None, length, 1), lambda h: (0, 0, 0)),
-        ]
-        + [tall] * 3,
-        out_specs=[pl.BlockSpec((groups, part, HEAD_DIM), lambda h: (0, 0, h))] * PARTS,
-        out_shape=[out] * PARTS,
+        in_specs=[pl.BlockSpec((1, length), lambda h: (0, 0))] + [tall] * 3,
+        out_specs=pl.BlockSpec((groups, part, HEAD_DIM), lambda h: (0, 0, h)),
+        out_shape=jax.ShapeDtypeStruct((groups, part, local), BF16),
         compiler_params=pltpu.CompilerParams(vmem_limit_bytes=VMEM),
-        cost_estimate=cost(4 * length * length * local),
-    )(*segment_views(segments), query, key, value)
+        cost_estimate=cost(2**20),
+    )(segments, query, key, value)
 
 
 def attend_back(segments, query, key, value, got):
@@ -141,10 +136,7 @@
     return pl.pallas_call(
         functools.partial(backward_kernel, min(256, length)),
         grid=(query.shape[1] // HEAD_DIM,),
-        in_specs=[
-            pl.BlockSpec((None, 1, length), lambda h: (0, 0, 0)),
-            pl.BlockSpec((None, length, 1), lambda h: (0, 0, 0)),
-        ]
+        in_specs=[pl.BlockSpec((1, length), lambda h: (0, 0))]
         + [tall] * 3
         + [pl.BlockSpec(got.shape[:3] + (HEAD_DIM,), lambda h: (0, 0, 0, h))],
         out_specs=[tall] * 3,
@@ -156,7 +148,7 @@
         out_shape=[jax.ShapeDtypeStruct(query.shape, BF16)] * 3,
         compiler_params=pltpu.CompilerParams(vmem_limit_bytes=VMEM),
         cost_estimate=cost(10 * query.shape[0] * length * query.shape[1]),
-    )(*segment_views(segments), query, key, value, got)
+    )(segments, query, key, value, got)
 
 
 def place_bits(blocks):
@@ -493,7 +485,7 @@
 
 def input_back(d_normed, x, d_mid, gain):
     rows, width = x.shape
-    size = min(64, rows)
+    size = min(128, rows)
 
     def kernel(terms, x_ref, mid, gain_ref, out):
         values = x_ref[...].astype(F32)
@@ -616,6 +608,38 @@
     )(*flat)
 
 
+def finish_sum(live, width, cuts, turned, kind):
+    rows, columns = live[0].shape[1:]
+    count = columns // width
+    total = 2 * columns
+
+    def kernel(*refs):
+        sums = []
+        for c in range(2 * count):
+            keep, got = refs[2 * (c % 2) : 2 * (c % 2) + 2]
+            place = slice(c // 2 * width, (c // 2 + 1) * width)
+            sums.append(keep[0, :, place].astype(F32) + got[0, :, place].astype(F32))
+        value = jnp.concatenate(sums, axis=1)
+        if turned:
+            refs[4][...] = value.T.astype(kind)
+            return
+        for k in range(cuts):
+            refs[4 + k][...] = value[:, k * total // cuts : (k + 1) * total // cuts].astype(kind)
+
+    size = rows if turned else min(64, rows)
+    shape = (total, rows) if turned else (rows, total // cuts)
+    block = (total, rows) if turned else (size, total // cuts)
+    return pl.pallas_call(
+        kernel,
+        grid=(rows // size,),
+        in_specs=[pl.BlockSpec((1, size, columns), lambda i: (0, i, 0))] * 4,
+        out_specs=[pl.BlockSpec(block, lambda i: (i, 0) if not turned else (0, 0))] * cuts,
+        out_shape=[jax.ShapeDtypeStruct(shape, kind)] * cuts,
+        compiler_params=pltpu.CompilerParams(vmem_limit_bytes=VMEM),
+        cost_estimate=cost(2**20),
+    )(*live)
+
+
 class DpSum:
     def __init__(self, send, keep, cuts):
         self.live = [send, keep]
@@ -661,15 +685,8 @@
             self.add()
             self.send()
 
-    def total(self):
-        sums = [
-            self.live[2 * odd][0].astype(F32) + self.live[2 * odd + 1][0].astype(F32)
-            for odd in range(2)
-        ]
-        size = self.width
-        return [
-            sums[c % 2][:, c // 2 * size : (c // 2 + 1) * size] for c in range(self.cuts)
-        ]
+    def total(self, cuts=1, turned=False, kind=F32):
+        return finish_sum(self.live, self.width, cuts, turned, kind)
 
 
 class WeightGather:
@@ -850,14 +867,15 @@
         value_weight,
         value_bias,
     )
-    heads = attend(segments, query, key, value, groups)
-    heads = [h.reshape(groups * part, local) for h in heads]
-    cot, *heads = fence([weight], (cotangent, *heads))
-
-    heads[0] = lax.all_gather(heads[0], "tensor", axis=0)
+    heads = [None] * PARTS
+    heads[0] = attend(0, segments, query, key, value, groups)
+    cot, heads[0], query, key, value = fence([weight], (cotangent, heads[0], query, key, value))
+
+    heads[0] = lax.all_gather(heads[0].reshape(groups * part, local), "tensor", axis=0)
     weight.advance(1)
+    heads[1] = attend(1, segments, query, key, value, groups)
     cot, heads[1] = fence([weight], (cot, heads[1]))
-    heads[1] = lax.all_gather(heads[1], "tensor", axis=0)
+    heads[1] = lax.all_gather(heads[1].reshape(groups * part, local), "tensor", axis=0)
     weight.advance(2)
     cot_parts = by_part(cot)
     cots = [(cot_parts, c) for c in range(PARTS)]
@@ -951,17 +969,14 @@
     terms_in, gain1, bias1 = normed_back(
         d_query, d_key, d_value, query_weight, key_weight, value_weight, inputs
     )
+    qkv_sum.split()
+    wo_sum.add()
     gain1, bias1, terms_in, d_query, d_value = fence(
-        [qkv_sum, wo_sum], (gain1, bias1, terms_in, d_query, d_value)
+        [qkv_sum, wo_sum, down_sum], (gain1, bias1, terms_in, d_query, d_value)
     )
 
     d_normed = lax.psum_scatter(
         terms_in.reshape(groups, share, width), "tensor", scatter_dimension=0
-    )
-    qkv_sum.split()
-    wo_sum.add()
-    gain1, bias1, d_query, d_value = fence(
-        [qkv_sum, wo_sum, down_sum], (gain1, bias1, d_query, d_value)
     )
     qkv_sum.first(0, 1)
     wo_sum.send()
@@ -980,38 +995,43 @@
         ],
         me[:1],
     )
+    small.tensor()
     down_sum.add()
     out_sum, *_ = fence([qkv_sum, wo_sum, down_sum, small, up_sum], (out_sum,))
+    down_sum.send()
     qkv_sum.add()
     qkv_sum.send()
-    down_sum.send()
-    small.tensor()
-    wo_terms = jnp.concatenate(wo_sum.total(), axis=1).T
-    wo_terms = wo_terms.astype(BF16).reshape(groups, local, size)
+    small.move()
+    small.move()
+    small.move()
+    wo_terms = wo_sum.total(turned=True, kind=BF16)[0].reshape(groups, local, size)
     to_all = [
         lax.dynamic_index_in_dim(wo_terms, (here - m) % groups, 0, keepdims=False)
         for m in range(groups)
     ]
     up_sum.add()
     out_sum, *to_all = fence([qkv_sum, small, down_sum, up_sum], (out_sum, *to_all))
-    output_weight_grad = to_all[0].astype(F32)
+    wo_got = [to_all[0]]
     for m in range(1, groups):
         ring = [(i, (i - m) % groups) for i in range(groups)]
-        output_weight_grad = output_weight_grad + lax.ppermute(to_all[m], "tensor", ring).astype(F32)
+        wo_got.append(lax.ppermute(to_all[m], "tensor", ring))
     up_sum.send()
-    small.move()
-    small.move()
-    small.move()
     total = [own_mid[c] + (out_sum[c].astype(F32) + down_bias) for c in range(PARTS)]
     output = jnp.concatenate([t.astype(BF16) for t in total], axis=0)
-    qkv_grad = jnp.concatenate(qkv_sum.total(), axis=1)
-    up_weight_grad = jnp.concatenate(up_sum.total(), axis=1)
-    down_weight_grad = jnp.concatenate(down_sum.total(), axis=1).T
-    up_weight_grad, down_weight_grad, qkv_grad, output_weight_grad = fence(
-        [small], (up_weight_grad, down_weight_grad, qkv_grad, output_weight_grad)
-    )
-    (d_normed,) = fence([small], (d_normed,))
-    input_grad = input_back(d_normed, own(inputs), jnp.concatenate(d_mids, axis=0), norm1_gain)
+    qkv_grads = qkv_sum.total(3)
+    (up_weight_grad,) = up_sum.total()
+    (down_weight_grad,) = down_sum.total(turned=True)
+    d_mid = jnp.concatenate(d_mids, axis=0)
+    rows_own = own(inputs)
+    small_sums = small.total()
+    up_weight_grad, down_weight_grad, output, d_mid, rows_own, *others = fence(
+        [],
+        (up_weight_grad, down_weight_grad, output, d_mid, rows_own, *qkv_grads, *small_sums),
+    )
+    qkv_grads, small_sums = others[:3], others[3:]
+    input_grad = input_back(d_normed, rows_own, d_mid, norm1_gain)
+    input_grad, *wo_got = fence([], (input_grad, *wo_got))
+    output_weight_grad = sum(g.astype(F32) for g in wo_got)
     (
         norm1_gain_grad,
         norm1_bias_grad,
@@ -1022,16 +1042,16 @@
         query_bias_grad,
         value_bias_grad,
         up_bias_grad,
-    ) = small.total()
+    ) = small_sums
     return (
         output,
         input_grad,
         norm1_gain_grad,
         norm1_bias_grad,
-        qkv_grad[:, :local],
+        qkv_grads[0],
         query_bias_grad,
-        qkv_grad[:, local : 2 * local],
-        qkv_grad[:, 2 * local :],
+        qkv_grads[1],
+        qkv_grads[2],
         value_bias_grad,
         output_weight_grad,
         output_bias_grad,

time: 469 us -> 455 us (0.970)
  Pallas kernels: 265 us -> 282 us
  waiting for transfers between devices: 90.8 us -> 79.4 us
  local copies, waits for them, and re-layouts: 26.3 us -> 16.8 us
  other arithmetic: 22.6 us -> 15 us
    pallas_call x1 -> x6, Pallas kernels: 8.83 us -> 26.6 us  [the longest x4 13.8 us: finish_sum(): pl.pallas_call(kernel, grid=(rows // size,), in_specs=[pl.BlockSpec((1, s...]
    ppermute x3, waiting for transfers between devices: 15.3 us -> 6.99 us  [on_device(): wo_got.append(lax.ppermute(to_all[m], 'tensor', ring))]
    add x9 -> x1, other arithmetic: 7.49 us -> 2.02 us  [on_device(): output_weight_grad = sum((g.astype(F32) for g in wo_got))]
    unnamed x81 -> x72, local copies, waits for them, and re-layouts: 9.49 us -> 6.53 us
  transfers between devices with their start and end apart: 48 -> 48, of which waited for: 17 -> 20; matrix products, arithmetic and copies ran while one was open for 9% -> 5% of each run, Pallas kernels for 55% -> 61%
where the time goes in v3:
time: 455 us; the launch traced here: 447 us
  Pallas kernels  282 us (62%)
  waiting for transfers between devices  79.4 us (17%)
  starting transfers between devices  39.2 us (9%)
  local copies, waits for them, and re-layouts  16.8 us (4%)
  other arithmetic  15 us (3%)
  between operations  15 us (3%)
    pallas_call x2, Pallas kernels, middle_call(): pl.pallas_call(functools.partial(middle_kernel, (first, second)), grid_sp...  55.3 us
    pallas_call x4, Pallas kernels, gradient_terms(): pl.pallas_call(kernel, grid_spec=pltpu.PrefetchScalarGridSpec(num_scalar_...  54.5 us
    ppermute x35, waiting for transfers between devices, swap_bit(): return lax.ppermute(values, axis, [(i, i ^ 1 << bit) for i in range(size)])  49.9 us
    pallas_call x8, Pallas kernels, add_and_split(): pl.pallas_call(kernel, grid=(rows // size,), in_specs=[block(places, v.sh...  40.2 us
    pallas_call x2, Pallas kernels, both_parts(): pl.pallas_call(kernel, grid=(columns // block,), in_specs=[left_spec(left...  26.8 us
    ppermute x35, starting transfers between devices, swap_bit(): return lax.ppermute(values, axis, [(i, i ^ 1 << bit) for i in range(size)])  26.5 us
    pallas_call x1, Pallas kernels, attend_back(): pl.pallas_call(functools.partial(backward_kernel, min(256, length)), grid...  17.3 us
    pallas_call x2, Pallas kernels, middle_back(): pl.pallas_call(functools.partial(middle_back_kernel, len(before)), grid=(...  16.7 us
  transfers between devices with their start and end apart: 48, of which 20 were waited for; matrix products, arithmetic and copies ran while one was open for 5% of the time, Pallas kernels for 61%

profile of v3, /device:TPU:0, one launch (start us, length us, event | category | flops | bytes accessed | tf_op | source)
XLA Modules:
  0.0 447.0 jit_solution(2370942166163541905)
XLA Ops:
  14.9 13.4 %shard_map.305 = (bf16[1024,2048]{1,0:T(8,128)(2,1)}, bf16[1024,512]{1,0:T(8,128)(2,1)}, bf16[1024,512]{1,0:T(8,128)(2,1)}, bf16[1024,512]{1,0:T(8,128)(2,1)}) custom-call(bf16[1024,2048]{1,0:T(8,128)(2,1)} %x.3, f32[1,2048]{1,0:T(1,128)} %bitcast.99, f32[1,2048]{1,0:T(1,128)} %bitcast.107, bf16[2048,512]{1,0:T(8,128)(2,1)} %wq.3, f32[1,512]{1,0:T(1,128)} %bitcast.108, ...), custom_call_target="tpu_custom_call" | custom-call | bytes 1024 | tf_op jit(solution)/shard_map/pallas_call | solution.py:192
  28.3 6.2 %shard_map.306 = bf16[4,128,512]{2,1,0:T(8,128)(2,1)} custom-call(s32[1,1024]{1,0:T(1,128)} %seg_row.5, bf16[1024,512]{1,0:T(8,128)(2,1)} %get-tuple-element.274.query, bf16[1024,512]{1,0:T(8,128)(2,1)} %get-tuple-element.275.key, bf16[1024,512]{1,0:T(8,128)(2,1)} %get-tuple-element.276.value), custom_call_target="tpu_custom_call" | custom-call | bytes 1024 | tf_op jit(solution)/shard_map/pallas_call | solution.py:122
  39.9 6.6 %shard_map.307 = bf16[4,128,512]{2,1,0:T(8,128)(2,1)} custom-call(s32[1,1024]{1,0:T(1,128)} %seg_row.5, bf16[1024,512]{1,0:T(8,128)(2,1)} %get-tuple-element.274.query, bf16[1024,512]{1,0:T(8,128)(2,1)} %get-tuple-element.275.key, bf16[1024,512]{1,0:T(8,128)(2,1)} %get-tuple-element.276.value), custom_call_target="tpu_custom_call" | custom-call | bytes 1024 | tf_op jit(solution)/shard_map/pallas_call | solution.py:122
  58.7 13.4 %shard_map.309.d_hid = bf16[2,512,2048]{2,1,0:T(8,128)(2,1)} custom-call(bf16[4,2,128,2048]{3,2,1,0:T(8,128)(2,1)} %bitcast.67, bf16[4,2,128,2048]{3,2,1,0:T(8,128)(2,1)} %bitcast.68, bf16[2048,2048]{1,0:T(8,128)(2,1)} %refs_2_.3), custom_call_target="tpu_custom_call" | custom-call | bytes 1024 | tf_op jit(solution)/shard_map/pallas_call | solution.py:539
  87.6 5.7 %shard_map.310.wo.refs_4_ = bf16[2048,2048]{1,0:T(8,128)(2,1)} custom-call(s32[3]{0:T(128)} %pad_add_fusion.me_ref.here_ref, bf16[2,1024,256]{2,1,0:T(8,128)(2,1)} %copy-done.8, bf16[2,1024,256]{2,1,0:T(8,128)(2,1)} %copy-done.8, bf16[2,1024,256]{2,1,0:T(8,128)(2,1)} %collective-permute-done.8.refs_2_.refs_3_, ...), custom_call_target="tpu_custom_call", output_to_operand_aliasing={{}: (9, {})} | custom-call | bytes 1024 | tf_op jit(solution)/shard_map/pallas_call | solution.py:760
  93.2 27.6 %shard_map.311 = (f32[128,2048]{1,0:T(8,128)}, bf16[512,2048]{1,0:T(8,128)(2,1)}, bf16[512,2048]{1,0:T(8,128)(2,1)}, bf16[512,2048]{1,0:T(8,128)(2,1)}, bf16[512,2048]{1,0:T(8,128)(2,1)}) custom-call(s32[3]{0:T(128)} %pad_add_fusion.me_ref.here_ref, bf16[4,512,512]{2,1,0:T(8,128)(2,1)} %all-gather.3.cloned.1.call-done.heads, ...), custom_call_target="tpu_custom_call" | custom-call | bytes 1024 | tf_op jit(solution)/shard_map/pallas_call | solution.py:276
  120.9 8.4 %all-gather.5.cloned.1.call-done.heads = bf16[4,512,512]{2,1,0:T(8,128)(2,1)} async-done(((bf16[1,512,512]{2,1,0:T(8,128)(2,1)}), bf16[4,512,512]{2,1,0:T(8,128)(2,1)}) %all-gather.5.cloned.1.call-update) | async-done | bytes 2097168 | tf_op jit(solution)/shard_map/all_gather | solution.py:878
  131.3 27.7 %shard_map.312 = (f32[128,2048]{1,0:T(8,128)}, bf16[512,2048]{1,0:T(8,128)(2,1)}, bf16[512,2048]{1,0:T(8,128)(2,1)}, bf16[512,2048]{1,0:T(8,128)(2,1)}, bf16[512,2048]{1,0:T(8,128)(2,1)}) custom-call(s32[3]{0:T(128)} %pad_add_fusion.me_ref.here_ref, bf16[4,512,512]{2,1,0:T(8,128)(2,1)} %all-gather.5.cloned.1.call-done.heads, ...), custom_call_target="tpu_custom_call" | custom-call | bytes 1024 | tf_op jit(solution)/shard_map/pallas_call | solution.py:276
  163.3 15.3 %shard_map.313 = (bf16[4,256,2048]{2,1,0:T(8,128)(2,1)}, bf16[4,256,2048]{2,1,0:T(8,128)(2,1)}) custom-call(s32[3]{0:T(128)} %pad_add_fusion.me_ref.here_ref, bf16[512,2048]{1,0:T(8,128)(2,1)} %get-tuple-element.310.refs_0_, bf16[512,2048]{1,0:T(8,128)(2,1)} %get-tuple-element.311.refs_1_, bf16[512,2048]{1,0:T(8,128)(2,1)} %get-tuple-element.312.refs_2_, ...), custom_call_target="tpu_custom_call" | custom-call | bytes 1024 | tf_op jit(solution)/shard_map/pallas_call | solution.py:430
  179.7 8.4 %shard_map.314 = (f32[128,2048]{1,0:T(8,128)}, bf16[128,2048]{1,0:T(8,128)(2,1)}, f32[8,2048]{1,0:T(8,128)}, bf16[4,1,128,512]{3,2,1,0:T(8,128)(2,1)}) custom-call(bf16[128,2048]{1,0:T(8,128)(2,1)} %bitcast.93, f32[128,2048]{1,0:T(8,128)} %get-tuple-element.319.refs_1_, bf16[128,2048]{1,0:T(8,128)(2,1)} %get-tuple-element.527.refs_2_, f32[1,2048]{1,0:T(1,128)} %bitcast.97, ...), custom_call_target="tpu_custom_call" | custom-call | bytes 1024 | tf_op jit(solution)/shard_map/pallas_call | solution.py:350
  188.1 13.3 %shard_map.315 = bf16[4,2,128,2048]{3,2,1,0:T(8,128)(2,1)} custom-call(bf16[512,2048]{1,0:T(8,128)(2,1)} %get-tuple-element.326.refs_0_.refs_2_, bf16[512,2048]{1,0:T(8,128)(2,1)} %get-tuple-element.327.refs_1_.refs_3_, bf16[2048,2048]{1,0:T(8,128)(2,1)} %refs_2_.3), custom_call_target="tpu_custom_call" | custom-call | bytes 1024 | tf_op jit(solution)/shard_map/pallas_call | solution.py:539
  201.4 15.4 %shard_map.316 = (bf16[4,256,2048]{2,1,0:T(8,128)(2,1)}, bf16[4,256,2048]{2,1,0:T(8,128)(2,1)}) custom-call(s32[3]{0:T(128)} %pad_add_fusion.me_ref.here_ref, bf16[4,2,128,2048]{3,2,1,0:T(8,128)(2,1)} %bitcast.69, bf16[4,2,128,2048]{3,2,1,0:T(8,128)(2,1)} %bitcast.70, bf16[512,2048]{1,0:T(8,128)(2,1)} %get-tuple-element.326.refs_0_.refs_2_, ...), custom_call_target="tpu_custom_call" | custom-call | bytes 1024 | tf_op jit(solution)/shard_map/pallas_call | solution.py:430
  219.7 8.3 %shard_map.317 = (f32[128,2048]{1,0:T(8,128)}, bf16[128,2048]{1,0:T(8,128)(2,1)}, f32[8,2048]{1,0:T(8,128)}, bf16[4,2,128,512]{3,2,1,0:T(8,128)(2,1)}) custom-call(bf16[128,2048]{1,0:T(8,128)(2,1)} %bitcast.94, f32[128,2048]{1,0:T(8,128)} %get-tuple-element.339.refs_1_, bf16[128,2048]{1,0:T(8,128)(2,1)} %get-tuple-element.526.refs_2_, f32[1,2048]{1,0:T(1,128)} %bitcast.98, ...), custom_call_target="tpu_custom_call" | custom-call | bytes 1024 | tf_op jit(solution)/shard_map/pallas_call | solution.py:350
  232.1 10.6 %shard_map.318 = (bf16[4,256,2048]{2,1,0:T(8,128)(2,1)}, bf16[4,256,2048]{2,1,0:T(8,128)(2,1)}) custom-call(s32[3]{0:T(128)} %pad_add_fusion.me_ref.here_ref, bf16[128,2048]{1,0:T(8,128)(2,1)} %get-tuple-element.344.refs_0_, bf16[128,2048]{1,0:T(8,128)(2,1)} %get-tuple-element.345.refs_1_, bf16[4,4,128,512]{3,2,1,0:T(8,128)(2,1)} %bitcast.73, ...), custom_call_target="tpu_custom_call" | custom-call | bytes 1024 | tf_op jit(solution)/shard_map/pallas_call | solution.py:430
  242.7 6.1 %shard_map.319 = (bf16[2,256,1024]{2,1,0:T(8,128)(2,1)}, bf16[2,256,1024]{2,1,0:T(8,128)(2,1)}, bf16[2,256,1024]{2,1,0:T(8,128)(2,1)}, bf16[2,256,1024]{2,1,0:T(8,128)(2,1)}) custom-call(bf16[4,256,2048]{2,1,0:T(8,128)(2,1)} %get-tuple-element.348.refs_0_, bf16[4,256,2048]{2,1,0:T(8,128)(2,1)} %collective-permute-done.13.refs_1_), custom_call_target="tpu_custom_call" | custom-call | bytes 1024 | tf_op jit(solution)/shard_map/pallas_call | solution.py:598
  248.8 9.5 %all-to-all-done.got = bf16[4,2,128,512]{3,2,1,0:T(8,128)(2,1)S(1)} async-done(((bf16[4,2,128,512]{3,2,1,0:T(8,128)(2,1)}), bf16[4,2,128,512]{3,2,1,0:T(8,128)(2,1)S(1)}, u32[]{:S(2)}, u32[]{:S(2)}) %all-to-all-start) | async-done | bytes 1048608 | tf_op jit(solution)/shard_map/all_to_all | solution.py:570
  262.1 17.3 %shard_map.321 = (bf16[1024,512]{1,0:T(8,128)(2,1)}, bf16[1024,512]{1,0:T(8,128)(2,1)}, bf16[1024,512]{1,0:T(8,128)(2,1)}) custom-call(s32[1,1024]{1,0:T(1,128)} %seg_row.5, bf16[1024,512]{1,0:T(8,128)(2,1)} %get-tuple-element.274.query, bf16[1024,512]{1,0:T(8,128)(2,1)} %get-tuple-element.275.key, bf16[1024,512]{1,0:T(8,128)(2,1)} %get-tuple-element.276.value, ...), custom_call_target="tpu_custom_call" | custom-call | bytes 1024 | tf_op jit(solution)/shard_map/pallas_call | solution.py:136
  279.5 6.0 %shard_map.320 = (bf16[2,256,1024]{2,1,0:T(8,128)(2,1)}, bf16[2,256,1024]{2,1,0:T(8,128)(2,1)}, bf16[2,256,1024]{2,1,0:T(8,128)(2,1)}, bf16[2,256,1024]{2,1,0:T(8,128)(2,1)}) custom-call(bf16[4,256,2048]{2,1,0:T(8,128)(2,1)} %get-tuple-element.362.refs_0_, bf16[4,256,2048]{2,1,0:T(8,128)(2,1)} %collective-permute-done.17.refs_1_), custom_call_target="tpu_custom_call" | custom-call | bytes 1024 | tf_op jit(solution)/shard_map/pallas_call | solution.py:598
  287.2 6.1 %shard_map.323 = (bf16[2,256,1024]{2,1,0:T(8,128)(2,1)}, bf16[2,256,1024]{2,1,0:T(8,128)(2,1)}, bf16[2,256,1024]{2,1,0:T(8,128)(2,1)}, bf16[2,256,1024]{2,1,0:T(8,128)(2,1)}) custom-call(bf16[4,256,2048]{2,1,0:T(8,128)(2,1)} %get-tuple-element.384.refs_0_, bf16[4,256,2048]{2,1,0:T(8,128)(2,1)} %collective-permute-done.14.refs_1_), custom_call_target="tpu_custom_call" | custom-call | bytes 1024 | tf_op jit(solution)/shard_map/pallas_call | solution.py:598
  293.3 13.1 %shard_map.322 = (bf16[4,256,1536]{2,1,0:T(8,128)(2,1)}, bf16[4,256,1536]{2,1,0:T(8,128)(2,1)}) custom-call(s32[3]{0:T(128)} %pad_add_fusion.me_ref.here_ref, bf16[1024,2048]{1,0:T(8,128)(2,1)} %get-tuple-element.378.refs_0_, bf16[1024,512]{1,0:T(8,128)(2,1)} %get-tuple-element.435.refs_1_.dq, bf16[1024,512]{1,0:T(8,128)(2,1)} %get-tuple-element.409.refs_2_.dk, ...), custom_call_target="tpu_custom_call" | custom-call | bytes 1024 | tf_op jit(solution)/shard_map/pallas_call | solution.py:430
  312.5 15.3 %shard_map.326 = (bf16[1024,2048]{1,0:T(8,128)(2,1)}, f32[1,2048]{1,0:T(1,128)}, f32[1,2048]{1,0:T(1,128)}) custom-call(bf16[1024,512]{1,0:T(8,128)(2,1)} %get-tuple-element.435.refs_1_.dq, bf16[1024,512]{1,0:T(8,128)(2,1)} %get-tuple-element.409.refs_2_.dk, bf16[1024,512]{1,0:T(8,128)(2,1)} %get-tuple-element.436.refs_3_.dv, bf16[2048,512]{1,0:T(8,128)(2,1)} %wq.3, ...), custom_call_target="tpu_custom_call" | custom-call | bytes 1024 | tf_op jit(solution)/shard_map/pallas_call | solution.py:471
  358.9 15.5 %collective-permute-done.25.refs_1_ = bf16[1,256,1024]{2,1,0:T(8,128)(2,1)S(1)} collective-permute-done((bf16[1,256,1024]{2,1,0:T(8,128)(2,1)}, bf16[1,256,1024]{2,1,0:T(8,128)(2,1)S(1)}, u32[]{:S(2)}, u32[]{:S(2)}) %collective-permute-start.25) | collective-permute-done | bytes 524320 | tf_op jit(solution)/shard_map/ppermute | solution.py:552
  399.1 7.6 %collective-permute-done.33 = f32[1920]{0:T(1024)S(1)} collective-permute-done((f32[1920]{0:T(1024)S(1)}, f32[1920]{0:T(1024)S(1)}, u32[]{:S(2)}, u32[]{:S(2)}) %collective-permute-start.33) | collective-permute-done | bytes 7712 | tf_op jit(solution)/shard_map/ppermute | solution.py:552
  430.9 7.0 %collective-permute-done.39 = bf16[512,256]{1,0:T(8,128)(2,1)} collective-permute-done((bf16[512,256]{1,0:T(8,128)(2,1)}, bf16[512,256]{1,0:T(8,128)(2,1)}, u32[]{:S(2)}, u32[]{:S(2)}) %collective-permute-start.39) | collective-permute-done | bytes 262176 | tf_op jit(solution)/shard_map/ppermute | solution.py:1017
  (237 shorter events, 148.0 us)
Async XLA Ops:
  7.2 86.0 %all-gather.3.cloned.1.call-start = ((), (), s32[]{:S(2)}) async-start(), calls=%async_computation.5 | async-start | bytes 2621440 | tf_op jit(solution)/shard_map/all_gather | solution.py:874
  8.8 25.7 %collective-permute-start.2 = (bf16[512,256]{1,0:T(8,128)(2,1)S(1)}, bf16[512,256]{1,0:T(8,128)(2,1)S(1)}, u32[]{:S(2)}, u32[]{:S(2)}) collective-permute-start(bf16[512,256]{1,0:T(8,128)(2,1)S(1)} %constant_dynamic-slice_fusion.2), channel_id=1, source_target_pairs={{0,3},{1,0},{2,1},{3,2},{4,7},{5,4},{6,5},{7,6},{8,11},{9,8},{10,9... | collective-permute-start | bytes 786440 | tf_op jit(solution)/shard_map/ppermute | solution.py:710
  36.3 93.1 %all-gather.5.cloned.1.call-start = ((), (), s32[]{:S(2)}) async-start(), calls=%async_computation.6 | async-start | bytes 2621440 | tf_op jit(solution)/shard_map/all_gather | solution.py:878
  52.7 127.0 %reduce-scatter.5.cloned.1.call-start = ((), (), s32[]{:S(2)}) async-start(), calls=%async_computation.7 | async-start | bytes 2621440 | tf_op jit(solution)/shard_map/reduce_scatter | solution.py:913
  54.3 24.7 %collective-permute-start.7 = (bf16[2,1024,256]{2,1,0:T(8,128)(2,1)S(1)}, bf16[2,1024,256]{2,1,0:T(8,128)(2,1)S(1)}, u32[]{:S(2)}, u32[]{:S(2)}) collective-permute-start(bf16[2,1024,256]{2,1,0:T(8,128)(2,1)S(1)} %pad_maximum_fusion.1.refs_0_.refs_1_), channel_id=1, source_target_pairs={{0,16},{4,20},{8,24},{12,28},{16,0},{20,4},{24,8},{28,12},{1,17},{... | collective-permute-start | bytes 3145736 | tf_op jit(solution)/shard_map/ppermute | solution.py:552
  57.0 24.5 %collective-permute-start.8 = (bf16[2,1024,256]{2,1,0:T(8,128)(2,1)S(1)}, bf16[2,1024,256]{2,1,0:T(8,128)(2,1)}, u32[]{:S(2)}, u32[]{:S(2)}) collective-permute-start(bf16[2,1024,256]{2,1,0:T(8,128)(2,1)S(1)} %pad_maximum_fusion.2.refs_2_.refs_3_), channel_id=1, source_target_pairs={{0,8},{4,12},{8,0},{12,4},{16,24},{20,28},{24,16},{28,20},{1,9},{5... | collective-permute-start | bytes 3145736 | tf_op jit(solution)/shard_map/ppermute | solution.py:552
  129.4 90.3 %reduce-scatter.7.cloned.1.call-start = ((), (), s32[]{:S(2)}) async-start(), calls=%async_computation.8 | async-start | bytes 2621440 | tf_op jit(solution)/shard_map/reduce_scatter | solution.py:920
  228.0 30.2 %collective-permute-start.14 = (bf16[4,256,2048]{2,1,0:T(8,128)(2,1)}, bf16[4,256,2048]{2,1,0:T(8,128)(2,1)}, u32[]{:S(2)}, u32[]{:S(2)}) collective-permute-start(bf16[4,256,2048]{2,1,0:T(8,128)(2,1)} %get-tuple-element.355), channel_id=1, source_target_pairs={{0,4},{4,0},{8,12},{12,8},{16,20},{20,16},{24,28},{28,24},{1,5},{5... | collective-permute-start | bytes 12582920 | tf_op jit(solution)/shard_map/ppermute | solution.py:552
  228.5 29.7 %all-to-all-start = ((bf16[4,2,128,512]{3,2,1,0:T(8,128)(2,1)}), bf16[4,2,128,512]{3,2,1,0:T(8,128)(2,1)S(1)}, u32[]{:S(2)}, u32[]{:S(2)}) async-start(bf16[4,2,128,512]{3,2,1,0:T(8,128)(2,1)} %get-tuple-element.356), calls=%async_computation.2 | async-start | bytes 2097152 | tf_op jit(solution)/shard_map/all_to_all | solution.py:570
  232.0 126.9 %reduce-scatter.9.cloned.1.call-start = ((), (), s32[]{:S(2)}) async-start(), calls=%async_computation.9 | async-start | bytes 5242880 | tf_op jit(solution)/shard_map/reduce_scatter | solution.py:955
  259.2 167.5 %reduce-scatter.11.cloned.1.call-start = ((), (), s32[]{:S(2)}) async-start(), calls=%async_computation.10 | async-start | bytes 5242880 | tf_op jit(solution)/shard_map/reduce_scatter | solution.py:978
  259.2 26.3 %collective-permute-start.15 = (bf16[2,256,1024]{2,1,0:T(8,128)(2,1)}, bf16[2,256,1024]{2,1,0:T(8,128)(2,1)S(1)}, u32[]{:S(2)}, u32[]{:S(2)}) collective-permute-start(bf16[2,256,1024]{2,1,0:T(8,128)(2,1)} %get-tuple-element.359), channel_id=1, source_target_pairs={{0,8},{4,12},{8,0},{12,4},{16,24},{20,28},{24,16},{28,20},{1,9},{5... | collective-permute-start | bytes 3145736 | tf_op jit(solution)/shard_map/ppermute | solution.py:552
  260.6 24.9 %collective-permute-start.16 = (bf16[2,256,1024]{2,1,0:T(8,128)(2,1)S(1)}, bf16[2,256,1024]{2,1,0:T(8,128)(2,1)S(1)}, u32[]{:S(2)}, u32[]{:S(2)}) collective-permute-start(bf16[2,256,1024]{2,1,0:T(8,128)(2,1)S(1)} %copy-done.35), channel_id=1, source_target_pairs={{0,16},{4,20},{8,24},{12,28},{16,0},{20,4},{24,8},{28,12},{1,17},{... | collective-permute-start | bytes 3145736 | tf_op jit(solution)/shard_map/ppermute | solution.py:552
  285.5 24.5 %collective-permute-start.18 = (bf16[2,256,1024]{2,1,0:T(8,128)(2,1)}, bf16[2,256,1024]{2,1,0:T(8,128)(2,1)S(1)}, u32[]{:S(2)}, u32[]{:S(2)}) collective-permute-start(bf16[2,256,1024]{2,1,0:T(8,128)(2,1)} %get-tuple-element.375), channel_id=1, source_target_pairs={{0,8},{4,12},{8,0},{12,4},{16,24},{20,28},{24,16},{28,20},{1,9},{5... | collective-permute-start | bytes 3145736 | tf_op jit(solution)/shard_map/ppermute | solution.py:552
  286.2 24.3 %collective-permute-start.19 = (bf16[2,256,1024]{2,1,0:T(8,128)(2,1)}, bf16[2,256,1024]{2,1,0:T(8,128)(2,1)}, u32[]{:S(2)}, u32[]{:S(2)}) collective-permute-start(bf16[2,256,1024]{2,1,0:T(8,128)(2,1)} %get-tuple-element.377), channel_id=1, source_target_pairs={{0,16},{4,20},{8,24},{12,28},{16,0},{20,4},{24,8},{28,12},{1,17},{... | collective-permute-start | bytes 3145736 | tf_op jit(solution)/shard_map/ppermute | solution.py:552
  310.4 26.9 %collective-permute-start.21 = (bf16[2,256,1024]{2,1,0:T(8,128)(2,1)}, bf16[2,256,1024]{2,1,0:T(8,128)(2,1)S(1)}, u32[]{:S(2)}, u32[]{:S(2)}) collective-permute-start(bf16[2,256,1024]{2,1,0:T(8,128)(2,1)} %get-tuple-element.405), channel_id=1, source_target_pairs={{0,8},{4,12},{8,0},{12,4},{16,24},{20,28},{24,16},{28,20},{1,9},{5... | collective-permute-start | bytes 3145736 | tf_op jit(solution)/shard_map/ppermute | solution.py:552
  311.9 25.5 %collective-permute-start.22 = (bf16[2,256,1024]{2,1,0:T(8,128)(2,1)}, bf16[2,256,1024]{2,1,0:T(8,128)(2,1)S(1)}, u32[]{:S(2)}, u32[]{:S(2)}) collective-permute-start(bf16[2,256,1024]{2,1,0:T(8,128)(2,1)} %get-tuple-element.407), channel_id=1, source_target_pairs={{0,16},{4,20},{8,24},{12,28},{16,0},{20,4},{24,8},{28,12},{1,17},{... | collective-permute-start | bytes 3145736 | tf_op jit(solution)/shard_map/ppermute | solution.py:552
  342.9 31.5 %collective-permute-start.23 = (bf16[2,256,768]{2,1,0:T(8,128)(2,1)}, bf16[2,256,768]{2,1,0:T(8,128)(2,1)S(1)}, u32[]{:S(2)}, u32[]{:S(2)}) collective-permute-start(bf16[2,256,768]{2,1,0:T(8,128)(2,1)} %get-tuple-element.415), channel_id=1, source_target_pairs={{0,8},{4,12},{8,0},{12,4},{16,24},{20,28},{24,16},{28,20},{1,9},{5... | collective-permute-start | bytes 2359304 | tf_op jit(solution)/shard_map/ppermute | solution.py:552
  343.9 30.6 %collective-permute-start.24 = (bf16[2,256,768]{2,1,0:T(8,128)(2,1)}, bf16[2,256,768]{2,1,0:T(8,128)(2,1)}, u32[]{:S(2)}, u32[]{:S(2)}) collective-permute-start(bf16[2,256,768]{2,1,0:T(8,128)(2,1)} %get-tuple-element.417), channel_id=1, source_target_pairs={{0,16},{4,20},{8,24},{12,28},{16,0},{20,4},{24,8},{28,12},{1,17},{... | collective-permute-start | bytes 2359304 | tf_op jit(solution)/shard_map/ppermute | solution.py:552
  345.2 29.2 %collective-permute-start.25 = (bf16[1,256,1024]{2,1,0:T(8,128)(2,1)}, bf16[1,256,1024]{2,1,0:T(8,128)(2,1)S(1)}, u32[]{:S(2)}, u32[]{:S(2)}) collective-permute-start(bf16[1,256,1024]{2,1,0:T(8,128)(2,1)} %get-tuple-element.419), channel_id=1, source_target_pairs={{0,16},{4,20},{8,24},{12,28},{16,0},{20,4},{24,8},{28,12},{1,17},{... | collective-permute-start | bytes 1572872 | tf_op jit(solution)/shard_map/ppermute | solution.py:552
  346.2 28.3 %collective-permute-start.26 = (bf16[1,256,1024]{2,1,0:T(8,128)(2,1)}, bf16[1,256,1024]{2,1,0:T(8,128)(2,1)}, u32[]{:S(2)}, u32[]{:S(2)}) collective-permute-start(bf16[1,256,1024]{2,1,0:T(8,128)(2,1)} %get-tuple-element.421), channel_id=1, source_target_pairs={{0,8},{4,12},{8,0},{12,4},{16,24},{20,28},{24,16},{28,20},{1,9},{5... | collective-permute-start | bytes 1572872 | tf_op jit(solution)/shard_map/ppermute | solution.py:552
  407.6 23.3 %collective-permute-start.38 = (bf16[512,256]{1,0:T(8,128)(2,1)}, bf16[512,256]{1,0:T(8,128)(2,1)}, u32[]{:S(2)}, u32[]{:S(2)}) collective-permute-start(bf16[512,256]{1,0:T(8,128)(2,1)} %get-tuple-element.493), channel_id=1, source_target_pairs={{0,3},{1,0},{2,1},{3,2},{4,7},{5,4},{6,5},{7,6},{8,11},{9,8},{10,9... | collective-permute-start | bytes 786440 | tf_op jit(solution)/shard_map/ppermute | solution.py:1017
  409.2 28.7 %collective-permute-start.39 = (bf16[512,256]{1,0:T(8,128)(2,1)}, bf16[512,256]{1,0:T(8,128)(2,1)}, u32[]{:S(2)}, u32[]{:S(2)}) collective-permute-start(bf16[512,256]{1,0:T(8,128)(2,1)} %get-tuple-element.494), channel_id=1, source_target_pairs={{0,2},{1,3},{2,0},{3,1},{4,6},{5,7},{6,4},{7,5},{8,10},{9,11},{10,... | collective-permute-start | bytes 786440 | tf_op jit(solution)/shard_map/ppermute | solution.py:1017
  409.2 28.7 %collective-permute-start.40 = (bf16[512,256]{1,0:T(8,128)(2,1)}, bf16[512,256]{1,0:T(8,128)(2,1)}, u32[]{:S(2)}, u32[]{:S(2)}) collective-permute-start(bf16[512,256]{1,0:T(8,128)(2,1)} %get-tuple-element.495), channel_id=1, source_target_pairs={{0,1},{1,2},{2,3},{3,0},{4,5},{5,6},{6,7},{7,4},{8,9},{9,10},{10,1... | collective-permute-start | bytes 786440 | tf_op jit(solution)/shard_map/ppermute | solution.py:1017
  (60 other events, 606.2 us)
Sparse Core Ops, SparseCore 0:
  36.4 46.4 all-gather.2
  84.4 44.8 all-gather.4
  131.6 42.5 reduce-scatter.4
  176.5 43.1 reduce-scatter.6
  258.4 75.9 reduce-scatter.8
  338.6 80.2 reduce-scatter.10

commit v4 on v3

--- a/solution.py
+++ b/solution.py
@@ -91,13 +91,14 @@
         out[t] = trans_times(probs.astype(BF16), value[low:last, :]).astype(BF16)
 
 
-def backward_kernel(size, seg_row, query, key, value, got, *refs):
-    d_query, d_key, d_value, d_attended, key_sum, value_sum = refs
-    groups, parts, part = got.shape[:3]
+def backward_kernel(size, seg_row, query, key, value, *refs):
+    got = refs[:PARTS]
+    d_query, d_key, d_value, d_attended, key_sum, value_sum = refs[PARTS:]
+    groups, part = got[0].shape[:2]
     for t in range(groups):
-        for c in range(parts):
-            start = (t * parts + c) * part
-            d_attended[start : start + part, :] = got[t, c]
+        for c in range(PARTS):
+            start = (t * PARTS + c) * part
+            d_attended[start : start + part, :] = got[c][t]
     seg_col = segment_column(seg_row)
     key_sum[...] = jnp.zeros_like(key_sum)
     value_sum[...] = jnp.zeros_like(value_sum)
@@ -138,7 +139,7 @@
         grid=(query.shape[1] // HEAD_DIM,),
         in_specs=[pl.BlockSpec((1, length), lambda h: (0, 0))]
         + [tall] * 3
-        + [pl.BlockSpec(got.shape[:3] + (HEAD_DIM,), lambda h: (0, 0, 0, h))],
+        + [pl.BlockSpec(g.shape[:2] + (HEAD_DIM,), lambda h: (0, 0, h)) for g in got],
         out_specs=[tall] * 3,
         scratch_shapes=[
             pltpu.VMEM((length, HEAD_DIM), BF16),
@@ -148,7 +149,7 @@
         out_shape=[jax.ShapeDtypeStruct(query.shape, BF16)] * 3,
         compiler_params=pltpu.CompilerParams(vmem_limit_bytes=VMEM),
         cost_estimate=cost(10 * query.shape[0] * length * query.shape[1]),
-    )(segments, query, key, value, got)
+    )(segments, query, key, value, *got)
 
 
 def place_bits(blocks):
@@ -317,9 +318,7 @@
     )(here, heads, wo, x, bo, gain, bias, wup, bup, d_hid, wup)
 
 
-def middle_back_kernel(count, *refs):
-    (terms, mid, cot, gain, wo), before = refs[:5], refs[5 : 5 + count]
-    d_mid, d_branch, sums, d_att = refs[5 + count :]
+def middle_back_kernel(terms, mid, cot, gain, wo, d_mid, d_branch, sums, d_att):
 
     @pl.when(pl.program_id(0) == 0)
     def _():
@@ -336,19 +335,16 @@
         sums[1:2, :] = jnp.sum(d_normed, axis=0, keepdims=True)
         sums[2:3, :] = jnp.sum(low.astype(F32), axis=0, keepdims=True)
 
-    for c in range(count):
-        d_att[c] = before[c][...]
-    d_att[count] = times_trans(d_branch[...], wo[...]).astype(BF16)
-
-
-def middle_back(terms, mid, cot, gain, wo, before):
+    d_att[...] = times_trans(d_branch[...], wo[...]).astype(BF16)
+
+
+def middle_back(terms, mid, cot, gain, wo):
     part, width = mid.shape
     groups = lax.axis_size("tensor")
     block = width // groups
-    count = len(before) + 1
     rows = pl.BlockSpec((part, width), lambda j: (0, 0))
     return pl.pallas_call(
-        functools.partial(middle_back_kernel, len(before)),
+        middle_back_kernel,
         grid=(groups,),
         in_specs=[
             rows,
@@ -356,23 +352,22 @@
             rows,
             pl.BlockSpec((1, width), lambda j: (0, 0)),
             pl.BlockSpec((block, width), lambda j: (j, 0)),
-        ]
-        + [pl.BlockSpec((None, None, part, block), lambda j: (j, 0, 0, 0))] * len(before),
+        ],
         out_specs=[
             rows,
             rows,
             pl.BlockSpec((8, width), lambda j: (0, 0)),
-            pl.BlockSpec((None, count, part, block), lambda j: (j, 0, 0, 0)),
+            pl.BlockSpec((None, part, block), lambda j: (j, 0, 0)),
         ],
         out_shape=[
             jax.ShapeDtypeStruct((part, width), F32),
             jax.ShapeDtypeStruct((part, width), BF16),
             jax.ShapeDtypeStruct((8, width), F32),
-            jax.ShapeDtypeStruct((groups, count, part, block), BF16),
+            jax.ShapeDtypeStruct((groups, part, block), BF16),
         ],
         compiler_params=pltpu.CompilerParams(vmem_limit_bytes=VMEM),
         cost_estimate=cost(2 * part * width * width),
-    )(terms, mid, cot, gain.reshape(1, -1), wo, *before)
+    )(terms, mid, cot, gain.reshape(1, -1), wo)
 
 
 def gradient_terms(lefts, groups, me, blocks):
@@ -921,41 +916,43 @@
     up_terms = gradient_terms(low, [d_up], me, blocks)
     d_mids, d_branches, sums = ([None] * PARTS for _ in range(3))
 
-    def back(c, before):
+    def back(c):
         d_mids[c], d_branches[c], sums[c], d_att = middle_back(
-            terms[c], own_mid[c], cot_own[c * part : (c + 1) * part], norm2_gain, whole, before
+            terms[c], own_mid[c], cot_own[c * part : (c + 1) * part], norm2_gain, whole
         )
         return d_att
 
     terms[0], hidden[0], hidden[1], *up_terms = fence([], (terms[0], *hidden, *up_terms))
-    d_att = back(0, [])
+    d_att = back(0)
     d_att, hidden[0], hidden[1] = fence([], (d_att, *hidden))
     out_terms = both_parts(hidden, down_weight, False, width, groups)
     out_terms, hidden[0], hidden[1] = fence([], (out_terms, *hidden))
     down_terms = gradient_terms(cots, [hidden], me, blocks)
+    d_att, *down_terms = fence([], (d_att, *down_terms))
+    got = [exchange(d_att), None]
     cot_sum = column_sums(cot)
     up_bias_sum = column_sums(d_up[0]) + column_sums(d_up[1])
     up_sum = DpSum(*up_terms, 2)
     down_sum = DpSum(*down_terms, 2)
-    terms[1], out_terms, d_branches[0], cot_sum, up_bias_sum, d_att = fence(
-        [up_sum, down_sum], (terms[1], out_terms, d_branches[0], cot_sum, up_bias_sum, d_att)
-    )
-
-    d_att = back(1, [d_att])
-    d_att, *d_branches = fence([up_sum, down_sum], (d_att, *d_branches))
-    d_att = exchange(d_att)
+    terms[1], out_terms, d_branches[0], cot_sum, up_bias_sum = fence(
+        [up_sum, down_sum], (terms[1], out_terms, d_branches[0], cot_sum, up_bias_sum)
+    )
+
+    d_att = back(1)
+    d_att, got[0], *d_branches = fence([up_sum, down_sum], (d_att, got[0], *d_branches))
+    got[1] = exchange(d_att)
     up_sum.core()
     down_sum.core()
     views = [h.reshape(groups, groups, part, local) for h in heads]
     wo_terms = gradient_terms(d_branches, [[(v, t) for v in views] for t in range(groups)], me, blocks)
     wo_sum = DpSum(*wo_terms, 2)
+    got[1], out_terms = fence([wo_sum, up_sum, down_sum], (got[1], out_terms))
+
+    out_sum = lax.psum_scatter(out_terms, "tensor", scatter_dimension=0)
     up_sum.split()
-    d_att, out_terms = fence([wo_sum, up_sum, down_sum], (d_att, out_terms))
-
-    out_sum = lax.psum_scatter(out_terms, "tensor", scatter_dimension=0)
     up_sum.first(0, 1)
     wo_sum.core()
-    d_query, d_key, d_value = attend_back(segments, query, key, value, d_att)
+    d_query, d_key, d_value = attend_back(segments, query, key, value, got)
     wo_sum.split()
     d_query, d_key, d_value = fence([up_sum, wo_sum, down_sum], (d_query, d_key, d_value))
     wo_sum.first(0, 1)

time: 455 us -> 452 us (level)
  waiting for transfers between devices: 79.4 us -> 72.4 us
    all_to_all x1 -> x2, waiting for transfers between devices: 9.45 us -> 6.28 us  [exchange(): return lax.all_to_all(values, 'tensor', 0, 0)]
  transfers between devices with their start and end apart: 48 -> 49, of which waited for: 20 -> 19; matrix products, arithmetic and copies ran while one was open for 5% -> 5% of each run, Pallas kernels for 61% -> 63%
where the time goes in v4:
time: 452 us; the launch traced here: 444 us
  Pallas kernels  282 us (62%)
  waiting for transfers between devices  72.4 us (16%)
  starting transfers between devices  43.3 us (10%)
  local copies, waits for them, and re-layouts  16.6 us (4%)
  other arithmetic  15 us (3%)
  between operations  15 us (3%)
    pallas_call x2, Pallas kernels, middle_call(): pl.pallas_call(functools.partial(middle_kernel, (first, second)), grid_sp...  55.3 us
    pallas_call x4, Pallas kernels, gradient_terms(): pl.pallas_call(kernel, grid_spec=pltpu.PrefetchScalarGridSpec(num_scalar_...  54.3 us
    ppermute x35, waiting for transfers between devices, swap_bit(): return lax.ppermute(values, axis, [(i, i ^ 1 << bit) for i in range(size)])  48.9 us
    pallas_call x8, Pallas kernels, add_and_split(): pl.pallas_call(kernel, grid=(rows // size,), in_specs=[block(places, v.sh...  40.6 us
    ppermute x35, starting transfers between devices, swap_bit(): return lax.ppermute(values, axis, [(i, i ^ 1 << bit) for i in range(size)])  27.2 us
    pallas_call x2, Pallas kernels, both_parts(): pl.pallas_call(kernel, grid=(columns // block,), in_specs=[left_spec(left...  26.7 us
    pallas_call x1, Pallas kernels, attend_back(): pl.pallas_call(functools.partial(backward_kernel, min(256, length)), grid...  17.3 us
    pallas_call x2, Pallas kernels, middle_back(): pl.pallas_call(middle_back_kernel, grid=(groups,), in_specs=[rows, rows,...  16.7 us
  transfers between devices with their start and end apart: 49, of which 19 were waited for; matrix products, arithmetic and copies ran while one was open for 5% of the time, Pallas kernels for 63%

profile of v4, /device:TPU:0, one launch (start us, length us, event | category | flops | bytes accessed | tf_op | source)
XLA Modules:
  0.0 443.9 jit_solution(4467287619089452386)
XLA Ops:
  14.9 13.4 %shard_map.305 = (bf16[1024,2048]{1,0:T(8,128)(2,1)}, bf16[1024,512]{1,0:T(8,128)(2,1)}, bf16[1024,512]{1,0:T(8,128)(2,1)}, bf16[1024,512]{1,0:T(8,128)(2,1)}) custom-call(bf16[1024,2048]{1,0:T(8,128)(2,1)} %x.3, f32[1,2048]{1,0:T(1,128)} %bitcast.99, f32[1,2048]{1,0:T(1,128)} %bitcast.107, bf16[2048,512]{1,0:T(8,128)(2,1)} %wq.3, f32[1,512]{1,0:T(1,128)} %bitcast.108, ...), custom_call_target="tpu_custom_call" | custom-call | bytes 1024 | tf_op jit(solution)/shard_map/pallas_call | solution.py:193
  28.3 6.2 %shard_map.306 = bf16[4,128,512]{2,1,0:T(8,128)(2,1)} custom-call(s32[1,1024]{1,0:T(1,128)} %seg_row.5, bf16[1024,512]{1,0:T(8,128)(2,1)} %get-tuple-element.275.query, bf16[1024,512]{1,0:T(8,128)(2,1)} %get-tuple-element.276.key, bf16[1024,512]{1,0:T(8,128)(2,1)} %get-tuple-element.277.value), custom_call_target="tpu_custom_call" | custom-call | bytes 1024 | tf_op jit(solution)/shard_map/pallas_call | solution.py:123
  39.9 6.6 %shard_map.307 = bf16[4,128,512]{2,1,0:T(8,128)(2,1)} custom-call(s32[1,1024]{1,0:T(1,128)} %seg_row.5, bf16[1024,512]{1,0:T(8,128)(2,1)} %get-tuple-element.275.query, bf16[1024,512]{1,0:T(8,128)(2,1)} %get-tuple-element.276.key, bf16[1024,512]{1,0:T(8,128)(2,1)} %get-tuple-element.277.value), custom_call_target="tpu_custom_call" | custom-call | bytes 1024 | tf_op jit(solution)/shard_map/pallas_call | solution.py:123
  58.6 13.4 %shard_map.309.d_hid = bf16[2,512,2048]{2,1,0:T(8,128)(2,1)} custom-call(bf16[4,2,128,2048]{3,2,1,0:T(8,128)(2,1)} %bitcast.67, bf16[4,2,128,2048]{3,2,1,0:T(8,128)(2,1)} %bitcast.68, bf16[2048,2048]{1,0:T(8,128)(2,1)} %refs_2_.3), custom_call_target="tpu_custom_call" | custom-call | bytes 1024 | tf_op jit(solution)/shard_map/pallas_call | solution.py:534
  72.1 5.5 %shard_map.308.refs_8_ = bf16[2048,2048]{1,0:T(8,128)(2,1)} custom-call(s32[3]{0:T(128)} %pad_add_fusion.me_ref.here_ref, bf16[2,1024,256]{2,1,0:T(8,128)(2,1)} %copy-done.2, bf16[2,1024,256]{2,1,0:T(8,128)(2,1)} %copy-done.2, bf16[2,1024,256]{2,1,0:T(8,128)(2,1)} %copy-done.3, bf16[2,1024,256]{2,1,0:T(8,128)(2,1)} %copy-done.3, ...), custom_call_target="tpu_custom_call" | custom-call | bytes 1024 | tf_op jit(solution)/shard_map/pallas_call | solution.py:755
  87.5 5.7 %shard_map.310.wo = bf16[2048,2048]{1,0:T(8,128)(2,1)} custom-call(s32[3]{0:T(128)} %pad_add_fusion.me_ref.here_ref, bf16[2,1024,256]{2,1,0:T(8,128)(2,1)} %copy-done.8, bf16[2,1024,256]{2,1,0:T(8,128)(2,1)} %copy-done.8, bf16[2,1024,256]{2,1,0:T(8,128)(2,1)} %collective-permute-done.8.refs_2_.refs_3_, ...), custom_call_target="tpu_custom_call", output_to_operand_aliasing={{}: (9, {})} | custom-call | bytes 1024 | tf_op jit(solution)/shard_map/pallas_call | solution.py:755
  93.2 27.6 %shard_map.311 = (f32[128,2048]{1,0:T(8,128)}, bf16[512,2048]{1,0:T(8,128)(2,1)}, bf16[512,2048]{1,0:T(8,128)(2,1)}, bf16[512,2048]{1,0:T(8,128)(2,1)}, bf16[512,2048]{1,0:T(8,128)(2,1)}) custom-call(s32[3]{0:T(128)} %pad_add_fusion.me_ref.here_ref, bf16[4,512,512]{2,1,0:T(8,128)(2,1)} %all-gather.3.cloned.1.call-done.heads, ...), custom_call_target="tpu_custom_call" | custom-call | bytes 1024 | tf_op jit(solution)/shard_map/pallas_call | solution.py:277
  120.8 8.6 %all-gather.5.cloned.1.call-done.heads = bf16[4,512,512]{2,1,0:T(8,128)(2,1)} async-done(((bf16[1,512,512]{2,1,0:T(8,128)(2,1)}), bf16[4,512,512]{2,1,0:T(8,128)(2,1)}) %all-gather.5.cloned.1.call-update) | async-done | bytes 2097168 | tf_op jit(solution)/shard_map/all_gather | solution.py:873
  131.1 27.7 %shard_map.312 = (f32[128,2048]{1,0:T(8,128)}, bf16[512,2048]{1,0:T(8,128)(2,1)}, bf16[512,2048]{1,0:T(8,128)(2,1)}, bf16[512,2048]{1,0:T(8,128)(2,1)}, bf16[512,2048]{1,0:T(8,128)(2,1)}) custom-call(s32[3]{0:T(128)} %pad_add_fusion.me_ref.here_ref, bf16[4,512,512]{2,1,0:T(8,128)(2,1)} %all-gather.5.cloned.1.call-done.heads, ...), custom_call_target="tpu_custom_call" | custom-call | bytes 1024 | tf_op jit(solution)/shard_map/pallas_call | solution.py:277
  158.9 15.3 %shard_map.313 = (bf16[4,256,2048]{2,1,0:T(8,128)(2,1)}, bf16[4,256,2048]{2,1,0:T(8,128)(2,1)}) custom-call(s32[3]{0:T(128)} %pad_add_fusion.me_ref.here_ref, bf16[512,2048]{1,0:T(8,128)(2,1)} %get-tuple-element.311.refs_0_, bf16[512,2048]{1,0:T(8,128)(2,1)} %get-tuple-element.312.refs_1_, bf16[512,2048]{1,0:T(8,128)(2,1)} %get-tuple-element.313.refs_2_, ...), custom_call_target="tpu_custom_call" | custom-call | bytes 1024 | tf_op jit(solution)/shard_map/pallas_call | solution.py:425
  175.2 8.3 %shard_map.314 = (f32[128,2048]{1,0:T(8,128)}, bf16[128,2048]{1,0:T(8,128)(2,1)}, f32[8,2048]{1,0:T(8,128)}, bf16[4,128,512]{2,1,0:T(8,128)(2,1)}) custom-call(bf16[128,2048]{1,0:T(8,128)(2,1)} %bitcast.94, f32[128,2048]{1,0:T(8,128)} %get-tuple-element.320.mid, bf16[128,2048]{1,0:T(8,128)(2,1)} %get-tuple-element.529.cot, f32[1,2048]{1,0:T(1,128)} %bitcast.97, ...), custom_call_target="tpu_custom_call" | custom-call | bytes 1024 | tf_op jit(solution)/shard_map/pallas_call | solution.py:346
  183.5 13.3 %shard_map.315 = bf16[4,2,128,2048]{3,2,1,0:T(8,128)(2,1)} custom-call(bf16[512,2048]{1,0:T(8,128)(2,1)} %get-tuple-element.328.refs_0_.refs_2_, bf16[512,2048]{1,0:T(8,128)(2,1)} %get-tuple-element.329.refs_1_.refs_3_, bf16[2048,2048]{1,0:T(8,128)(2,1)} %refs_2_.3), custom_call_target="tpu_custom_call" | custom-call | bytes 1024 | tf_op jit(solution)/shard_map/pallas_call | solution.py:534
  196.8 15.2 %shard_map.316 = (bf16[4,256,2048]{2,1,0:T(8,128)(2,1)}, bf16[4,256,2048]{2,1,0:T(8,128)(2,1)}) custom-call(s32[3]{0:T(128)} %pad_add_fusion.me_ref.here_ref, bf16[4,2,128,2048]{3,2,1,0:T(8,128)(2,1)} %bitcast.69, bf16[4,2,128,2048]{3,2,1,0:T(8,128)(2,1)} %bitcast.70, bf16[512,2048]{1,0:T(8,128)(2,1)} %get-tuple-element.328.refs_0_.refs_2_, ...), custom_call_target="tpu_custom_call" | custom-call | bytes 1024 | tf_op jit(solution)/shard_map/pallas_call | solution.py:425
  219.9 8.3 %shard_map.317 = (f32[128,2048]{1,0:T(8,128)}, bf16[128,2048]{1,0:T(8,128)(2,1)}, f32[8,2048]{1,0:T(8,128)}, bf16[4,128,512]{2,1,0:T(8,128)(2,1)}) custom-call(bf16[128,2048]{1,0:T(8,128)(2,1)} %bitcast.93, f32[128,2048]{1,0:T(8,128)} %get-tuple-element.342.mid, bf16[128,2048]{1,0:T(8,128)(2,1)} %get-tuple-element.528.cot, f32[1,2048]{1,0:T(1,128)} %bitcast.98, ...), custom_call_target="tpu_custom_call" | custom-call | bytes 1024 | tf_op jit(solution)/shard_map/pallas_call | solution.py:346
  234.3 10.6 %shard_map.318 = (bf16[4,256,2048]{2,1,0:T(8,128)(2,1)}, bf16[4,256,2048]{2,1,0:T(8,128)(2,1)}) custom-call(s32[3]{0:T(128)} %pad_add_fusion.me_ref.here_ref, bf16[128,2048]{1,0:T(8,128)(2,1)} %get-tuple-element.347.refs_0_, bf16[128,2048]{1,0:T(8,128)(2,1)} %get-tuple-element.348.refs_1_, bf16[4,4,128,512]{3,2,1,0:T(8,128)(2,1)} %bitcast.73, ...), custom_call_target="tpu_custom_call" | custom-call | bytes 1024 | tf_op jit(solution)/shard_map/pallas_call | solution.py:425
  250.1 6.4 %shard_map.319 = (bf16[2,256,1024]{2,1,0:T(8,128)(2,1)}, bf16[2,256,1024]{2,1,0:T(8,128)(2,1)}, bf16[2,256,1024]{2,1,0:T(8,128)(2,1)}, bf16[2,256,1024]{2,1,0:T(8,128)(2,1)}) custom-call(bf16[4,256,2048]{2,1,0:T(8,128)(2,1)} %get-tuple-element.357.refs_0_, bf16[4,256,2048]{2,1,0:T(8,128)(2,1)} %collective-permute-done.13.refs_1_), custom_call_target="tpu_custom_call" | custom-call | bytes 1024 | tf_op jit(solution)/shard_map/pallas_call | solution.py:593
  259.2 17.3 %shard_map.321 = (bf16[1024,512]{1,0:T(8,128)(2,1)}, bf16[1024,512]{1,0:T(8,128)(2,1)}, bf16[1024,512]{1,0:T(8,128)(2,1)}) custom-call(s32[1,1024]{1,0:T(1,128)} %seg_row.5, bf16[1024,512]{1,0:T(8,128)(2,1)} %get-tuple-element.275.query, bf16[1024,512]{1,0:T(8,128)(2,1)} %get-tuple-element.276.key, bf16[1024,512]{1,0:T(8,128)(2,1)} %get-tuple-element.277.value, ...), custom_call_target="tpu_custom_call" | custom-call | bytes 1024 | tf_op jit(solution)/shard_map/pallas_call | solution.py:137
  276.5 6.0 %shard_map.320 = (bf16[2,256,1024]{2,1,0:T(8,128)(2,1)}, bf16[2,256,1024]{2,1,0:T(8,128)(2,1)}, bf16[2,256,1024]{2,1,0:T(8,128)(2,1)}, bf16[2,256,1024]{2,1,0:T(8,128)(2,1)}) custom-call(bf16[4,256,2048]{2,1,0:T(8,128)(2,1)} %get-tuple-element.363.refs_0_, bf16[4,256,2048]{2,1,0:T(8,128)(2,1)} %collective-permute-done.17.refs_1_), custom_call_target="tpu_custom_call" | custom-call | bytes 1024 | tf_op jit(solution)/shard_map/pallas_call | solution.py:593
  284.6 6.1 %shard_map.323 = (bf16[2,256,1024]{2,1,0:T(8,128)(2,1)}, bf16[2,256,1024]{2,1,0:T(8,128)(2,1)}, bf16[2,256,1024]{2,1,0:T(8,128)(2,1)}, bf16[2,256,1024]{2,1,0:T(8,128)(2,1)}) custom-call(bf16[4,256,2048]{2,1,0:T(8,128)(2,1)} %get-tuple-element.386.refs_0_, bf16[4,256,2048]{2,1,0:T(8,128)(2,1)} %collective-permute-done.14.refs_1_), custom_call_target="tpu_custom_call" | custom-call | bytes 1024 | tf_op jit(solution)/shard_map/pallas_call | solution.py:593
  290.7 13.2 %shard_map.322 = (bf16[4,256,1536]{2,1,0:T(8,128)(2,1)}, bf16[4,256,1536]{2,1,0:T(8,128)(2,1)}) custom-call(s32[3]{0:T(128)} %pad_add_fusion.me_ref.here_ref, bf16[1024,2048]{1,0:T(8,128)(2,1)} %get-tuple-element.380.refs_0_, bf16[1024,512]{1,0:T(8,128)(2,1)} %get-tuple-element.437.refs_1_.dq, bf16[1024,512]{1,0:T(8,128)(2,1)} %get-tuple-element.411.refs_2_.dk, ...), custom_call_target="tpu_custom_call" | custom-call | bytes 1024 | tf_op jit(solution)/shard_map/pallas_call | solution.py:425
  309.8 15.3 %shard_map.326 = (bf16[1024,2048]{1,0:T(8,128)(2,1)}, f32[1,2048]{1,0:T(1,128)}, f32[1,2048]{1,0:T(1,128)}) custom-call(bf16[1024,512]{1,0:T(8,128)(2,1)} %get-tuple-element.437.refs_1_.dq, bf16[1024,512]{1,0:T(8,128)(2,1)} %get-tuple-element.411.refs_2_.dk, bf16[1024,512]{1,0:T(8,128)(2,1)} %get-tuple-element.438.refs_3_.dv, bf16[2048,512]{1,0:T(8,128)(2,1)} %wq.3, ...), custom_call_target="tpu_custom_call" | custom-call | bytes 1024 | tf_op jit(solution)/shard_map/pallas_call | solution.py:466
  356.1 15.6 %collective-permute-done.25.refs_1_ = bf16[1,256,1024]{2,1,0:T(8,128)(2,1)S(1)} collective-permute-done((bf16[1,256,1024]{2,1,0:T(8,128)(2,1)}, bf16[1,256,1024]{2,1,0:T(8,128)(2,1)S(1)}, u32[]{:S(2)}, u32[]{:S(2)}) %collective-permute-start.25) | collective-permute-done | bytes 524320 | tf_op jit(solution)/shard_map/ppermute | solution.py:547
  396.2 7.8 %collective-permute-done.33 = f32[1920]{0:T(1024)S(1)} collective-permute-done((f32[1920]{0:T(1024)S(1)}, f32[1920]{0:T(1024)S(1)}, u32[]{:S(2)}, u32[]{:S(2)}) %collective-permute-start.33) | collective-permute-done | bytes 7712 | tf_op jit(solution)/shard_map/ppermute | solution.py:547
  427.9 6.9 %collective-permute-done.39 = bf16[512,256]{1,0:T(8,128)(2,1)} collective-permute-done((bf16[512,256]{1,0:T(8,128)(2,1)}, bf16[512,256]{1,0:T(8,128)(2,1)}, u32[]{:S(2)}, u32[]{:S(2)}) %collective-permute-start.39) | collective-permute-done | bytes 262176 | tf_op jit(solution)/shard_map/ppermute | solution.py:1014
  (239 shorter events, 148.5 us)
Async XLA Ops:
  7.2 85.9 %all-gather.3.cloned.1.call-start = ((), (), s32[]{:S(2)}) async-start(), calls=%async_computation.6 | async-start | bytes 2621440 | tf_op jit(solution)/shard_map/all_gather | solution.py:869
  8.8 25.7 %collective-permute-start.2 = (bf16[512,256]{1,0:T(8,128)(2,1)S(1)}, bf16[512,256]{1,0:T(8,128)(2,1)S(1)}, u32[]{:S(2)}, u32[]{:S(2)}) collective-permute-start(bf16[512,256]{1,0:T(8,128)(2,1)S(1)} %constant_dynamic-slice_fusion.2), channel_id=1, source_target_pairs={{0,3},{1,0},{2,1},{3,2},{4,7},{5,4},{6,5},{7,6},{8,11},{9,8},{10,9... | collective-permute-start | bytes 786440 | tf_op jit(solution)/shard_map/ppermute | solution.py:705
  36.3 93.1 %all-gather.5.cloned.1.call-start = ((), (), s32[]{:S(2)}) async-start(), calls=%async_computation.7 | async-start | bytes 2621440 | tf_op jit(solution)/shard_map/all_gather | solution.py:873
  52.7 122.5 %reduce-scatter.5.cloned.1.call-start = ((), (), s32[]{:S(2)}) async-start(), calls=%async_computation.8 | async-start | bytes 2621440 | tf_op jit(solution)/shard_map/reduce_scatter | solution.py:908
  54.2 24.7 %collective-permute-start.7 = (bf16[2,1024,256]{2,1,0:T(8,128)(2,1)S(1)}, bf16[2,1024,256]{2,1,0:T(8,128)(2,1)S(1)}, u32[]{:S(2)}, u32[]{:S(2)}) collective-permute-start(bf16[2,1024,256]{2,1,0:T(8,128)(2,1)S(1)} %pad_maximum_fusion.1.refs_0_.refs_1_), channel_id=1, source_target_pairs={{0,16},{4,20},{8,24},{12,28},{16,0},{20,4},{24,8},{28,12},{1,17},{... | collective-permute-start | bytes 3145736 | tf_op jit(solution)/shard_map/ppermute | solution.py:547
  56.9 24.5 %collective-permute-start.8 = (bf16[2,1024,256]{2,1,0:T(8,128)(2,1)S(1)}, bf16[2,1024,256]{2,1,0:T(8,128)(2,1)}, u32[]{:S(2)}, u32[]{:S(2)}) collective-permute-start(bf16[2,1024,256]{2,1,0:T(8,128)(2,1)S(1)} %pad_maximum_fusion.2.refs_2_.refs_3_), channel_id=1, source_target_pairs={{0,8},{4,12},{8,0},{12,4},{16,24},{20,28},{24,16},{28,20},{1,9},{5... | collective-permute-start | bytes 3145736 | tf_op jit(solution)/shard_map/ppermute | solution.py:547
  129.4 90.5 %reduce-scatter.7.cloned.1.call-start = ((), (), s32[]{:S(2)}) async-start(), calls=%async_computation.9 | async-start | bytes 2621440 | tf_op jit(solution)/shard_map/reduce_scatter | solution.py:915
  234.3 121.8 %reduce-scatter.9.cloned.1.call-start = ((), (), s32[]{:S(2)}) async-start(), calls=%async_computation.10 | async-start | bytes 5242880 | tf_op jit(solution)/shard_map/reduce_scatter | solution.py:951
  249.2 27.3 %collective-permute-start.17 = (bf16[4,256,2048]{2,1,0:T(8,128)(2,1)}, bf16[4,256,2048]{2,1,0:T(8,128)(2,1)}, u32[]{:S(2)}, u32[]{:S(2)}) collective-permute-start(bf16[4,256,2048]{2,1,0:T(8,128)(2,1)} %get-tuple-element.364), channel_id=1, source_target_pairs={{0,4},{4,0},{8,12},{12,8},{16,20},{20,16},{24,28},{28,24},{1,5},{5... | collective-permute-start | bytes 12582920 | tf_op jit(solution)/shard_map/ppermute | solution.py:547
  250.0 173.8 %reduce-scatter.11.cloned.1.call-start = ((), (), s32[]{:S(2)}) async-start(), calls=%async_computation.11 | async-start | bytes 5242880 | tf_op jit(solution)/shard_map/reduce_scatter | solution.py:975
  256.6 25.9 %collective-permute-start.15 = (bf16[2,256,1024]{2,1,0:T(8,128)(2,1)}, bf16[2,256,1024]{2,1,0:T(8,128)(2,1)S(1)}, u32[]{:S(2)}, u32[]{:S(2)}) collective-permute-start(bf16[2,256,1024]{2,1,0:T(8,128)(2,1)} %get-tuple-element.360), channel_id=1, source_target_pairs={{0,8},{4,12},{8,0},{12,4},{16,24},{20,28},{24,16},{28,20},{1,9},{5... | collective-permute-start | bytes 3145736 | tf_op jit(solution)/shard_map/ppermute | solution.py:547
  257.7 24.8 %collective-permute-start.16 = (bf16[2,256,1024]{2,1,0:T(8,128)(2,1)}, bf16[2,256,1024]{2,1,0:T(8,128)(2,1)S(1)}, u32[]{:S(2)}, u32[]{:S(2)}) collective-permute-start(bf16[2,256,1024]{2,1,0:T(8,128)(2,1)} %get-tuple-element.362), channel_id=1, source_target_pairs={{0,16},{4,20},{8,24},{12,28},{16,0},{20,4},{24,8},{28,12},{1,17},{... | collective-permute-start | bytes 3145736 | tf_op jit(solution)/shard_map/ppermute | solution.py:547
  282.5 24.6 %collective-permute-start.18 = (bf16[2,256,1024]{2,1,0:T(8,128)(2,1)}, bf16[2,256,1024]{2,1,0:T(8,128)(2,1)S(1)}, u32[]{:S(2)}, u32[]{:S(2)}) collective-permute-start(bf16[2,256,1024]{2,1,0:T(8,128)(2,1)} %get-tuple-element.377), channel_id=1, source_target_pairs={{0,8},{4,12},{8,0},{12,4},{16,24},{20,28},{24,16},{28,20},{1,9},{5... | collective-permute-start | bytes 3145736 | tf_op jit(solution)/shard_map/ppermute | solution.py:547
  283.2 24.4 %collective-permute-start.19 = (bf16[2,256,1024]{2,1,0:T(8,128)(2,1)}, bf16[2,256,1024]{2,1,0:T(8,128)(2,1)}, u32[]{:S(2)}, u32[]{:S(2)}) collective-permute-start(bf16[2,256,1024]{2,1,0:T(8,128)(2,1)} %get-tuple-element.379), channel_id=1, source_target_pairs={{0,16},{4,20},{8,24},{12,28},{16,0},{20,4},{24,8},{28,12},{1,17},{... | collective-permute-start | bytes 3145736 | tf_op jit(solution)/shard_map/ppermute | solution.py:547
  307.5 27.2 %collective-permute-start.21 = (bf16[2,256,1024]{2,1,0:T(8,128)(2,1)}, bf16[2,256,1024]{2,1,0:T(8,128)(2,1)S(1)}, u32[]{:S(2)}, u32[]{:S(2)}) collective-permute-start(bf16[2,256,1024]{2,1,0:T(8,128)(2,1)} %get-tuple-element.407), channel_id=1, source_target_pairs={{0,8},{4,12},{8,0},{12,4},{16,24},{20,28},{24,16},{28,20},{1,9},{5... | collective-permute-start | bytes 3145736 | tf_op jit(solution)/shard_map/ppermute | solution.py:547
  309.0 25.8 %collective-permute-start.22 = (bf16[2,256,1024]{2,1,0:T(8,128)(2,1)}, bf16[2,256,1024]{2,1,0:T(8,128)(2,1)S(1)}, u32[]{:S(2)}, u32[]{:S(2)}) collective-permute-start(bf16[2,256,1024]{2,1,0:T(8,128)(2,1)} %get-tuple-element.409), channel_id=1, source_target_pairs={{0,16},{4,20},{8,24},{12,28},{16,0},{20,4},{24,8},{28,12},{1,17},{... | collective-permute-start | bytes 3145736 | tf_op jit(solution)/shard_map/ppermute | solution.py:547
  340.4 31.3 %collective-permute-start.23 = (bf16[2,256,768]{2,1,0:T(8,128)(2,1)}, bf16[2,256,768]{2,1,0:T(8,128)(2,1)S(1)}, u32[]{:S(2)}, u32[]{:S(2)}) collective-permute-start(bf16[2,256,768]{2,1,0:T(8,128)(2,1)} %get-tuple-element.417), channel_id=1, source_target_pairs={{0,8},{4,12},{8,0},{12,4},{16,24},{20,28},{24,16},{28,20},{1,9},{5... | collective-permute-start | bytes 2359304 | tf_op jit(solution)/shard_map/ppermute | solution.py:547
  341.1 30.6 %collective-permute-start.24 = (bf16[2,256,768]{2,1,0:T(8,128)(2,1)}, bf16[2,256,768]{2,1,0:T(8,128)(2,1)}, u32[]{:S(2)}, u32[]{:S(2)}) collective-permute-start(bf16[2,256,768]{2,1,0:T(8,128)(2,1)} %get-tuple-element.419), channel_id=1, source_target_pairs={{0,16},{4,20},{8,24},{12,28},{16,0},{20,4},{24,8},{28,12},{1,17},{... | collective-permute-start | bytes 2359304 | tf_op jit(solution)/shard_map/ppermute | solution.py:547
  342.4 29.3 %collective-permute-start.25 = (bf16[1,256,1024]{2,1,0:T(8,128)(2,1)}, bf16[1,256,1024]{2,1,0:T(8,128)(2,1)S(1)}, u32[]{:S(2)}, u32[]{:S(2)}) collective-permute-start(bf16[1,256,1024]{2,1,0:T(8,128)(2,1)} %get-tuple-element.421), channel_id=1, source_target_pairs={{0,16},{4,20},{8,24},{12,28},{16,0},{20,4},{24,8},{28,12},{1,17},{... | collective-permute-start | bytes 1572872 | tf_op jit(solution)/shard_map/ppermute | solution.py:547
  343.4 28.3 %collective-permute-start.26 = (bf16[1,256,1024]{2,1,0:T(8,128)(2,1)}, bf16[1,256,1024]{2,1,0:T(8,128)(2,1)}, u32[]{:S(2)}, u32[]{:S(2)}) collective-permute-start(bf16[1,256,1024]{2,1,0:T(8,128)(2,1)} %get-tuple-element.423), channel_id=1, source_target_pairs={{0,8},{4,12},{8,0},{12,4},{16,24},{20,28},{24,16},{28,20},{1,9},{5... | collective-permute-start | bytes 1572872 | tf_op jit(solution)/shard_map/ppermute | solution.py:547
  381.5 22.5 %collective-permute-start.29 = (bf16[1,256,768]{2,1,0:T(8,128)(2,1)}, bf16[1,256,768]{2,1,0:T(8,128)(2,1)S(1)}, u32[]{:S(2)}, u32[]{:S(2)}) collective-permute-start(bf16[1,256,768]{2,1,0:T(8,128)(2,1)} %get-tuple-element.450), channel_id=1, source_target_pairs={{0,16},{4,20},{8,24},{12,28},{16,0},{20,4},{24,8},{28,12},{1,17},{... | collective-permute-start | bytes 1179656 | tf_op jit(solution)/shard_map/ppermute | solution.py:547
  404.8 23.2 %collective-permute-start.38 = (bf16[512,256]{1,0:T(8,128)(2,1)}, bf16[512,256]{1,0:T(8,128)(2,1)}, u32[]{:S(2)}, u32[]{:S(2)}) collective-permute-start(bf16[512,256]{1,0:T(8,128)(2,1)} %get-tuple-element.495), channel_id=1, source_target_pairs={{0,3},{1,0},{2,1},{3,2},{4,7},{5,4},{6,5},{7,6},{8,11},{9,8},{10,9... | collective-permute-start | bytes 786440 | tf_op jit(solution)/shard_map/ppermute | solution.py:1014
  406.3 28.5 %collective-permute-start.39 = (bf16[512,256]{1,0:T(8,128)(2,1)}, bf16[512,256]{1,0:T(8,128)(2,1)}, u32[]{:S(2)}, u32[]{:S(2)}) collective-permute-start(bf16[512,256]{1,0:T(8,128)(2,1)} %get-tuple-element.496), channel_id=1, source_target_pairs={{0,2},{1,3},{2,0},{3,1},{4,6},{5,7},{6,4},{7,5},{8,10},{9,11},{10,... | collective-permute-start | bytes 786440 | tf_op jit(solution)/shard_map/ppermute | solution.py:1014
  406.3 28.5 %collective-permute-start.40 = (bf16[512,256]{1,0:T(8,128)(2,1)}, bf16[512,256]{1,0:T(8,128)(2,1)}, u32[]{:S(2)}, u32[]{:S(2)}) collective-permute-start(bf16[512,256]{1,0:T(8,128)(2,1)} %get-tuple-element.497), channel_id=1, source_target_pairs={{0,1},{1,2},{2,3},{3,0},{4,5},{5,6},{6,7},{7,4},{8,9},{9,10},{10,1... | collective-permute-start | bytes 786440 | tf_op jit(solution)/shard_map/ppermute | solution.py:1014
  (61 other events, 636.2 us)
Sparse Core Ops, SparseCore 0:
  36.4 46.4 all-gather.2
  84.4 44.8 all-gather.4
  131.6 42.5 reduce-scatter.4
  176.5 43.1 reduce-scatter.6
  249.4 75.9 reduce-scatter.8
  336.0 80.2 reduce-scatter.10

commit v5 on v4

--- a/solution.py
+++ b/solution.py
@@ -568,7 +568,7 @@
 def add_and_split(sources, outs, dims):
     places = 2**dims
     rows = sources[0][0].shape[1]
-    size = min(64, rows)
+    size = min(128, rows)
     widths = [sum(stop - start for _, start, stop in picks) for picks, _ in outs]
 
     def kernel(*refs):
@@ -933,7 +933,7 @@
     cot_sum = column_sums(cot)
     up_bias_sum = column_sums(d_up[0]) + column_sums(d_up[1])
     up_sum = DpSum(*up_terms, 2)
-    down_sum = DpSum(*down_terms, 2)
+    down_sum = DpSum(*down_terms, 4)
     terms[1], out_terms, d_branches[0], cot_sum, up_bias_sum = fence(
         [up_sum, down_sum], (terms[1], out_terms, d_branches[0], cot_sum, up_bias_sum)
     )
@@ -962,18 +962,22 @@
     down_sum.split()
     d_query, d_key, d_value = fence([wo_sum, qkv_sum, down_sum], (d_query, d_key, d_value))
     qkv_sum.core()
-    down_sum.first(0, 1)
+    down_sum.first(0, 3)
     terms_in, gain1, bias1 = normed_back(
         d_query, d_key, d_value, query_weight, key_weight, value_weight, inputs
     )
+    gain1, bias1, terms_in, d_query, d_value = fence(
+        [qkv_sum, wo_sum, down_sum], (gain1, bias1, terms_in, d_query, d_value)
+    )
+
+    d_normed = lax.psum_scatter(
+        terms_in.reshape(groups, share, width), "tensor", scatter_dimension=0
+    )
+    down_sum.first(1, 2)
     qkv_sum.split()
     wo_sum.add()
-    gain1, bias1, terms_in, d_query, d_value = fence(
-        [qkv_sum, wo_sum, down_sum], (gain1, bias1, terms_in, d_query, d_value)
-    )
-
-    d_normed = lax.psum_scatter(
-        terms_in.reshape(groups, share, width), "tensor", scatter_dimension=0
+    gain1, bias1, d_query, d_value = fence(
+        [qkv_sum, wo_sum, down_sum], (gain1, bias1, d_query, d_value)
     )
     qkv_sum.first(0, 1)
     wo_sum.send()

time: 452 us -> 446 us (0.987)
  Pallas kernels: 282 us -> 275 us
    pallas_call x8, Pallas kernels: 40.6 us -> 33.6 us  [add_and_split(): pl.pallas_call(kernel, grid=(rows // size,), in_specs=[block(places, v.sh...]
    ppermute x35 -> x37, waiting for transfers between devices: 48.9 us -> 55.7 us  [swap_bit(): return lax.ppermute(values, axis, [(i, i ^ 1 << bit) for i in range(size)])]
    ppermute x3, waiting for transfers between devices: 6.86 us -> 0.01 us  [on_device(): wo_got.append(lax.ppermute(to_all[m], 'tensor', ring))]
    ppermute x35 -> x37, starting transfers between devices: 27.2 us -> 29.1 us  [swap_bit(): return lax.ppermute(values, axis, [(i, i ^ 1 << bit) for i in range(size)])]
  transfers between devices with their start and end apart: 49 -> 51, of which waited for: 19 -> 22; matrix products, arithmetic and copies ran while one was open for 5% -> 5% of each run, Pallas kernels for 63% -> 63%
where the time goes in v5:
time: 446 us; the launch traced here: 438 us
  Pallas kernels  275 us (62%)
  waiting for transfers between devices  72.5 us (16%)
  starting transfers between devices  45.3 us (10%)
  local copies, waits for them, and re-layouts  15.5 us (3%)
  between operations  15.1 us (3%)
  other arithmetic  14.9 us (3%)
    ppermute x37, waiting for transfers between devices, swap_bit(): return lax.ppermute(values, axis, [(i, i ^ 1 << bit) for i in range(size)])  55.7 us
    pallas_call x2, Pallas kernels, middle_call(): pl.pallas_call(functools.partial(middle_kernel, (first, second)), grid_sp...  55.3 us
    pallas_call x4, Pallas kernels, gradient_terms(): pl.pallas_call(kernel, grid_spec=pltpu.PrefetchScalarGridSpec(num_scalar_...  54.4 us
    pallas_call x8, Pallas kernels, add_and_split(): pl.pallas_call(kernel, grid=(rows // size,), in_specs=[block(places, v.sh...  33.6 us
    ppermute x37, starting transfers between devices, swap_bit(): return lax.ppermute(values, axis, [(i, i ^ 1 << bit) for i in range(size)])  29.1 us
    pallas_call x2, Pallas kernels, both_parts(): pl.pallas_call(kernel, grid=(columns // block,), in_specs=[left_spec(left...  26.7 us
    pallas_call x1, Pallas kernels, attend_back(): pl.pallas_call(functools.partial(backward_kernel, min(256, length)), grid...  17.3 us
    pallas_call x2, Pallas kernels, middle_back(): pl.pallas_call(middle_back_kernel, grid=(groups,), in_specs=[rows, rows,...  16.7 us
  transfers between devices with their start and end apart: 51, of which 22 were waited for; matrix products, arithmetic and copies ran while one was open for 5% of the time, Pallas kernels for 63%

profile of v5, /device:TPU:0, one launch (start us, length us, event | category | flops | bytes accessed | tf_op | source)
XLA Modules:
  0.0 437.9 jit_solution(17082957027438398849)
XLA Ops:
  8.8 5.1 %collective-permute-start.2 = (bf16[512,256]{1,0:T(8,128)(2,1)S(1)}, bf16[512,256]{1,0:T(8,128)(2,1)S(1)}, u32[]{:S(2)}, u32[]{:S(2)}) collective-permute-start(bf16[512,256]{1,0:T(8,128)(2,1)S(1)} %constant_dynamic-slice_fusion.2), channel_id=1, source_target_pairs={{0,3},{1,0},{2,1},{3,2},{4,7},{5,4},{6,5},{7,6},{8,11},{9,8},{10,9... | collective-permute-start | bytes 786440 | tf_op jit(solution)/shard_map/ppermute | solution.py:705
  14.9 13.4 %shard_map.305 = (bf16[1024,2048]{1,0:T(8,128)(2,1)}, bf16[1024,512]{1,0:T(8,128)(2,1)}, bf16[1024,512]{1,0:T(8,128)(2,1)}, bf16[1024,512]{1,0:T(8,128)(2,1)}) custom-call(bf16[1024,2048]{1,0:T(8,128)(2,1)} %x.3, f32[1,2048]{1,0:T(1,128)} %bitcast.99, f32[1,2048]{1,0:T(1,128)} %bitcast.107, bf16[2048,512]{1,0:T(8,128)(2,1)} %wq.3, f32[1,512]{1,0:T(1,128)} %bitcast.108, ...), custom_call_target="tpu_custom_call" | custom-call | bytes 1024 | tf_op jit(solution)/shard_map/pallas_call | solution.py:193
  28.3 6.2 %shard_map.306 = bf16[4,128,512]{2,1,0:T(8,128)(2,1)} custom-call(s32[1,1024]{1,0:T(1,128)} %seg_row.5, bf16[1024,512]{1,0:T(8,128)(2,1)} %get-tuple-element.305.query, bf16[1024,512]{1,0:T(8,128)(2,1)} %get-tuple-element.306.key, bf16[1024,512]{1,0:T(8,128)(2,1)} %get-tuple-element.307.value), custom_call_target="tpu_custom_call" | custom-call | bytes 1024 | tf_op jit(solution)/shard_map/pallas_call | solution.py:123
  39.9 6.6 %shard_map.307 = bf16[4,128,512]{2,1,0:T(8,128)(2,1)} custom-call(s32[1,1024]{1,0:T(1,128)} %seg_row.5, bf16[1024,512]{1,0:T(8,128)(2,1)} %get-tuple-element.305.query, bf16[1024,512]{1,0:T(8,128)(2,1)} %get-tuple-element.306.key, bf16[1024,512]{1,0:T(8,128)(2,1)} %get-tuple-element.307.value), custom_call_target="tpu_custom_call" | custom-call | bytes 1024 | tf_op jit(solution)/shard_map/pallas_call | solution.py:123
  58.6 13.4 %shard_map.309.d_hid = bf16[2,512,2048]{2,1,0:T(8,128)(2,1)} custom-call(bf16[4,2,128,2048]{3,2,1,0:T(8,128)(2,1)} %bitcast.67, bf16[4,2,128,2048]{3,2,1,0:T(8,128)(2,1)} %bitcast.68, bf16[2048,2048]{1,0:T(8,128)(2,1)} %refs_2_.3), custom_call_target="tpu_custom_call" | custom-call | bytes 1024 | tf_op jit(solution)/shard_map/pallas_call | solution.py:534
  72.1 5.5 %shard_map.308.refs_8_ = bf16[2048,2048]{1,0:T(8,128)(2,1)} custom-call(s32[3]{0:T(128)} %pad_add_fusion.me_ref.here_ref, bf16[2,1024,256]{2,1,0:T(8,128)(2,1)} %copy-done.2, bf16[2,1024,256]{2,1,0:T(8,128)(2,1)} %copy-done.2, bf16[2,1024,256]{2,1,0:T(8,128)(2,1)} %copy-done.3, bf16[2,1024,256]{2,1,0:T(8,128)(2,1)} %copy-done.3, ...), custom_call_target="tpu_custom_call" | custom-call | bytes 1024 | tf_op jit(solution)/shard_map/pallas_call | solution.py:755
  87.5 5.7 %shard_map.310.wo = bf16[2048,2048]{1,0:T(8,128)(2,1)} custom-call(s32[3]{0:T(128)} %pad_add_fusion.me_ref.here_ref, bf16[2,1024,256]{2,1,0:T(8,128)(2,1)} %copy-done.8, bf16[2,1024,256]{2,1,0:T(8,128)(2,1)} %copy-done.8, bf16[2,1024,256]{2,1,0:T(8,128)(2,1)} %collective-permute-done.8.refs_2_.refs_3_, ...), custom_call_target="tpu_custom_call", output_to_operand_aliasing={{}: (9, {})} | custom-call | bytes 1024 | tf_op jit(solution)/shard_map/pallas_call | solution.py:755
  93.2 27.6 %shard_map.311 = (f32[128,2048]{1,0:T(8,128)}, bf16[512,2048]{1,0:T(8,128)(2,1)}, bf16[512,2048]{1,0:T(8,128)(2,1)}, bf16[512,2048]{1,0:T(8,128)(2,1)}, bf16[512,2048]{1,0:T(8,128)(2,1)}) custom-call(s32[3]{0:T(128)} %pad_add_fusion.me_ref.here_ref, bf16[4,512,512]{2,1,0:T(8,128)(2,1)} %all-gather.3.cloned.1.call-done.heads, ...), custom_call_target="tpu_custom_call" | custom-call | bytes 1024 | tf_op jit(solution)/shard_map/pallas_call | solution.py:277
  120.8 8.6 %all-gather.5.cloned.1.call-done.heads = bf16[4,512,512]{2,1,0:T(8,128)(2,1)} async-done(((bf16[1,512,512]{2,1,0:T(8,128)(2,1)}), bf16[4,512,512]{2,1,0:T(8,128)(2,1)}) %all-gather.5.cloned.1.call-update) | async-done | bytes 2097168 | tf_op jit(solution)/shard_map/all_gather | solution.py:873
  131.1 27.7 %shard_map.312 = (f32[128,2048]{1,0:T(8,128)}, bf16[512,2048]{1,0:T(8,128)(2,1)}, bf16[512,2048]{1,0:T(8,128)(2,1)}, bf16[512,2048]{1,0:T(8,128)(2,1)}, bf16[512,2048]{1,0:T(8,128)(2,1)}) custom-call(s32[3]{0:T(128)} %pad_add_fusion.me_ref.here_ref, bf16[4,512,512]{2,1,0:T(8,128)(2,1)} %all-gather.5.cloned.1.call-done.heads, ...), custom_call_target="tpu_custom_call" | custom-call | bytes 1024 | tf_op jit(solution)/shard_map/pallas_call | solution.py:277
  158.9 15.3 %shard_map.313 = (bf16[4,256,2048]{2,1,0:T(8,128)(2,1)}, bf16[4,256,2048]{2,1,0:T(8,128)(2,1)}) custom-call(s32[3]{0:T(128)} %pad_add_fusion.me_ref.here_ref, bf16[512,2048]{1,0:T(8,128)(2,1)} %get-tuple-element.341.refs_0_, bf16[512,2048]{1,0:T(8,128)(2,1)} %get-tuple-element.342.refs_1_, bf16[512,2048]{1,0:T(8,128)(2,1)} %get-tuple-element.343.refs_2_, ...), custom_call_target="tpu_custom_call" | custom-call | bytes 1024 | tf_op jit(solution)/shard_map/pallas_call | solution.py:425
  175.2 8.3 %shard_map.314 = (f32[128,2048]{1,0:T(8,128)}, bf16[128,2048]{1,0:T(8,128)(2,1)}, f32[8,2048]{1,0:T(8,128)}, bf16[4,128,512]{2,1,0:T(8,128)(2,1)}) custom-call(bf16[128,2048]{1,0:T(8,128)(2,1)} %bitcast.94, f32[128,2048]{1,0:T(8,128)} %get-tuple-element.350.mid, bf16[128,2048]{1,0:T(8,128)(2,1)} %get-tuple-element.589.cot, f32[1,2048]{1,0:T(1,128)} %bitcast.97, ...), custom_call_target="tpu_custom_call" | custom-call | bytes 1024 | tf_op jit(solution)/shard_map/pallas_call | solution.py:346
  183.6 13.3 %shard_map.315 = bf16[4,2,128,2048]{3,2,1,0:T(8,128)(2,1)} custom-call(bf16[512,2048]{1,0:T(8,128)(2,1)} %get-tuple-element.358.refs_0_.refs_2_, bf16[512,2048]{1,0:T(8,128)(2,1)} %get-tuple-element.359.refs_1_.refs_3_, bf16[2048,2048]{1,0:T(8,128)(2,1)} %refs_2_.3), custom_call_target="tpu_custom_call" | custom-call | bytes 1024 | tf_op jit(solution)/shard_map/pallas_call | solution.py:534
  196.8 15.2 %shard_map.316 = (bf16[4,256,2048]{2,1,0:T(8,128)(2,1)}, bf16[4,256,2048]{2,1,0:T(8,128)(2,1)}) custom-call(s32[3]{0:T(128)} %pad_add_fusion.me_ref.here_ref, bf16[4,2,128,2048]{3,2,1,0:T(8,128)(2,1)} %bitcast.69, bf16[4,2,128,2048]{3,2,1,0:T(8,128)(2,1)} %bitcast.70, bf16[512,2048]{1,0:T(8,128)(2,1)} %get-tuple-element.358.refs_0_.refs_2_, ...), custom_call_target="tpu_custom_call" | custom-call | bytes 1024 | tf_op jit(solution)/shard_map/pallas_call | solution.py:425
  219.9 8.3 %shard_map.317 = (f32[128,2048]{1,0:T(8,128)}, bf16[128,2048]{1,0:T(8,128)(2,1)}, f32[8,2048]{1,0:T(8,128)}, bf16[4,128,512]{2,1,0:T(8,128)(2,1)}) custom-call(bf16[128,2048]{1,0:T(8,128)(2,1)} %bitcast.93, f32[128,2048]{1,0:T(8,128)} %get-tuple-element.372.mid, bf16[128,2048]{1,0:T(8,128)(2,1)} %get-tuple-element.588.cot, f32[1,2048]{1,0:T(1,128)} %bitcast.98, ...), custom_call_target="tpu_custom_call" | custom-call | bytes 1024 | tf_op jit(solution)/shard_map/pallas_call | solution.py:346
  234.3 10.6 %shard_map.318 = (bf16[4,256,2048]{2,1,0:T(8,128)(2,1)}, bf16[4,256,2048]{2,1,0:T(8,128)(2,1)}) custom-call(s32[3]{0:T(128)} %pad_add_fusion.me_ref.here_ref, bf16[128,2048]{1,0:T(8,128)(2,1)} %get-tuple-element.377.refs_0_, bf16[128,2048]{1,0:T(8,128)(2,1)} %get-tuple-element.378.refs_1_, bf16[4,4,128,512]{3,2,1,0:T(8,128)(2,1)} %bitcast.73, ...), custom_call_target="tpu_custom_call" | custom-call | bytes 1024 | tf_op jit(solution)/shard_map/pallas_call | solution.py:425
  250.1 5.3 %shard_map.319 = (bf16[2,256,1024]{2,1,0:T(8,128)(2,1)}, bf16[2,256,1024]{2,1,0:T(8,128)(2,1)}, bf16[2,256,1024]{2,1,0:T(8,128)(2,1)}, bf16[2,256,1024]{2,1,0:T(8,128)(2,1)}) custom-call(bf16[4,256,2048]{2,1,0:T(8,128)(2,1)} %get-tuple-element.387.refs_0_, bf16[4,256,2048]{2,1,0:T(8,128)(2,1)} %collective-permute-done.13.refs_1_), custom_call_target="tpu_custom_call" | custom-call | bytes 1024 | tf_op jit(solution)/shard_map/pallas_call | solution.py:593
  258.4 17.3 %shard_map.321 = (bf16[1024,512]{1,0:T(8,128)(2,1)}, bf16[1024,512]{1,0:T(8,128)(2,1)}, bf16[1024,512]{1,0:T(8,128)(2,1)}) custom-call(s32[1,1024]{1,0:T(1,128)} %seg_row.5, bf16[1024,512]{1,0:T(8,128)(2,1)} %get-tuple-element.305.query, bf16[1024,512]{1,0:T(8,128)(2,1)} %get-tuple-element.306.key, bf16[1024,512]{1,0:T(8,128)(2,1)} %get-tuple-element.307.value, ...), custom_call_target="tpu_custom_call" | custom-call | bytes 1024 | tf_op jit(solution)/shard_map/pallas_call | solution.py:137
  275.7 5.3 %shard_map.320 = (bf16[2,256,1024]{2,1,0:T(8,128)(2,1)}, bf16[2,256,1024]{2,1,0:T(8,128)(2,1)}, bf16[2,256,1024]{2,1,0:T(8,128)(2,1)}, bf16[2,256,1024]{2,1,0:T(8,128)(2,1)}) custom-call(bf16[4,256,2048]{2,1,0:T(8,128)(2,1)} %get-tuple-element.393.refs_0_, bf16[4,256,2048]{2,1,0:T(8,128)(2,1)} %collective-permute-done.17.refs_1_), custom_call_target="tpu_custom_call" | custom-call | bytes 1024 | tf_op jit(solution)/shard_map/pallas_call | solution.py:593
  283.8 5.3 %shard_map.323 = (bf16[2,256,512]{2,1,0:T(8,128)(2,1)}, bf16[2,256,512]{2,1,0:T(8,128)(2,1)}, bf16[2,256,512]{2,1,0:T(8,128)(2,1)}, bf16[2,256,512]{2,1,0:T(8,12...) custom-call(bf16[4,256,2048]{2,1,0:T(8,128)(2,1)} %get-tuple-element, ...), custom_call_target="tpu_custom_call" | custom-call | bytes 1024 | tf_op jit(solution)/shard_map/pallas_call | solution.py:593
  289.1 13.3 %shard_map.322 = (bf16[4,256,1536]{2,1,0:T(8,128)(2,1)}, bf16[4,256,1536]{2,1,0:T(8,128)(2,1)}) custom-call(s32[3]{0:T(128)} %pad_add_fusion.me_ref.here_ref, bf16[1024,2048]{1,0:T(8,128)(2,1)} %get-tuple-element.410.refs_0_, bf16[1024,512]{1,0:T(8,128)(2,1)} %get-tuple-element.497.refs_1_.dq, bf16[1024,512]{1,0:T(8,128)(2,1)} %get-tuple-element.441.refs_2_.dk, ...), custom_call_target="tpu_custom_call" | custom-call | bytes 1024 | tf_op jit(solution)/shard_map/pallas_call | solution.py:425
  309.1 15.3 %shard_map.324 = (bf16[1024,2048]{1,0:T(8,128)(2,1)}, f32[1,2048]{1,0:T(1,128)}, f32[1,2048]{1,0:T(1,128)}) custom-call(bf16[1024,512]{1,0:T(8,128)(2,1)} %get-tuple-element.497.refs_1_.dq, bf16[1024,512]{1,0:T(8,128)(2,1)} %get-tuple-element.441.refs_2_.dk, bf16[1024,512]{1,0:T(8,128)(2,1)} %get-tuple-element.498.refs_3_.dv, bf16[2048,512]{1,0:T(8,128)(2,1)} %wq.3, ...), custom_call_target="tpu_custom_call" | custom-call | bytes 1024 | tf_op jit(solution)/shard_map/pallas_call | solution.py:466
  356.6 16.8 %collective-permute-done.27.refs_1_ = bf16[1,256,1024]{2,1,0:T(8,128)(2,1)} collective-permute-done((bf16[1,256,1024]{2,1,0:T(8,128)(2,1)}, bf16[1,256,1024]{2,1,0:T(8,128)(2,1)}, u32[]{:S(2)}, u32[]{:S(2)}) %collective-permute-start.27) | collective-permute-done | bytes 524320 | tf_op jit(solution)/shard_map/ppermute | solution.py:547
  395.9 8.6 %collective-permute-done.35 = f32[1920]{0:T(1024)S(1)} collective-permute-done((f32[1920]{0:T(1024)S(1)}, f32[1920]{0:T(1024)S(1)}, u32[]{:S(2)}, u32[]{:S(2)}) %collective-permute-start.35) | collective-permute-done | bytes 7712 | tf_op jit(solution)/shard_map/ppermute | solution.py:547
  (249 shorter events, 144.8 us)
Async XLA Ops:
  7.2 86.0 %all-gather.3.cloned.1.call-start = ((), (), s32[]{:S(2)}) async-start(), calls=%async_computation.6 | async-start | bytes 2621440 | tf_op jit(solution)/shard_map/all_gather | solution.py:869
  8.8 25.7 %collective-permute-start.2 = (bf16[512,256]{1,0:T(8,128)(2,1)S(1)}, bf16[512,256]{1,0:T(8,128)(2,1)S(1)}, u32[]{:S(2)}, u32[]{:S(2)}) collective-permute-start(bf16[512,256]{1,0:T(8,128)(2,1)S(1)} %constant_dynamic-slice_fusion.2), channel_id=1, source_target_pairs={{0,3},{1,0},{2,1},{3,2},{4,7},{5,4},{6,5},{7,6},{8,11},{9,8},{10,9... | collective-permute-start | bytes 786440 | tf_op jit(solution)/shard_map/ppermute | solution.py:705
  13.9 22.3 %collective-permute-start.1 = (bf16[512,256]{1,0:T(8,128)(2,1)S(1)}, bf16[512,256]{1,0:T(8,128)(2,1)S(1)}, u32[]{:S(2)}, u32[]{:S(2)}) collective-permute-start(bf16[512,256]{1,0:T(8,128)(2,1)S(1)} %constant_dynamic-slice_fusion.2), channel_id=1, source_target_pairs={{0,2},{1,3},{2,0},{3,1},{4,6},{5,7},{6,4},{7,5},{8,10},{9,11},{10,... | collective-permute-start | bytes 786440 | tf_op jit(solution)/shard_map/ppermute | solution.py:705
  13.9 22.3 %collective-permute-start = (bf16[512,256]{1,0:T(8,128)(2,1)S(1)}, bf16[512,256]{1,0:T(8,128)(2,1)S(1)}, u32[]{:S(2)}, u32[]{:S(2)}) collective-permute-start(bf16[512,256]{1,0:T(8,128)(2,1)S(1)} %constant_dynamic-slice_fusion.2), channel_id=1, source_target_pairs={{0,1},{1,2},{2,3},{3,0},{4,5},{5,6},{6,7},{7,4},{8,9},{9,10},{10,1... | collective-permute-start | bytes 786440 | tf_op jit(solution)/shard_map/ppermute | solution.py:705
  36.3 93.1 %all-gather.5.cloned.1.call-start = ((), (), s32[]{:S(2)}) async-start(), calls=%async_computation.7 | async-start | bytes 2621440 | tf_op jit(solution)/shard_map/all_gather | solution.py:873
  52.7 122.5 %reduce-scatter.5.cloned.1.call-start = ((), (), s32[]{:S(2)}) async-start(), calls=%async_computation.8 | async-start | bytes 2621440 | tf_op jit(solution)/shard_map/reduce_scatter | solution.py:908
  54.2 24.7 %collective-permute-start.7 = (bf16[2,1024,256]{2,1,0:T(8,128)(2,1)S(1)}, bf16[2,1024,256]{2,1,0:T(8,128)(2,1)S(1)}, u32[]{:S(2)}, u32[]{:S(2)}) collective-permute-start(bf16[2,1024,256]{2,1,0:T(8,128)(2,1)S(1)} %pad_maximum_fusion.1.refs_0_.refs_1_), channel_id=1, source_target_pairs={{0,16},{4,20},{8,24},{12,28},{16,0},{20,4},{24,8},{28,12},{1,17},{... | collective-permute-start | bytes 3145736 | tf_op jit(solution)/shard_map/ppermute | solution.py:547
  56.9 24.5 %collective-permute-start.8 = (bf16[2,1024,256]{2,1,0:T(8,128)(2,1)S(1)}, bf16[2,1024,256]{2,1,0:T(8,128)(2,1)}, u32[]{:S(2)}, u32[]{:S(2)}) collective-permute-start(bf16[2,1024,256]{2,1,0:T(8,128)(2,1)S(1)} %pad_maximum_fusion.2.refs_2_.refs_3_), channel_id=1, source_target_pairs={{0,8},{4,12},{8,0},{12,4},{16,24},{20,28},{24,16},{28,20},{1,9},{5... | collective-permute-start | bytes 3145736 | tf_op jit(solution)/shard_map/ppermute | solution.py:547
  129.4 90.5 %reduce-scatter.7.cloned.1.call-start = ((), (), s32[]{:S(2)}) async-start(), calls=%async_computation.9 | async-start | bytes 2621440 | tf_op jit(solution)/shard_map/reduce_scatter | solution.py:915
  234.2 122.3 %reduce-scatter.9.cloned.1.call-start = ((), (), s32[]{:S(2)}) async-start(), calls=%async_computation.10 | async-start | bytes 5242880 | tf_op jit(solution)/shard_map/reduce_scatter | solution.py:951
  249.2 26.5 %collective-permute-start.17 = (bf16[4,256,2048]{2,1,0:T(8,128)(2,1)}, bf16[4,256,2048]{2,1,0:T(8,128)(2,1)}, u32[]{:S(2)}, u32[]{:S(2)}) collective-permute-start(bf16[4,256,2048]{2,1,0:T(8,128)(2,1)} %get-tuple-element.394), channel_id=1, source_target_pairs={{0,4},{4,0},{8,12},{12,8},{16,20},{20,16},{24,28},{28,24},{1,5},{5... | collective-permute-start | bytes 12582920 | tf_op jit(solution)/shard_map/ppermute | solution.py:547
  249.9 174.7 %reduce-scatter.11.cloned.1.call-start = ((), (), s32[]{:S(2)}) async-start(), calls=%async_computation.11 | async-start | bytes 5242880 | tf_op jit(solution)/shard_map/reduce_scatter | solution.py:973
  255.4 25.6 %collective-permute-start.15 = (bf16[2,256,1024]{2,1,0:T(8,128)(2,1)}, bf16[2,256,1024]{2,1,0:T(8,128)(2,1)S(1)}, u32[]{:S(2)}, u32[]{:S(2)}) collective-permute-start(bf16[2,256,1024]{2,1,0:T(8,128)(2,1)} %get-tuple-element.390), channel_id=1, source_target_pairs={{0,8},{4,12},{8,0},{12,4},{16,24},{20,28},{24,16},{28,20},{1,9},{5... | collective-permute-start | bytes 3145736 | tf_op jit(solution)/shard_map/ppermute | solution.py:547
  256.9 24.8 %collective-permute-start.16 = (bf16[2,256,1024]{2,1,0:T(8,128)(2,1)}, bf16[2,256,1024]{2,1,0:T(8,128)(2,1)S(1)}, u32[]{:S(2)}, u32[]{:S(2)}) collective-permute-start(bf16[2,256,1024]{2,1,0:T(8,128)(2,1)} %get-tuple-element.392), channel_id=1, source_target_pairs={{0,16},{4,20},{8,24},{12,28},{16,0},{20,4},{24,8},{28,12},{1,17},{... | collective-permute-start | bytes 3145736 | tf_op jit(solution)/shard_map/ppermute | solution.py:547
  281.7 24.0 %collective-permute-start.18 = (bf16[2,256,1024]{2,1,0:T(8,128)(2,1)}, bf16[2,256,1024]{2,1,0:T(8,128)(2,1)S(1)}, u32[]{:S(2)}, u32[]{:S(2)}) collective-permute-start(bf16[2,256,1024]{2,1,0:T(8,128)(2,1)} %get-tuple-element.407), channel_id=1, source_target_pairs={{0,8},{4,12},{8,0},{12,4},{16,24},{20,28},{24,16},{28,20},{1,9},{5... | collective-permute-start | bytes 3145736 | tf_op jit(solution)/shard_map/ppermute | solution.py:547
  282.3 23.9 %collective-permute-start.19 = (bf16[2,256,1024]{2,1,0:T(8,128)(2,1)}, bf16[2,256,1024]{2,1,0:T(8,128)(2,1)}, u32[]{:S(2)}, u32[]{:S(2)}) collective-permute-start(bf16[2,256,1024]{2,1,0:T(8,128)(2,1)} %get-tuple-element.409), channel_id=1, source_target_pairs={{0,16},{4,20},{8,24},{12,28},{16,0},{20,4},{24,8},{28,12},{1,17},{... | collective-permute-start | bytes 3145736 | tf_op jit(solution)/shard_map/ppermute | solution.py:547
  343.0 30.4 %collective-permute-start.25 = (bf16[2,256,768]{2,1,0:T(8,128)(2,1)}, bf16[2,256,768]{2,1,0:T(8,128)(2,1)S(1)}, u32[]{:S(2)}, u32[]{:S(2)}) collective-permute-start(bf16[2,256,768]{2,1,0:T(8,128)(2,1)} %get-tuple-element.473), channel_id=1, source_target_pairs={{0,8},{4,12},{8,0},{12,4},{16,24},{20,28},{24,16},{28,20},{1,9},{5... | collective-permute-start | bytes 2359304 | tf_op jit(solution)/shard_map/ppermute | solution.py:547
  343.8 29.6 %collective-permute-start.26 = (bf16[2,256,768]{2,1,0:T(8,128)(2,1)}, bf16[2,256,768]{2,1,0:T(8,128)(2,1)}, u32[]{:S(2)}, u32[]{:S(2)}) collective-permute-start(bf16[2,256,768]{2,1,0:T(8,128)(2,1)} %get-tuple-element.475), channel_id=1, source_target_pairs={{0,16},{4,20},{8,24},{12,28},{16,0},{20,4},{24,8},{28,12},{1,17},{... | collective-permute-start | bytes 2359304 | tf_op jit(solution)/shard_map/ppermute | solution.py:547
  345.4 28.0 %collective-permute-start.27 = (bf16[1,256,1024]{2,1,0:T(8,128)(2,1)}, bf16[1,256,1024]{2,1,0:T(8,128)(2,1)}, u32[]{:S(2)}, u32[]{:S(2)}) collective-permute-start(bf16[1,256,1024]{2,1,0:T(8,128)(2,1)} %get-tuple-element.477), channel_id=1, source_target_pairs={{0,16},{4,20},{8,24},{12,28},{16,0},{20,4},{24,8},{28,12},{1,17},{... | collective-permute-start | bytes 1572872 | tf_op jit(solution)/shard_map/ppermute | solution.py:547
  346.1 27.3 %collective-permute-start.28 = (bf16[1,256,1024]{2,1,0:T(8,128)(2,1)}, bf16[1,256,1024]{2,1,0:T(8,128)(2,1)}, u32[]{:S(2)}, u32[]{:S(2)}) collective-permute-start(bf16[1,256,1024]{2,1,0:T(8,128)(2,1)} %get-tuple-element.479), channel_id=1, source_target_pairs={{0,8},{4,12},{8,0},{12,4},{16,24},{20,28},{24,16},{28,20},{1,9},{5... | collective-permute-start | bytes 1572872 | tf_op jit(solution)/shard_map/ppermute | solution.py:547
  381.9 22.7 %collective-permute-start.31 = (bf16[1,256,768]{2,1,0:T(8,128)(2,1)}, bf16[1,256,768]{2,1,0:T(8,128)(2,1)S(1)}, u32[]{:S(2)}, u32[]{:S(2)}) collective-permute-start(bf16[1,256,768]{2,1,0:T(8,128)(2,1)} %get-tuple-element.510), channel_id=1, source_target_pairs={{0,16},{4,20},{8,24},{12,28},{16,0},{20,4},{24,8},{28,12},{1,17},{... | collective-permute-start | bytes 1179656 | tf_op jit(solution)/shard_map/ppermute | solution.py:547
  405.5 23.3 %collective-permute-start.40 = (bf16[512,256]{1,0:T(8,128)(2,1)}, bf16[512,256]{1,0:T(8,128)(2,1)}, u32[]{:S(2)}, u32[]{:S(2)}) collective-permute-start(bf16[512,256]{1,0:T(8,128)(2,1)} %get-tuple-element.555), channel_id=1, source_target_pairs={{0,3},{1,0},{2,1},{3,2},{4,7},{5,4},{6,5},{7,6},{8,11},{9,8},{10,9... | collective-permute-start | bytes 786440 | tf_op jit(solution)/shard_map/ppermute | solution.py:1018
  407.0 21.8 %collective-permute-start.41 = (bf16[512,256]{1,0:T(8,128)(2,1)}, bf16[512,256]{1,0:T(8,128)(2,1)}, u32[]{:S(2)}, u32[]{:S(2)}) collective-permute-start(bf16[512,256]{1,0:T(8,128)(2,1)} %get-tuple-element.556), channel_id=1, source_target_pairs={{0,2},{1,3},{2,0},{3,1},{4,6},{5,7},{6,4},{7,5},{8,10},{9,11},{10,... | collective-permute-start | bytes 786440 | tf_op jit(solution)/shard_map/ppermute | solution.py:1018
  407.0 21.8 %collective-permute-start.42 = (bf16[512,256]{1,0:T(8,128)(2,1)}, bf16[512,256]{1,0:T(8,128)(2,1)}, u32[]{:S(2)}, u32[]{:S(2)}) collective-permute-start(bf16[512,256]{1,0:T(8,128)(2,1)} %get-tuple-element.557), channel_id=1, source_target_pairs={{0,1},{1,2},{2,3},{3,0},{4,5},{5,6},{6,7},{7,4},{8,9},{9,10},{10,1... | collective-permute-start | bytes 786440 | tf_op jit(solution)/shard_map/ppermute | solution.py:1018
  (66 other events, 717.9 us)
Sparse Core Ops, SparseCore 0:
  36.4 46.4 all-gather.2
  84.4 44.8 all-gather.4
  131.6 42.5 reduce-scatter.4
  176.5 43.1 reduce-scatter.6
  249.4 75.9 reduce-scatter.8
  327.6 79.0 reduce-scatter.10

commit v6 on v5

--- a/solution.py
+++ b/solution.py
@@ -869,7 +869,8 @@
     heads[0] = lax.all_gather(heads[0].reshape(groups * part, local), "tensor", axis=0)
     weight.advance(1)
     heads[1] = attend(1, segments, query, key, value, groups)
-    cot, heads[1] = fence([weight], (cot, heads[1]))
+    cot_sum = column_sums(cot)
+    cot, heads[1], cot_sum = fence([weight], (cot, heads[1], cot_sum))
     heads[1] = lax.all_gather(heads[1].reshape(groups * part, local), "tensor", axis=0)
     weight.advance(2)
     cot_parts = by_part(cot)
@@ -930,12 +931,10 @@
     down_terms = gradient_terms(cots, [hidden], me, blocks)
     d_att, *down_terms = fence([], (d_att, *down_terms))
     got = [exchange(d_att), None]
-    cot_sum = column_sums(cot)
-    up_bias_sum = column_sums(d_up[0]) + column_sums(d_up[1])
     up_sum = DpSum(*up_terms, 2)
     down_sum = DpSum(*down_terms, 4)
-    terms[1], out_terms, d_branches[0], cot_sum, up_bias_sum = fence(
-        [up_sum, down_sum], (terms[1], out_terms, d_branches[0], cot_sum, up_bias_sum)
+    terms[1], out_terms, d_branches[0] = fence(
+        [up_sum, down_sum], (terms[1], out_terms, d_branches[0])
     )
 
     d_att = back(1)
@@ -966,8 +965,8 @@
     terms_in, gain1, bias1 = normed_back(
         d_query, d_key, d_value, query_weight, key_weight, value_weight, inputs
     )
-    gain1, bias1, terms_in, d_query, d_value = fence(
-        [qkv_sum, wo_sum, down_sum], (gain1, bias1, terms_in, d_query, d_value)
+    gain1, bias1, terms_in, d_query, d_value, d_up[0], d_up[1] = fence(
+        [qkv_sum, wo_sum, down_sum], (gain1, bias1, terms_in, d_query, d_value, *d_up)
     )
 
     d_normed = lax.psum_scatter(
@@ -976,8 +975,9 @@
     down_sum.first(1, 2)
     qkv_sum.split()
     wo_sum.add()
-    gain1, bias1, d_query, d_value = fence(
-        [qkv_sum, wo_sum, down_sum], (gain1, bias1, d_query, d_value)
+    up_bias_sum = column_sums(d_up[0]) + column_sums(d_up[1])
+    gain1, bias1, d_query, d_value, up_bias_sum = fence(
+        [qkv_sum, wo_sum, down_sum], (gain1, bias1, d_query, d_value, up_bias_sum)
     )
     qkv_sum.first(0, 1)
     wo_sum.send()

time: 446 us -> 446 us (level)
    ppermute x37, waiting for transfers between devices: 55.7 us -> 50.2 us  [swap_bit(): return lax.ppermute(values, axis, [(i, i ^ 1 << bit) for i in range(size)])]
  transfers between devices with their start and end apart: 51 -> 51, of which waited for: 22 -> 22; matrix products, arithmetic and copies ran while one was open for 5% -> 6% of each run, Pallas kernels for 63% -> 63%
where the time goes in v6:
time: 446 us; the launch traced here: 438 us
  Pallas kernels  275 us (62%)
  waiting for transfers between devices  71.3 us (16%)
  starting transfers between devices  45.3 us (10%)
  other arithmetic  16.4 us (4%)
  local copies, waits for them, and re-layouts  15.2 us (3%)
  between operations  15.1 us (3%)
    pallas_call x2, Pallas kernels, middle_call(): pl.pallas_call(functools.partial(middle_kernel, (first, second)), grid_sp...  55.2 us
    pallas_call x4, Pallas kernels, gradient_terms(): pl.pallas_call(kernel, grid_spec=pltpu.PrefetchScalarGridSpec(num_scalar_...  54.4 us
    ppermute x37, waiting for transfers between devices, swap_bit(): return lax.ppermute(values, axis, [(i, i ^ 1 << bit) for i in range(size)])  50.2 us
    pallas_call x8, Pallas kernels, add_and_split(): pl.pallas_call(kernel, grid=(rows // size,), in_specs=[block(places, v.sh...  33.7 us
    ppermute x37, starting transfers between devices, swap_bit(): return lax.ppermute(values, axis, [(i, i ^ 1 << bit) for i in range(size)])  29.2 us
    pallas_call x2, Pallas kernels, both_parts(): pl.pallas_call(kernel, grid=(columns // block,), in_specs=[left_spec(left...  26.7 us
    pallas_call x1, Pallas kernels, attend_back(): pl.pallas_call(functools.partial(backward_kernel, min(256, length)), grid...  17.4 us
    pallas_call x2, Pallas kernels, middle_back(): pl.pallas_call(middle_back_kernel, grid=(groups,), in_specs=[rows, rows,...  16.6 us
  transfers between devices with their start and end apart: 51, of which 22 were waited for; matrix products, arithmetic and copies ran while one was open for 6% of the time, Pallas kernels for 63%

profile of v6, /device:TPU:0, one launch (start us, length us, event | category | flops | bytes accessed | tf_op | source)
XLA Modules:
  0.0 437.9 jit_solution(2191753526596884028)
XLA Ops:
  14.9 13.4 %shard_map.305 = (bf16[1024,2048]{1,0:T(8,128)(2,1)}, bf16[1024,512]{1,0:T(8,128)(2,1)}, bf16[1024,512]{1,0:T(8,128)(2,1)}, bf16[1024,512]{1,0:T(8,128)(2,1)}) custom-call(bf16[1024,2048]{1,0:T(8,128)(2,1)} %x.3, f32[1,2048]{1,0:T(1,128)} %bitcast.99, f32[1,2048]{1,0:T(1,128)} %bitcast.107, bf16[2048,512]{1,0:T(8,128)(2,1)} %wq.3, f32[1,512]{1,0:T(1,128)} %bitcast.108, ...), custom_call_target="tpu_custom_call" | custom-call | bytes 1024 | tf_op jit(solution)/shard_map/pallas_call | solution.py:193
  28.3 6.2 %shard_map.306 = bf16[4,128,512]{2,1,0:T(8,128)(2,1)} custom-call(s32[1,1024]{1,0:T(1,128)} %seg_row.5, bf16[1024,512]{1,0:T(8,128)(2,1)} %get-tuple-element.307.query, bf16[1024,512]{1,0:T(8,128)(2,1)} %get-tuple-element.308.key, bf16[1024,512]{1,0:T(8,128)(2,1)} %get-tuple-element.309.value), custom_call_target="tpu_custom_call" | custom-call | bytes 1024 | tf_op jit(solution)/shard_map/pallas_call | solution.py:123
  39.9 6.6 %shard_map.307 = bf16[4,128,512]{2,1,0:T(8,128)(2,1)} custom-call(s32[1,1024]{1,0:T(1,128)} %seg_row.5, bf16[1024,512]{1,0:T(8,128)(2,1)} %get-tuple-element.307.query, bf16[1024,512]{1,0:T(8,128)(2,1)} %get-tuple-element.308.key, bf16[1024,512]{1,0:T(8,128)(2,1)} %get-tuple-element.309.value), custom_call_target="tpu_custom_call" | custom-call | bytes 1024 | tf_op jit(solution)/shard_map/pallas_call | solution.py:123
  58.6 13.4 %shard_map.309.d_hid = bf16[2,512,2048]{2,1,0:T(8,128)(2,1)} custom-call(bf16[4,2,128,2048]{3,2,1,0:T(8,128)(2,1)} %bitcast.67, bf16[4,2,128,2048]{3,2,1,0:T(8,128)(2,1)} %bitcast.68, bf16[2048,2048]{1,0:T(8,128)(2,1)} %refs_2_.3), custom_call_target="tpu_custom_call" | custom-call | bytes 1024 | tf_op jit(solution)/shard_map/pallas_call | solution.py:534
  72.1 5.5 %shard_map.308.refs_8_ = bf16[2048,2048]{1,0:T(8,128)(2,1)} custom-call(s32[3]{0:T(128)} %pad_add_fusion.me_ref.here_ref, bf16[2,1024,256]{2,1,0:T(8,128)(2,1)} %copy-done.2, bf16[2,1024,256]{2,1,0:T(8,128)(2,1)} %copy-done.2, bf16[2,1024,256]{2,1,0:T(8,128)(2,1)} %copy-done.3, bf16[2,1024,256]{2,1,0:T(8,128)(2,1)} %copy-done.3, ...), custom_call_target="tpu_custom_call" | custom-call | bytes 1024 | tf_op jit(solution)/shard_map/pallas_call | solution.py:755
  87.5 5.7 %shard_map.310.wo = bf16[2048,2048]{1,0:T(8,128)(2,1)} custom-call(s32[3]{0:T(128)} %pad_add_fusion.me_ref.here_ref, bf16[2,1024,256]{2,1,0:T(8,128)(2,1)} %copy-done.7, bf16[2,1024,256]{2,1,0:T(8,128)(2,1)} %copy-done.7, bf16[2,1024,256]{2,1,0:T(8,128)(2,1)} %collective-permute-done.8.refs_2_.refs_3_, ...), custom_call_target="tpu_custom_call", output_to_operand_aliasing={{}: (9, {})} | custom-call | bytes 1024 | tf_op jit(solution)/shard_map/pallas_call | solution.py:755
  93.1 27.6 %shard_map.311 = (f32[128,2048]{1,0:T(8,128)}, bf16[512,2048]{1,0:T(8,128)(2,1)}, bf16[512,2048]{1,0:T(8,128)(2,1)}, bf16[512,2048]{1,0:T(8,128)(2,1)}, bf16[512,2048]{1,0:T(8,128)(2,1)}) custom-call(s32[3]{0:T(128)} %pad_add_fusion.me_ref.here_ref, bf16[4,512,512]{2,1,0:T(8,128)(2,1)} %all-gather.3.cloned.1.call-done.heads, ...), custom_call_target="tpu_custom_call" | custom-call | bytes 1024 | tf_op jit(solution)/shard_map/pallas_call | solution.py:277
  120.7 8.6 %all-gather.5.cloned.1.call-done.heads = bf16[4,512,512]{2,1,0:T(8,128)(2,1)} async-done(((bf16[1,512,512]{2,1,0:T(8,128)(2,1)}), bf16[4,512,512]{2,1,0:T(8,128)(2,1)}) %all-gather.5.cloned.1.call-update) | async-done | bytes 2097168 | tf_op jit(solution)/shard_map/all_gather | solution.py:874
  131.1 27.6 %shard_map.312 = (f32[128,2048]{1,0:T(8,128)}, bf16[512,2048]{1,0:T(8,128)(2,1)}, bf16[512,2048]{1,0:T(8,128)(2,1)}, bf16[512,2048]{1,0:T(8,128)(2,1)}, bf16[512,2048]{1,0:T(8,128)(2,1)}) custom-call(s32[3]{0:T(128)} %pad_add_fusion.me_ref.here_ref, bf16[4,512,512]{2,1,0:T(8,128)(2,1)} %all-gather.5.cloned.1.call-done.heads, ...), custom_call_target="tpu_custom_call" | custom-call | bytes 1024 | tf_op jit(solution)/shard_map/pallas_call | solution.py:277
  158.8 15.3 %shard_map.313 = (bf16[4,256,2048]{2,1,0:T(8,128)(2,1)}, bf16[4,256,2048]{2,1,0:T(8,128)(2,1)}) custom-call(s32[3]{0:T(128)} %pad_add_fusion.me_ref.here_ref, bf16[512,2048]{1,0:T(8,128)(2,1)} %get-tuple-element.343.refs_0_, bf16[512,2048]{1,0:T(8,128)(2,1)} %get-tuple-element.344.refs_1_, bf16[512,2048]{1,0:T(8,128)(2,1)} %get-tuple-element.474.refs_2_, ...), custom_call_target="tpu_custom_call" | custom-call | bytes 1024 | tf_op jit(solution)/shard_map/pallas_call | solution.py:425
  175.1 8.3 %shard_map.314 = (f32[128,2048]{1,0:T(8,128)}, bf16[128,2048]{1,0:T(8,128)(2,1)}, f32[8,2048]{1,0:T(8,128)}, bf16[4,128,512]{2,1,0:T(8,128)(2,1)}) custom-call(bf16[128,2048]{1,0:T(8,128)(2,1)} %bitcast.94, f32[128,2048]{1,0:T(8,128)} %get-tuple-element.352.mid, bf16[128,2048]{1,0:T(8,128)(2,1)} %get-tuple-element.593.cot, f32[1,2048]{1,0:T(1,128)} %bitcast.97, ...), custom_call_target="tpu_custom_call" | custom-call | bytes 1024 | tf_op jit(solution)/shard_map/pallas_call | solution.py:346
  183.5 13.3 %shard_map.315 = bf16[4,2,128,2048]{3,2,1,0:T(8,128)(2,1)} custom-call(bf16[512,2048]{1,0:T(8,128)(2,1)} %get-tuple-element.360.refs_0_.refs_2_, bf16[512,2048]{1,0:T(8,128)(2,1)} %get-tuple-element.361.refs_1_.refs_3_, bf16[2048,2048]{1,0:T(8,128)(2,1)} %refs_2_.3), custom_call_target="tpu_custom_call" | custom-call | bytes 1024 | tf_op jit(solution)/shard_map/pallas_call | solution.py:534
  196.7 15.2 %shard_map.316 = (bf16[4,256,2048]{2,1,0:T(8,128)(2,1)}, bf16[4,256,2048]{2,1,0:T(8,128)(2,1)}) custom-call(s32[3]{0:T(128)} %pad_add_fusion.me_ref.here_ref, bf16[4,2,128,2048]{3,2,1,0:T(8,128)(2,1)} %bitcast.69, bf16[4,2,128,2048]{3,2,1,0:T(8,128)(2,1)} %bitcast.70, bf16[512,2048]{1,0:T(8,128)(2,1)} %get-tuple-element.360.refs_0_.refs_2_, ...), custom_call_target="tpu_custom_call" | custom-call | bytes 1024 | tf_op jit(solution)/shard_map/pallas_call | solution.py:425
  219.7 8.3 %shard_map.317 = (f32[128,2048]{1,0:T(8,128)}, bf16[128,2048]{1,0:T(8,128)(2,1)}, f32[8,2048]{1,0:T(8,128)}, bf16[4,128,512]{2,1,0:T(8,128)(2,1)}) custom-call(bf16[128,2048]{1,0:T(8,128)(2,1)} %bitcast.93, f32[128,2048]{1,0:T(8,128)} %get-tuple-element.374.mid, bf16[128,2048]{1,0:T(8,128)(2,1)} %get-tuple-element.592.cot, f32[1,2048]{1,0:T(1,128)} %bitcast.98, ...), custom_call_target="tpu_custom_call" | custom-call | bytes 1024 | tf_op jit(solution)/shard_map/pallas_call | solution.py:346
  234.2 10.6 %shard_map.318 = (bf16[4,256,2048]{2,1,0:T(8,128)(2,1)}, bf16[4,256,2048]{2,1,0:T(8,128)(2,1)}) custom-call(s32[3]{0:T(128)} %pad_add_fusion.me_ref.here_ref, bf16[128,2048]{1,0:T(8,128)(2,1)} %get-tuple-element.379.refs_0_, bf16[128,2048]{1,0:T(8,128)(2,1)} %get-tuple-element.380.refs_1_, bf16[4,4,128,512]{3,2,1,0:T(8,128)(2,1)} %bitcast.73, ...), custom_call_target="tpu_custom_call" | custom-call | bytes 1024 | tf_op jit(solution)/shard_map/pallas_call | solution.py:425
  250.0 5.3 %shard_map.319 = (bf16[2,256,1024]{2,1,0:T(8,128)(2,1)}, bf16[2,256,1024]{2,1,0:T(8,128)(2,1)}, bf16[2,256,1024]{2,1,0:T(8,128)(2,1)}, bf16[2,256,1024]{2,1,0:T(8,128)(2,1)}) custom-call(bf16[4,256,2048]{2,1,0:T(8,128)(2,1)} %get-tuple-element.389.refs_0_, bf16[4,256,2048]{2,1,0:T(8,128)(2,1)} %collective-permute-done.13.refs_1_), custom_call_target="tpu_custom_call" | custom-call | bytes 1024 | tf_op jit(solution)/shard_map/pallas_call | solution.py:593
  258.3 17.4 %shard_map.321 = (bf16[1024,512]{1,0:T(8,128)(2,1)}, bf16[1024,512]{1,0:T(8,128)(2,1)}, bf16[1024,512]{1,0:T(8,128)(2,1)}) custom-call(s32[1,1024]{1,0:T(1,128)} %seg_row.5, bf16[1024,512]{1,0:T(8,128)(2,1)} %get-tuple-element.307.query, bf16[1024,512]{1,0:T(8,128)(2,1)} %get-tuple-element.308.key, bf16[1024,512]{1,0:T(8,128)(2,1)} %get-tuple-element.309.value, ...), custom_call_target="tpu_custom_call" | custom-call | bytes 1024 | tf_op jit(solution)/shard_map/pallas_call | solution.py:137
  275.7 5.3 %shard_map.320 = (bf16[2,256,1024]{2,1,0:T(8,128)(2,1)}, bf16[2,256,1024]{2,1,0:T(8,128)(2,1)}, bf16[2,256,1024]{2,1,0:T(8,128)(2,1)}, bf16[2,256,1024]{2,1,0:T(8,128)(2,1)}) custom-call(bf16[4,256,2048]{2,1,0:T(8,128)(2,1)} %get-tuple-element.395.refs_0_, bf16[4,256,2048]{2,1,0:T(8,128)(2,1)} %collective-permute-done.17.refs_1_), custom_call_target="tpu_custom_call" | custom-call | bytes 1024 | tf_op jit(solution)/shard_map/pallas_call | solution.py:593
  283.7 5.3 %shard_map.323 = (bf16[2,256,512]{2,1,0:T(8,128)(2,1)}, bf16[2,256,512]{2,1,0:T(8,128)(2,1)}, bf16[2,256,512]{2,1,0:T(8,128)(2,1)}, bf16[2,256,512]{2,1,0:T(8,12...) custom-call(bf16[4,256,2048]{2,1,0:T(8,128)(2,1)} %get-tuple-element, ...), custom_call_target="tpu_custom_call" | custom-call | bytes 1024 | tf_op jit(solution)/shard_map/pallas_call | solution.py:593
  289.0 13.3 %shard_map.322 = (bf16[4,256,1536]{2,1,0:T(8,128)(2,1)}, bf16[4,256,1536]{2,1,0:T(8,128)(2,1)}) custom-call(s32[3]{0:T(128)} %pad_add_fusion.me_ref.here_ref, bf16[1024,2048]{1,0:T(8,128)(2,1)} %get-tuple-element.412.refs_0_, bf16[1024,512]{1,0:T(8,128)(2,1)} %get-tuple-element.501.refs_1_.dq, bf16[1024,512]{1,0:T(8,128)(2,1)} %get-tuple-element.443.refs_2_.dk, ...), custom_call_target="tpu_custom_call" | custom-call | bytes 1024 | tf_op jit(solution)/shard_map/pallas_call | solution.py:425
  309.1 15.3 %shard_map.324 = (bf16[1024,2048]{1,0:T(8,128)(2,1)}, f32[1,2048]{1,0:T(1,128)}, f32[1,2048]{1,0:T(1,128)}) custom-call(bf16[1024,512]{1,0:T(8,128)(2,1)} %get-tuple-element.501.refs_1_.dq, bf16[1024,512]{1,0:T(8,128)(2,1)} %get-tuple-element.443.refs_2_.dk, bf16[1024,512]{1,0:T(8,128)(2,1)} %get-tuple-element.502.refs_3_.dv, bf16[2048,512]{1,0:T(8,128)(2,1)} %wq.3, ...), custom_call_target="tpu_custom_call" | custom-call | bytes 1024 | tf_op jit(solution)/shard_map/pallas_call | solution.py:466
  347.6 5.3 %collective-permute-done.29 = f32[2,2,2,1280]{3,2,1,0:T(2,128)S(1)} collective-permute-done((f32[2,2,2,1280]{3,2,1,0:T(2,128)S(1)}, f32[2,2,2,1280]{3,2,1,0:T(2,128)S(1)}, u32[]{:S(2)}, u32[]{:S(2)}) %collective-permute-start.29) | collective-permute-done | bytes 40992 | tf_op jit(solution)/shard_map/ppermute | solution.py:547
  360.9 12.7 %collective-permute-done.27.refs_1_ = bf16[1,256,1024]{2,1,0:T(8,128)(2,1)S(1)} collective-permute-done((bf16[1,256,1024]{2,1,0:T(8,128)(2,1)}, bf16[1,256,1024]{2,1,0:T(8,128)(2,1)S(1)}, u32[]{:S(2)}, u32[]{:S(2)}) %collective-permute-start.27) | collective-permute-done | bytes 524320 | tf_op jit(solution)/shard_map/ppermute | solution.py:547
  396.3 8.5 %collective-permute-done.35 = f32[1920]{0:T(1024)S(1)} collective-permute-done((f32[1920]{0:T(1024)S(1)}, f32[1920]{0:T(1024)S(1)}, u32[]{:S(2)}, u32[]{:S(2)}) %collective-permute-start.35) | collective-permute-done | bytes 7712 | tf_op jit(solution)/shard_map/ppermute | solution.py:547
  (249 shorter events, 149.0 us)
Async XLA Ops:
  7.2 85.9 %all-gather.3.cloned.1.call-start = ((), (), s32[]{:S(2)}) async-start(), calls=%async_computation.6 | async-start | bytes 2621440 | tf_op jit(solution)/shard_map/all_gather | solution.py:869
  8.8 25.7 %collective-permute-start.2 = (bf16[512,256]{1,0:T(8,128)(2,1)S(1)}, bf16[512,256]{1,0:T(8,128)(2,1)S(1)}, u32[]{:S(2)}, u32[]{:S(2)}) collective-permute-start(bf16[512,256]{1,0:T(8,128)(2,1)S(1)} %constant_dynamic-slice_fusion.2), channel_id=1, source_target_pairs={{0,3},{1,0},{2,1},{3,2},{4,7},{5,4},{6,5},{7,6},{8,11},{9,8},{10,9... | collective-permute-start | bytes 786440 | tf_op jit(solution)/shard_map/ppermute | solution.py:705
  13.9 22.3 %collective-permute-start.1 = (bf16[512,256]{1,0:T(8,128)(2,1)S(1)}, bf16[512,256]{1,0:T(8,128)(2,1)S(1)}, u32[]{:S(2)}, u32[]{:S(2)}) collective-permute-start(bf16[512,256]{1,0:T(8,128)(2,1)S(1)} %constant_dynamic-slice_fusion.2), channel_id=1, source_target_pairs={{0,2},{1,3},{2,0},{3,1},{4,6},{5,7},{6,4},{7,5},{8,10},{9,11},{10,... | collective-permute-start | bytes 786440 | tf_op jit(solution)/shard_map/ppermute | solution.py:705
  13.9 22.3 %collective-permute-start = (bf16[512,256]{1,0:T(8,128)(2,1)S(1)}, bf16[512,256]{1,0:T(8,128)(2,1)S(1)}, u32[]{:S(2)}, u32[]{:S(2)}) collective-permute-start(bf16[512,256]{1,0:T(8,128)(2,1)S(1)} %constant_dynamic-slice_fusion.2), channel_id=1, source_target_pairs={{0,1},{1,2},{2,3},{3,0},{4,5},{5,6},{6,7},{7,4},{8,9},{9,10},{10,1... | collective-permute-start | bytes 786440 | tf_op jit(solution)/shard_map/ppermute | solution.py:705
  36.3 93.1 %all-gather.5.cloned.1.call-start = ((), (), s32[]{:S(2)}) async-start(), calls=%async_computation.7 | async-start | bytes 2621440 | tf_op jit(solution)/shard_map/all_gather | solution.py:874
  52.7 122.5 %reduce-scatter.5.cloned.1.call-start = ((), (), s32[]{:S(2)}) async-start(), calls=%async_computation.8 | async-start | bytes 2621440 | tf_op jit(solution)/shard_map/reduce_scatter | solution.py:909
  54.2 24.7 %collective-permute-start.7 = (bf16[2,1024,256]{2,1,0:T(8,128)(2,1)S(1)}, bf16[2,1024,256]{2,1,0:T(8,128)(2,1)S(1)}, u32[]{:S(2)}, u32[]{:S(2)}) collective-permute-start(bf16[2,1024,256]{2,1,0:T(8,128)(2,1)S(1)} %pad_maximum_fusion.1.refs_0_.refs_1_), channel_id=1, source_target_pairs={{0,16},{4,20},{8,24},{12,28},{16,0},{20,4},{24,8},{28,12},{1,17},{... | collective-permute-start | bytes 3145736 | tf_op jit(solution)/shard_map/ppermute | solution.py:547
  56.9 24.5 %collective-permute-start.8 = (bf16[2,1024,256]{2,1,0:T(8,128)(2,1)S(1)}, bf16[2,1024,256]{2,1,0:T(8,128)(2,1)}, u32[]{:S(2)}, u32[]{:S(2)}) collective-permute-start(bf16[2,1024,256]{2,1,0:T(8,128)(2,1)S(1)} %pad_maximum_fusion.2.refs_2_.refs_3_), channel_id=1, source_target_pairs={{0,8},{4,12},{8,0},{12,4},{16,24},{20,28},{24,16},{28,20},{1,9},{5... | collective-permute-start | bytes 3145736 | tf_op jit(solution)/shard_map/ppermute | solution.py:547
  129.4 90.4 %reduce-scatter.7.cloned.1.call-start = ((), (), s32[]{:S(2)}) async-start(), calls=%async_computation.9 | async-start | bytes 2621440 | tf_op jit(solution)/shard_map/reduce_scatter | solution.py:916
  234.2 126.7 %reduce-scatter.9.cloned.1.call-start = ((), (), s32[]{:S(2)}) async-start(), calls=%async_computation.10 | async-start | bytes 5242880 | tf_op jit(solution)/shard_map/reduce_scatter | solution.py:950
  249.1 26.6 %collective-permute-start.17 = (bf16[4,256,2048]{2,1,0:T(8,128)(2,1)}, bf16[4,256,2048]{2,1,0:T(8,128)(2,1)}, u32[]{:S(2)}, u32[]{:S(2)}) collective-permute-start(bf16[4,256,2048]{2,1,0:T(8,128)(2,1)} %get-tuple-element.396), channel_id=1, source_target_pairs={{0,4},{4,0},{8,12},{12,8},{16,20},{20,16},{24,28},{28,24},{1,5},{5... | collective-permute-start | bytes 12582920 | tf_op jit(solution)/shard_map/ppermute | solution.py:547
  249.9 174.7 %reduce-scatter.11.cloned.1.call-start = ((), (), s32[]{:S(2)}) async-start(), calls=%async_computation.11 | async-start | bytes 5242880 | tf_op jit(solution)/shard_map/reduce_scatter | solution.py:972
  255.3 25.6 %collective-permute-start.15 = (bf16[2,256,1024]{2,1,0:T(8,128)(2,1)}, bf16[2,256,1024]{2,1,0:T(8,128)(2,1)S(1)}, u32[]{:S(2)}, u32[]{:S(2)}) collective-permute-start(bf16[2,256,1024]{2,1,0:T(8,128)(2,1)} %get-tuple-element.392), channel_id=1, source_target_pairs={{0,8},{4,12},{8,0},{12,4},{16,24},{20,28},{24,16},{28,20},{1,9},{5... | collective-permute-start | bytes 3145736 | tf_op jit(solution)/shard_map/ppermute | solution.py:547
  256.8 24.9 %collective-permute-start.16 = (bf16[2,256,1024]{2,1,0:T(8,128)(2,1)}, bf16[2,256,1024]{2,1,0:T(8,128)(2,1)S(1)}, u32[]{:S(2)}, u32[]{:S(2)}) collective-permute-start(bf16[2,256,1024]{2,1,0:T(8,128)(2,1)} %get-tuple-element.394), channel_id=1, source_target_pairs={{0,16},{4,20},{8,24},{12,28},{16,0},{20,4},{24,8},{28,12},{1,17},{... | collective-permute-start | bytes 3145736 | tf_op jit(solution)/shard_map/ppermute | solution.py:547
  281.7 24.1 %collective-permute-start.18 = (bf16[2,256,1024]{2,1,0:T(8,128)(2,1)}, bf16[2,256,1024]{2,1,0:T(8,128)(2,1)S(1)}, u32[]{:S(2)}, u32[]{:S(2)}) collective-permute-start(bf16[2,256,1024]{2,1,0:T(8,128)(2,1)} %get-tuple-element.409), channel_id=1, source_target_pairs={{0,8},{4,12},{8,0},{12,4},{16,24},{20,28},{24,16},{28,20},{1,9},{5... | collective-permute-start | bytes 3145736 | tf_op jit(solution)/shard_map/ppermute | solution.py:547
  282.3 24.0 %collective-permute-start.19 = (bf16[2,256,1024]{2,1,0:T(8,128)(2,1)}, bf16[2,256,1024]{2,1,0:T(8,128)(2,1)}, u32[]{:S(2)}, u32[]{:S(2)}) collective-permute-start(bf16[2,256,1024]{2,1,0:T(8,128)(2,1)} %get-tuple-element.411), channel_id=1, source_target_pairs={{0,16},{4,20},{8,24},{12,28},{16,0},{20,4},{24,8},{28,12},{1,17},{... | collective-permute-start | bytes 3145736 | tf_op jit(solution)/shard_map/ppermute | solution.py:547
  343.3 30.3 %collective-permute-start.25 = (bf16[2,256,768]{2,1,0:T(8,128)(2,1)}, bf16[2,256,768]{2,1,0:T(8,128)(2,1)S(1)}, u32[]{:S(2)}, u32[]{:S(2)}) collective-permute-start(bf16[2,256,768]{2,1,0:T(8,128)(2,1)} %get-tuple-element.477), channel_id=1, source_target_pairs={{0,8},{4,12},{8,0},{12,4},{16,24},{20,28},{24,16},{28,20},{1,9},{5... | collective-permute-start | bytes 2359304 | tf_op jit(solution)/shard_map/ppermute | solution.py:547
  344.1 29.5 %collective-permute-start.26 = (bf16[2,256,768]{2,1,0:T(8,128)(2,1)}, bf16[2,256,768]{2,1,0:T(8,128)(2,1)}, u32[]{:S(2)}, u32[]{:S(2)}) collective-permute-start(bf16[2,256,768]{2,1,0:T(8,128)(2,1)} %get-tuple-element.479), channel_id=1, source_target_pairs={{0,16},{4,20},{8,24},{12,28},{16,0},{20,4},{24,8},{28,12},{1,17},{... | collective-permute-start | bytes 2359304 | tf_op jit(solution)/shard_map/ppermute | solution.py:547
  345.6 27.9 %collective-permute-start.27 = (bf16[1,256,1024]{2,1,0:T(8,128)(2,1)}, bf16[1,256,1024]{2,1,0:T(8,128)(2,1)S(1)}, u32[]{:S(2)}, u32[]{:S(2)}) collective-permute-start(bf16[1,256,1024]{2,1,0:T(8,128)(2,1)} %get-tuple-element.481), channel_id=1, source_target_pairs={{0,16},{4,20},{8,24},{12,28},{16,0},{20,4},{24,8},{28,12},{1,17},{... | collective-permute-start | bytes 1572872 | tf_op jit(solution)/shard_map/ppermute | solution.py:547
  346.4 27.2 %collective-permute-start.28 = (bf16[1,256,1024]{2,1,0:T(8,128)(2,1)}, bf16[1,256,1024]{2,1,0:T(8,128)(2,1)}, u32[]{:S(2)}, u32[]{:S(2)}) collective-permute-start(bf16[1,256,1024]{2,1,0:T(8,128)(2,1)} %get-tuple-element.483), channel_id=1, source_target_pairs={{0,8},{4,12},{8,0},{12,4},{16,24},{20,28},{24,16},{28,20},{1,9},{5... | collective-permute-start | bytes 1572872 | tf_op jit(solution)/shard_map/ppermute | solution.py:547
  382.3 22.5 %collective-permute-start.31 = (bf16[1,256,768]{2,1,0:T(8,128)(2,1)}, bf16[1,256,768]{2,1,0:T(8,128)(2,1)S(1)}, u32[]{:S(2)}, u32[]{:S(2)}) collective-permute-start(bf16[1,256,768]{2,1,0:T(8,128)(2,1)} %get-tuple-element.514), channel_id=1, source_target_pairs={{0,16},{4,20},{8,24},{12,28},{16,0},{20,4},{24,8},{28,12},{1,17},{... | collective-permute-start | bytes 1179656 | tf_op jit(solution)/shard_map/ppermute | solution.py:547
  405.8 23.1 %collective-permute-start.40 = (bf16[512,256]{1,0:T(8,128)(2,1)}, bf16[512,256]{1,0:T(8,128)(2,1)}, u32[]{:S(2)}, u32[]{:S(2)}) collective-permute-start(bf16[512,256]{1,0:T(8,128)(2,1)} %get-tuple-element.559), channel_id=1, source_target_pairs={{0,3},{1,0},{2,1},{3,2},{4,7},{5,4},{6,5},{7,6},{8,11},{9,8},{10,9... | collective-permute-start | bytes 786440 | tf_op jit(solution)/shard_map/ppermute | solution.py:1018
  407.2 21.6 %collective-permute-start.41 = (bf16[512,256]{1,0:T(8,128)(2,1)}, bf16[512,256]{1,0:T(8,128)(2,1)}, u32[]{:S(2)}, u32[]{:S(2)}) collective-permute-start(bf16[512,256]{1,0:T(8,128)(2,1)} %get-tuple-element.560), channel_id=1, source_target_pairs={{0,2},{1,3},{2,0},{3,1},{4,6},{5,7},{6,4},{7,5},{8,10},{9,11},{10,... | collective-permute-start | bytes 786440 | tf_op jit(solution)/shard_map/ppermute | solution.py:1018
  407.2 21.6 %collective-permute-start.42 = (bf16[512,256]{1,0:T(8,128)(2,1)}, bf16[512,256]{1,0:T(8,128)(2,1)}, u32[]{:S(2)}, u32[]{:S(2)}) collective-permute-start(bf16[512,256]{1,0:T(8,128)(2,1)} %get-tuple-element.561), channel_id=1, source_target_pairs={{0,1},{1,2},{2,3},{3,0},{4,5},{5,6},{6,7},{7,4},{8,9},{9,10},{10,1... | collective-permute-start | bytes 786440 | tf_op jit(solution)/shard_map/ppermute | solution.py:1018
  (66 other events, 693.1 us)
Sparse Core Ops, SparseCore 0:
  36.4 46.2 all-gather.2
  84.2 45.0 all-gather.4
  131.6 42.5 reduce-scatter.4
  176.5 43.1 reduce-scatter.6
  249.3 75.9 reduce-scatter.8
  327.5 79.0 reduce-scatter.10
